TPU v7x, 32 devices: a whole 2x2x4 slice. The times are simulated.
32 devices in a mesh: shot: 4 (over y, x), box: 8 (over z, core).
Axes of the slice: x: 2, y: 2, z: 4, core: 2. Of those that a mesh axis runs over, the one named last changes fastest.
Arguments:
- u_prev: float32 [4, 8, 128, 256], P('shot', None, 'box'), may hold values from -6 to 6
- u_now: float32 [4, 8, 128, 256], P('shot', None, 'box'), may hold values from -6 to 6
- born_prev: float32 [4, 8, 128, 256], P('shot', None, 'box'), may hold values from -6 to 6
- born_now: float32 [4, 8, 128, 256], P('shot', None, 'box'), may hold values from -6 to 6
- adj_after: float32 [4, 8, 128, 256], P('shot', None, 'box'), may hold values from -6 to 6
- adj_last: float32 [4, 8, 128, 256], P('shot', None, 'box'), may hold values from -6 to 6
- velocity: float32 [4, 128, 256], P('shot', 'box'), may hold values from 0.08 to 0.45
- wavelet: float32 [4, 8, 4], P('shot'), may hold values from -12 to 12
- sources: int32 [4, 8], P('shot'), may hold values from 0 to 32767
- receivers: int32 [4, 64], P('shot', 'box'), may hold values from 0 to 32575, as said below
- observed: float32 [4, 8, 4, 64], P('shot', None, None, 'box'), may hold values from -6 to 6
- first_tile: int32 [4], P('shot'), may hold values from 0 to 32
- reflectivity: float32 [12, 8, 2, 256], P(None, 'box'), may hold values from -6 to 6
Outputs:
- migrated: float32 [12, 8, 2, 256], P(None, 'box')
Inputs may be any that keep to these rules, and one draw needn't show every extreme that they name: `receivers`: receiver r of every group lies in the grid columns r * 2 to (r + 1) * 2 - 1 of its box, at a depth cell under 256 // 4.
All inputs are finite; a program needn't handle non-finite values.
Results may differ from a plain program's by a relative error of at most 0.00011.
Values sent between devices are 32-bit elements; how exact they have to be, the bound alone decides.
No kernel may reach another device: no remote copies, remote signals or barrier semaphores. Data moves between devices by JAX's collectives and lax.ppermute only.
A program may use at most 64 MiB of HBM per device.

v0:
```python
import jax
import jax.numpy as jnp
from jax import lax
from jax.sharding import PartitionSpec as P

damping = 1.0


def padded_2(block, sides, width):
    for axis, dim in sides:
        count = lax.axis_size(axis)
        forward = [(i, i + 1) for i in range(count - 1)]
        backward = [(target, source) for source, target in forward]
        low = lax.ppermute(
            lax.slice_in_dim(block, block.shape[dim] - width, None, axis=dim), axis, forward
        )
        high = lax.ppermute(lax.slice_in_dim(block, 0, width, axis=dim), axis, backward)
        block = jnp.concatenate([low, block, high], axis=dim)
    return block


def laplace_rows(padded):
    center = padded[:, 1:-1]
    deeper = jnp.pad(center, ((0, 0), (0, 0), (1, 1)))
    return padded[:, 2:] + padded[:, :-2] + deeper[:, :, 2:] + deeper[:, :, :-2] - 4.0 * center


def on_device(
    u_prev,
    u_now,
    born_prev,
    born_now,
    adj_after,
    adj_last,
    velocity,
    wavelet,
    sources,
    receivers,
    observed,
    first_tile,
    reflectivity,
):
    owners = lax.axis_size("box")
    position = lax.axis_index("box")
    shot_count = u_now.shape[1]
    columns = u_now.shape[2]
    depth_cells = u_now.shape[3]
    step_count = wavelet.shape[2]
    tile_width = reflectivity.shape[2]
    start_tile = first_tile[0]
    round_base = start_tile // owners
    rotation = start_tile % owners
    first_round = round_base + (position < rotation).astype(jnp.int32)
    owned_tiles = reflectivity[:, 0]
    outgoing = lax.dynamic_slice_in_dim(owned_tiles, first_round, owners, 0)
    incoming = lax.all_to_all(outgoing, "box", split_axis=0, concat_axis=0, tiled=True)
    image_slab = jnp.roll(incoming, -rotation, axis=0).reshape(columns, depth_cells)
    speed_slab = velocity[0]
    column_start = position * columns
    source_column = sources[0] // depth_cells - column_start
    source_depth = sources[0] % depth_cells
    receiver_global = receivers[0] // depth_cells
    receiver_column = receiver_global - column_start
    receiver_depth = receivers[0] % depth_cells
    pulses = wavelet[0]
    recorded = observed[0]
    shot_lane = jnp.arange(shot_count, dtype=jnp.int32)
    accelerations = []
    predicted = []
    gradient = jnp.zeros((columns, depth_cells), jnp.float32)
    illumination = jnp.zeros((columns, depth_cells), jnp.float32)
    older_u, newer_u = (u_prev[0], u_now[0])
    older_b, newer_b = (born_prev[0], born_now[0])
    for moment in range(step_count):
        joined = jnp.concatenate([newer_u, newer_b], axis=0)
        padded = padded_2(joined, (("box", 1),), 1)
        lap_all = laplace_rows(padded)
        next_u = 2.0 * newer_u - older_u + speed_slab * lap_all[:shot_count]
        column = source_column
        inside = (column >= 0) & (column < next_u.shape[1])
        column = jnp.clip(column, 0, next_u.shape[1] - 1)
        next_u = next_u.at[shot_lane, column, source_depth].add(
            jnp.where(inside, pulses[:, moment], 0.0)
        )
        second_diff = next_u - 2.0 * newer_u + older_u
        next_b = (
            2.0 * newer_b - older_b + speed_slab * lap_all[shot_count:] + image_slab * second_diff
        )
        accelerations.append(second_diff)
        predicted.append(next_b[:, receiver_column, receiver_depth])
        older_u, newer_u = (newer_u, next_u)
        older_b, newer_b = (newer_b, next_b)
    adjoint_old, adjoint_new = (adj_after[0], adj_last[0])
    for moment in reversed(range(step_count)):
        padded_adjoint = padded_2(adjoint_new, (("box", 1),), 1)
        adjoint_next = 2.0 * adjoint_new - adjoint_old + speed_slab * laplace_rows(padded_adjoint)
        misfit = predicted[moment] - recorded[:, moment, :]
        adjoint_next = adjoint_next.at[:, receiver_column, receiver_depth].add(misfit)
        gradient = gradient + jnp.sum(adjoint_next * accelerations[moment], axis=0)
        illumination = illumination + jnp.sum(accelerations[moment] * accelerations[moment], axis=0)
        adjoint_old, adjoint_new = (adjoint_new, adjoint_next)

    def to_owner(slab_values):
        blocks = slab_values.reshape(owners, tile_width, depth_cells)
        return jnp.roll(blocks, rotation, axis=0)

    back_grad, back_illum = (
        lax.all_to_all(to_owner(gradient), "box", split_axis=0, concat_axis=0, tiled=True),
        lax.all_to_all(to_owner(illumination), "box", split_axis=0, concat_axis=0, tiled=True),
    )
    empty_rounds = jnp.zeros(owned_tiles.shape, jnp.float32)
    grad_rounds = lax.dynamic_update_slice_in_dim(empty_rounds, back_grad, first_round, 0)
    illum_rounds = lax.dynamic_update_slice_in_dim(empty_rounds, back_illum, first_round, 0)
    total_grad, total_illum = lax.psum((grad_rounds, illum_rounds), "shot")
    migrated = total_grad / jnp.sqrt(total_illum + damping)
    return migrated[:, None]


def solution(mesh):
    return jax.shard_map(
        on_device,
        mesh=mesh,
        in_specs=(
            P("shot", None, "box", None),
            P("shot", None, "box", None),
            P("shot", None, "box", None),
            P("shot", None, "box", None),
            P("shot", None, "box", None),
            P("shot", None, "box", None),
            P("shot", "box", None),
            P("shot", None, None),
            P("shot", None),
            P("shot", "box"),
            P("shot", None, None, "box"),
            P("shot"),
            P(None, "box", None, None),
        ),
        out_specs=P(None, "box", None, None),
        check_vma=False,
    )
```

profile of v0, /device:TPU:0, one launch (start us, length us, event | category | flops | bytes accessed | tf_op | source)
XLA Modules:
  0.0 124.2 jit_solution(1600782998836109316)
XLA Ops:
  0.8 0.6 dynamic-slice_bitcast_fusion
  1.4 6.3 %all-to-all-start = ((f32[8,2,256]{2,1,0:T(2,128)}), f32[8,2,256]{2,1,0:T(2,128)S(1)}, u32[]{:S(2)}, u32[]{:S(2)}) async-start(f32[8,2,256]{2,1,0:T(2,128)} %dynamic-slice_bitcast_fusion), calls=%async_computation | async-start | bytes 32768 | tf_op jit(solution)/shard_map/all_to_all | solution.py:56
  7.7 0.9 fusion.77
  8.6 1.3 %collective-permute-start = (f32[8,1,256]{2,1,0:T(1,128)S(1)}, f32[8,1,256]{2,1,0:T(1,128)S(1)}, u32[]{:S(2)}, u32[]{:S(2)}) collective-permute-start(f32[8,1,256]{2,1,0:T(1,128)S(1)} %get-tuple-element.47), channel_id=1, source_target_pairs={{1,0},{2,1},{3,2},{4,3},{5,4},{6,5},{7,6},{9,8},{10,9},{11,10},{12... | collective-permute-start | bytes 24584 | tf_op jit(solution)/shard_map/ppermute | solution.py:17
  9.9 3.0 %collective-permute-start.1 = (f32[8,1,256]{2,1,0:T(1,128)S(1)}, f32[8,1,256]{2,1,0:T(1,128)S(1)}, u32[]{:S(2)}, u32[]{:S(2)}) collective-permute-start(f32[8,1,256]{2,1,0:T(1,128)S(1)} %get-tuple-element.48), channel_id=1, source_target_pairs={{0,1},{1,2},{2,3},{3,4},{4,5},{5,6},{6,7},{8,9},{9,10},{10,11},{11... | collective-permute-start | bytes 24584 | tf_op jit(solution)/shard_map/ppermute | solution.py:14
  13.0 1.0 fusion.58
  13.9 1.3 %collective-permute-start.2 = (f32[16,1,256]{2,1,0:T(1,128)S(1)}, f32[16,1,256]{2,1,0:T(1,128)S(1)}, u32[]{:S(2)}, u32[]{:S(2)}) collective-permute-start(f32[16,1,256]{2,1,0:T(1,128)S(1)} %get-tuple-element.35), channel_id=1, source_target_pairs={{1,0},{2,1},{3,2},{4,3},{5,4},{6,5},{7,6},{9,8},{10,9},{11,10},{12... | collective-permute-start | bytes 49160 | tf_op jit(solution)/shard_map/ppermute | solution.py:17
  15.2 4.3 %collective-permute-start.3 = (f32[16,1,256]{2,1,0:T(1,128)S(1)}, f32[16,1,256]{2,1,0:T(1,128)S(1)}, u32[]{:S(2)}, u32[]{:S(2)}) collective-permute-start(f32[16,1,256]{2,1,0:T(1,128)S(1)} %get-tuple-element.36), channel_id=1, source_target_pairs={{0,1},{1,2},{2,3},{3,4},{4,5},{5,6},{6,7},{8,9},{9,10},{10,11},{11... | collective-permute-start | bytes 49160 | tf_op jit(solution)/shard_map/ppermute | solution.py:14
  19.5 0.7 fusion.71
  20.2 0.7 bitcast_select_fusion
  20.9 0.7 fusion.73
  21.6 0.8 bitcast_select_fusion.1
  22.4 0.7 copy.55
  23.1 1.0 pad_maximum_fusion
  24.4 1.3 %fusion.2 = f32[16,16,256]{2,1,0:T(8,128)S(1)} fusion(f32[16,16,256]{2,1,0:T(8,128)S(1)} %pad_maximum_fusion, f32[16,1,256]{2,1,0:T(1,128)S(1)} %collective-permute-done.3, f32[8,16,256]{2,1,0:T(8,128)} %bitcast.136, f32[8,16,256]{2,1,0:T(8,128)} %bitcast.133, f32[16,1,256]{2,1,0:T(1,128)S(1)} %collective-permute-done.2), kind=kLoop, calls=%fused_computation.42 | loop fusion | flops 589824 | bytes 819200 | tf_op jit(solution)/shard_map/sub | solution.py:25
  25.7 1.0 fusion.48
  26.8 0.9 scatter_fusion
  27.9 1.3 %collective-permute-start.4 = (f32[16,1,256]{2,1,0:T(1,128)S(1)}, f32[16,1,256]{2,1,0:T(1,128)S(1)}, u32[]{:S(2)}, u32[]{:S(2)}) collective-permute-start(f32[16,1,256]{2,1,0:T(1,128)S(1)} %get-tuple-element.33), channel_id=1, source_target_pairs={{1,0},{2,1},{3,2},{4,3},{5,4},{6,5},{7,6},{9,8},{10,9},{11,10},{12... | collective-permute-start | bytes 49160 | tf_op jit(solution)/shard_map/ppermute | solution.py:17
  29.2 4.3 %collective-permute-start.5 = (f32[16,1,256]{2,1,0:T(1,128)S(1)}, f32[16,1,256]{2,1,0:T(1,128)S(1)}, u32[]{:S(2)}, u32[]{:S(2)}) collective-permute-start(f32[16,1,256]{2,1,0:T(1,128)S(1)} %get-tuple-element.34), channel_id=1, source_target_pairs={{0,1},{1,2},{2,3},{3,4},{4,5},{5,6},{6,7},{8,9},{9,10},{10,11},{11... | collective-permute-start | bytes 49160 | tf_op jit(solution)/shard_map/ppermute | solution.py:14
  33.5 0.6 copy.50
  34.2 0.6 gather_fusion.3
  35.0 0.9 scatter_fusion.1
  36.0 0.7 fusion.47
  36.7 1.3 %collective-permute-start.6 = (f32[16,1,256]{2,1,0:T(1,128)S(1)}, f32[16,1,256]{2,1,0:T(1,128)S(1)}, u32[]{:S(2)}, u32[]{:S(2)}) collective-permute-start(f32[16,1,256]{2,1,0:T(1,128)S(1)} %get-tuple-element.31), channel_id=1, source_target_pairs={{1,0},{2,1},{3,2},{4,3},{5,4},{6,5},{7,6},{9,8},{10,9},{11,10},{12... | collective-permute-start | bytes 49160 | tf_op jit(solution)/shard_map/ppermute | solution.py:17
  38.0 4.3 %collective-permute-start.7 = (f32[16,1,256]{2,1,0:T(1,128)S(1)}, f32[16,1,256]{2,1,0:T(1,128)S(1)}, u32[]{:S(2)}, u32[]{:S(2)}) collective-permute-start(f32[16,1,256]{2,1,0:T(1,128)S(1)} %get-tuple-element.32), channel_id=1, source_target_pairs={{0,1},{1,2},{2,3},{3,4},{4,5},{5,6},{6,7},{8,9},{9,10},{10,11},{11... | collective-permute-start | bytes 49160 | tf_op jit(solution)/shard_map/ppermute | solution.py:14
  42.3 0.6 copy.38
  42.9 0.6 gather_fusion.2
  43.8 0.9 scatter_fusion.2
  44.7 0.7 fusion.44
  45.5 1.3 %collective-permute-start.8 = (f32[16,1,256]{2,1,0:T(1,128)S(1)}, f32[16,1,256]{2,1,0:T(1,128)S(1)}, u32[]{:S(2)}, u32[]{:S(2)}) collective-permute-start(f32[16,1,256]{2,1,0:T(1,128)S(1)} %get-tuple-element.29), channel_id=1, source_target_pairs={{1,0},{2,1},{3,2},{4,3},{5,4},{6,5},{7,6},{9,8},{10,9},{11,10},{12... | collective-permute-start | bytes 49160 | tf_op jit(solution)/shard_map/ppermute | solution.py:17
  46.8 4.4 %collective-permute-start.9 = (f32[16,1,256]{2,1,0:T(1,128)S(1)}, f32[16,1,256]{2,1,0:T(1,128)S(1)}, u32[]{:S(2)}, u32[]{:S(2)}) collective-permute-start(f32[16,1,256]{2,1,0:T(1,128)S(1)} %get-tuple-element.30), channel_id=1, source_target_pairs={{0,1},{1,2},{2,3},{3,4},{4,5},{5,6},{6,7},{8,9},{9,10},{10,11},{11... | collective-permute-start | bytes 49160 | tf_op jit(solution)/shard_map/ppermute | solution.py:14
  51.3 0.6 copy.26
  51.9 0.6 gather_fusion.1
  52.8 0.9 scatter_fusion.3
  53.9 0.6 copy.14
  54.5 0.6 gather_fusion
  55.1 0.6 copy.17
  55.8 0.8 scatter_fusion.4
  56.6 0.6 copy.18
  57.2 1.3 %collective-permute-start.10 = (f32[8,1,256]{2,1,0:T(1,128)S(1)}, f32[8,1,256]{2,1,0:T(1,128)S(1)}, u32[]{:S(2)}, u32[]{:S(2)}) collective-permute-start(f32[8,1,256]{2,1,0:T(1,128)S(1)} %get-tuple-element.45), channel_id=1, source_target_pairs={{1,0},{2,1},{3,2},{4,3},{5,4},{6,5},{7,6},{9,8},{10,9},{11,10},{12... | collective-permute-start | bytes 24584 | tf_op jit(solution)/shard_map/ppermute | solution.py:17
  58.5 4.4 %collective-permute-start.11 = (f32[8,1,256]{2,1,0:T(1,128)S(1)}, f32[8,1,256]{2,1,0:T(1,128)S(1)}, u32[]{:S(2)}, u32[]{:S(2)}) collective-permute-start(f32[8,1,256]{2,1,0:T(1,128)S(1)} %get-tuple-element.46), channel_id=1, source_target_pairs={{0,1},{1,2},{2,3},{3,4},{4,5},{5,6},{6,7},{8,9},{9,10},{10,11},{11... | collective-permute-start | bytes 24584 | tf_op jit(solution)/shard_map/ppermute | solution.py:14
  63.0 0.8 collective-permute-done.11
  63.9 0.6 copy.28
  64.5 0.9 scatter_fusion.5
  65.4 0.6 copy.29
  66.0 1.3 %collective-permute-start.12 = (f32[8,1,256]{2,1,0:T(1,128)S(1)}, f32[8,1,256]{2,1,0:T(1,128)S(1)}, u32[]{:S(2)}, u32[]{:S(2)}) collective-permute-start(f32[8,1,256]{2,1,0:T(1,128)S(1)} %get-tuple-element.43), channel_id=1, source_target_pairs={{1,0},{2,1},{3,2},{4,3},{5,4},{6,5},{7,6},{9,8},{10,9},{11,10},{12... | collective-permute-start | bytes 24584 | tf_op jit(solution)/shard_map/ppermute | solution.py:17
  67.3 4.4 %collective-permute-start.13 = (f32[8,1,256]{2,1,0:T(1,128)S(1)}, f32[8,1,256]{2,1,0:T(1,128)S(1)}, u32[]{:S(2)}, u32[]{:S(2)}) collective-permute-start(f32[8,1,256]{2,1,0:T(1,128)S(1)} %get-tuple-element.44), channel_id=1, source_target_pairs={{0,1},{1,2},{2,3},{3,4},{4,5},{5,6},{6,7},{8,9},{9,10},{10,11},{11... | collective-permute-start | bytes 24584 | tf_op jit(solution)/shard_map/ppermute | solution.py:14
  71.7 0.8 collective-permute-done.13
  72.6 0.6 copy.40
  73.3 0.9 scatter_fusion.6
  74.7 1.3 %collective-permute-start.14 = (f32[8,1,256]{2,1,0:T(1,128)S(1)}, f32[8,1,256]{2,1,0:T(1,128)S(1)}, u32[]{:S(2)}, u32[]{:S(2)}) collective-permute-start(f32[8,1,256]{2,1,0:T(1,128)S(1)} %get-tuple-element.41), channel_id=1, source_target_pairs={{1,0},{2,1},{3,2},{4,3},{5,4},{6,5},{7,6},{9,8},{10,9},{11,10},{12... | collective-permute-start | bytes 24584 | tf_op jit(solution)/shard_map/ppermute | solution.py:17
  76.0 4.8 %collective-permute-start.15 = (f32[8,1,256]{2,1,0:T(1,128)S(1)}, f32[8,1,256]{2,1,0:T(1,128)S(1)}, u32[]{:S(2)}, u32[]{:S(2)}) collective-permute-start(f32[8,1,256]{2,1,0:T(1,128)S(1)} %get-tuple-element.42), channel_id=1, source_target_pairs={{0,1},{1,2},{2,3},{3,4},{4,5},{5,6},{6,7},{8,9},{9,10},{10,11},{11... | collective-permute-start | bytes 24584 | tf_op jit(solution)/shard_map/ppermute | solution.py:14
  80.8 0.8 collective-permute-done.15
  81.8 0.6 copy.52
  82.4 0.9 scatter_fusion.7
  83.3 0.6 copy.53
  83.9 0.6 fusion.60
  84.6 7.7 %all-to-all-start.2 = ((f32[8,2,256]{2,1,0:T(2,128)}), f32[8,2,256]{2,1,0:T(2,128)S(1)}, u32[]{:S(2)}, u32[]{:S(2)}) async-start(f32[8,2,256]{2,1,0:T(2,128)} %fusion.60), calls=%async_computation.2 | async-start | bytes 32768 | tf_op jit(solution)/shard_map/all_to_all | solution.py:109
  92.3 0.6 fusion.61
  92.9 5.0 %all-to-all-done.2 = f32[8,2,256]{2,1,0:T(2,128)S(1)} async-done(((f32[8,2,256]{2,1,0:T(2,128)}), f32[8,2,256]{2,1,0:T(2,128)S(1)}, u32[]{:S(2)}, u32[]{:S(2)}) %all-to-all-start.2) | async-done | bytes 16416 | tf_op jit(solution)/shard_map/all_to_all | solution.py:109
  97.9 3.3 %all-to-all-start.1 = ((f32[8,2,256]{2,1,0:T(2,128)}), f32[8,2,256]{2,1,0:T(2,128)S(1)}, u32[]{:S(2)}, u32[]{:S(2)}) async-start(f32[8,2,256]{2,1,0:T(2,128)} %fusion.61), calls=%async_computation.1 | async-start | bytes 32768 | tf_op jit(solution)/shard_map/all_to_all | solution.py:108
  101.3 5.6 %all-to-all-done.1 = f32[8,2,256]{2,1,0:T(2,128)S(1)} async-done(((f32[8,2,256]{2,1,0:T(2,128)}), f32[8,2,256]{2,1,0:T(2,128)S(1)}, u32[]{:S(2)}, u32[]{:S(2)}) %all-to-all-start.1) | async-done | bytes 16416 | tf_op jit(solution)/shard_map/all_to_all | solution.py:108
  106.9 16.7 %all-reduce.8 = (f32[12,2,256]{2,1,0:T(2,128)S(1)}, f32[12,2,256]{2,1,0:T(2,128)S(1)}) all-reduce(f32[12,2,256]{2,1,0:T(2,128)S(1)} %constant_dynamic-update-slice_fusion.1, f32[12,2,256]{2,1,0:T(2,128)S(1)} %constant_dynamic-update-slice_fusion), channel_id=1, replica_groups=mesh['shot'=4,'box'=8] {'shot'}, use_global_device_ids=true, to_apply=%region_12.14 | all-reduce | flops 12288 | bytes 98304 | tf_op jit(solution)/shard_map/psum | solution.py:114
  123.6 0.6 multiply_bitcast_fusion
  (75 shorter events, 2.8 us)
Async XLA Ops:
  0.0 0.8 copy-start
  0.0 27.8 %copy-start.1 = (f32[1,8,16,256]{3,2,1,0:T(8,128)S(1)}, f32[1,8,16,256]{3,2,1,0:T(8,128)}, u32[]{:S(2)}) copy-start(f32[1,8,16,256]{3,2,1,0:T(8,128)} %param.16) | copy-start | bytes 393220
  0.0 27.8 %copy-start.2 = (f32[1,8,16,256]{3,2,1,0:T(8,128)S(1)}, f32[1,8,16,256]{3,2,1,0:T(8,128)}, u32[]{:S(2)}) copy-start(f32[1,8,16,256]{3,2,1,0:T(8,128)} %param.18) | copy-start | bytes 393220
  0.0 27.8 %copy-start.5 = (f32[1,8,16,256]{3,2,1,0:T(8,128)S(1)}, f32[1,8,16,256]{3,2,1,0:T(8,128)}, u32[]{:S(2)}) copy-start(f32[1,8,16,256]{3,2,1,0:T(8,128)} %param.15) | copy-start | bytes 393220
  0.0 27.8 %copy-start.3 = (f32[1,16,256]{2,1,0:T(8,128)S(1)}, f32[1,16,256]{2,1,0:T(8,128)}, u32[]{:S(2)}) copy-start(f32[1,16,256]{2,1,0:T(8,128)} %param.21) | copy-start | bytes 49156
  0.0 27.8 %copy-start.8 = (f32[1,8,16,256]{3,2,1,0:T(8,128)S(1)}, f32[1,8,16,256]{3,2,1,0:T(8,128)}, u32[]{:S(2)}) copy-start(f32[1,8,16,256]{3,2,1,0:T(8,128)} %param.17) | copy-start | bytes 393220
  1.4 26.3 %all-to-all-start = ((f32[8,2,256]{2,1,0:T(2,128)}), f32[8,2,256]{2,1,0:T(2,128)S(1)}, u32[]{:S(2)}, u32[]{:S(2)}) async-start(f32[8,2,256]{2,1,0:T(2,128)} %dynamic-slice_bitcast_fusion), calls=%async_computation | async-start | bytes 32768 | tf_op jit(solution)/shard_map/all_to_all | solution.py:56
  8.6 45.1 %collective-permute-start = (f32[8,1,256]{2,1,0:T(1,128)S(1)}, f32[8,1,256]{2,1,0:T(1,128)S(1)}, u32[]{:S(2)}, u32[]{:S(2)}) collective-permute-start(f32[8,1,256]{2,1,0:T(1,128)S(1)} %get-tuple-element.47), channel_id=1, source_target_pairs={{1,0},{2,1},{3,2},{4,3},{5,4},{6,5},{7,6},{9,8},{10,9},{11,10},{12... | collective-permute-start | bytes 24584 | tf_op jit(solution)/shard_map/ppermute | solution.py:17
  9.9 43.8 %collective-permute-start.1 = (f32[8,1,256]{2,1,0:T(1,128)S(1)}, f32[8,1,256]{2,1,0:T(1,128)S(1)}, u32[]{:S(2)}, u32[]{:S(2)}) collective-permute-start(f32[8,1,256]{2,1,0:T(1,128)S(1)} %get-tuple-element.48), channel_id=1, source_target_pairs={{0,1},{1,2},{2,3},{3,4},{4,5},{5,6},{6,7},{8,9},{9,10},{10,11},{11... | collective-permute-start | bytes 24584 | tf_op jit(solution)/shard_map/ppermute | solution.py:14
  13.9 10.5 %collective-permute-start.2 = (f32[16,1,256]{2,1,0:T(1,128)S(1)}, f32[16,1,256]{2,1,0:T(1,128)S(1)}, u32[]{:S(2)}, u32[]{:S(2)}) collective-permute-start(f32[16,1,256]{2,1,0:T(1,128)S(1)} %get-tuple-element.35), channel_id=1, source_target_pairs={{1,0},{2,1},{3,2},{4,3},{5,4},{6,5},{7,6},{9,8},{10,9},{11,10},{12... | collective-permute-start | bytes 49160 | tf_op jit(solution)/shard_map/ppermute | solution.py:17
  15.2 9.2 %collective-permute-start.3 = (f32[16,1,256]{2,1,0:T(1,128)S(1)}, f32[16,1,256]{2,1,0:T(1,128)S(1)}, u32[]{:S(2)}, u32[]{:S(2)}) collective-permute-start(f32[16,1,256]{2,1,0:T(1,128)S(1)} %get-tuple-element.36), channel_id=1, source_target_pairs={{0,1},{1,2},{2,3},{3,4},{4,5},{5,6},{6,7},{8,9},{9,10},{10,11},{11... | collective-permute-start | bytes 49160 | tf_op jit(solution)/shard_map/ppermute | solution.py:14
  27.9 6.8 %collective-permute-start.4 = (f32[16,1,256]{2,1,0:T(1,128)S(1)}, f32[16,1,256]{2,1,0:T(1,128)S(1)}, u32[]{:S(2)}, u32[]{:S(2)}) collective-permute-start(f32[16,1,256]{2,1,0:T(1,128)S(1)} %get-tuple-element.33), channel_id=1, source_target_pairs={{1,0},{2,1},{3,2},{4,3},{5,4},{6,5},{7,6},{9,8},{10,9},{11,10},{12... | collective-permute-start | bytes 49160 | tf_op jit(solution)/shard_map/ppermute | solution.py:17
  29.2 5.5 %collective-permute-start.5 = (f32[16,1,256]{2,1,0:T(1,128)S(1)}, f32[16,1,256]{2,1,0:T(1,128)S(1)}, u32[]{:S(2)}, u32[]{:S(2)}) collective-permute-start(f32[16,1,256]{2,1,0:T(1,128)S(1)} %get-tuple-element.34), channel_id=1, source_target_pairs={{0,1},{1,2},{2,3},{3,4},{4,5},{5,6},{6,7},{8,9},{9,10},{10,11},{11... | collective-permute-start | bytes 49160 | tf_op jit(solution)/shard_map/ppermute | solution.py:14
  36.7 6.8 %collective-permute-start.6 = (f32[16,1,256]{2,1,0:T(1,128)S(1)}, f32[16,1,256]{2,1,0:T(1,128)S(1)}, u32[]{:S(2)}, u32[]{:S(2)}) collective-permute-start(f32[16,1,256]{2,1,0:T(1,128)S(1)} %get-tuple-element.31), channel_id=1, source_target_pairs={{1,0},{2,1},{3,2},{4,3},{5,4},{6,5},{7,6},{9,8},{10,9},{11,10},{12... | collective-permute-start | bytes 49160 | tf_op jit(solution)/shard_map/ppermute | solution.py:17
  38.0 5.5 %collective-permute-start.7 = (f32[16,1,256]{2,1,0:T(1,128)S(1)}, f32[16,1,256]{2,1,0:T(1,128)S(1)}, u32[]{:S(2)}, u32[]{:S(2)}) collective-permute-start(f32[16,1,256]{2,1,0:T(1,128)S(1)} %get-tuple-element.32), channel_id=1, source_target_pairs={{0,1},{1,2},{2,3},{3,4},{4,5},{5,6},{6,7},{8,9},{9,10},{10,11},{11... | collective-permute-start | bytes 49160 | tf_op jit(solution)/shard_map/ppermute | solution.py:14
  45.5 7.0 %collective-permute-start.8 = (f32[16,1,256]{2,1,0:T(1,128)S(1)}, f32[16,1,256]{2,1,0:T(1,128)S(1)}, u32[]{:S(2)}, u32[]{:S(2)}) collective-permute-start(f32[16,1,256]{2,1,0:T(1,128)S(1)} %get-tuple-element.29), channel_id=1, source_target_pairs={{1,0},{2,1},{3,2},{4,3},{5,4},{6,5},{7,6},{9,8},{10,9},{11,10},{12... | collective-permute-start | bytes 49160 | tf_op jit(solution)/shard_map/ppermute | solution.py:17
  46.8 5.7 %collective-permute-start.9 = (f32[16,1,256]{2,1,0:T(1,128)S(1)}, f32[16,1,256]{2,1,0:T(1,128)S(1)}, u32[]{:S(2)}, u32[]{:S(2)}) collective-permute-start(f32[16,1,256]{2,1,0:T(1,128)S(1)} %get-tuple-element.30), channel_id=1, source_target_pairs={{0,1},{1,2},{2,3},{3,4},{4,5},{5,6},{6,7},{8,9},{9,10},{10,11},{11... | collective-permute-start | bytes 49160 | tf_op jit(solution)/shard_map/ppermute | solution.py:14
  51.2 2.5 %copy-start.4 = (f32[1,8,16,256]{3,2,1,0:T(8,128)S(1)}, f32[1,8,16,256]{3,2,1,0:T(8,128)}, u32[]{:S(2)}) copy-start(f32[1,8,16,256]{3,2,1,0:T(8,128)} %param.20) | copy-start | bytes 393220
  51.3 2.5 %copy-start.9 = (f32[1,8,16,256]{3,2,1,0:T(8,128)S(1)}, f32[1,8,16,256]{3,2,1,0:T(8,128)}, u32[]{:S(2)}) copy-start(f32[1,8,16,256]{3,2,1,0:T(8,128)} %param.19) | copy-start | bytes 393220
  57.2 5.7 %collective-permute-start.10 = (f32[8,1,256]{2,1,0:T(1,128)S(1)}, f32[8,1,256]{2,1,0:T(1,128)S(1)}, u32[]{:S(2)}, u32[]{:S(2)}) collective-permute-start(f32[8,1,256]{2,1,0:T(1,128)S(1)} %get-tuple-element.45), channel_id=1, source_target_pairs={{1,0},{2,1},{3,2},{4,3},{5,4},{6,5},{7,6},{9,8},{10,9},{11,10},{12... | collective-permute-start | bytes 24584 | tf_op jit(solution)/shard_map/ppermute | solution.py:17
  58.5 5.2 %collective-permute-start.11 = (f32[8,1,256]{2,1,0:T(1,128)S(1)}, f32[8,1,256]{2,1,0:T(1,128)S(1)}, u32[]{:S(2)}, u32[]{:S(2)}) collective-permute-start(f32[8,1,256]{2,1,0:T(1,128)S(1)} %get-tuple-element.46), channel_id=1, source_target_pairs={{0,1},{1,2},{2,3},{3,4},{4,5},{5,6},{6,7},{8,9},{9,10},{10,11},{11... | collective-permute-start | bytes 24584 | tf_op jit(solution)/shard_map/ppermute | solution.py:14
  66.0 5.7 %collective-permute-start.12 = (f32[8,1,256]{2,1,0:T(1,128)S(1)}, f32[8,1,256]{2,1,0:T(1,128)S(1)}, u32[]{:S(2)}, u32[]{:S(2)}) collective-permute-start(f32[8,1,256]{2,1,0:T(1,128)S(1)} %get-tuple-element.43), channel_id=1, source_target_pairs={{1,0},{2,1},{3,2},{4,3},{5,4},{6,5},{7,6},{9,8},{10,9},{11,10},{12... | collective-permute-start | bytes 24584 | tf_op jit(solution)/shard_map/ppermute | solution.py:17
  67.3 5.2 %collective-permute-start.13 = (f32[8,1,256]{2,1,0:T(1,128)S(1)}, f32[8,1,256]{2,1,0:T(1,128)S(1)}, u32[]{:S(2)}, u32[]{:S(2)}) collective-permute-start(f32[8,1,256]{2,1,0:T(1,128)S(1)} %get-tuple-element.44), channel_id=1, source_target_pairs={{0,1},{1,2},{2,3},{3,4},{4,5},{5,6},{6,7},{8,9},{9,10},{10,11},{11... | collective-permute-start | bytes 24584 | tf_op jit(solution)/shard_map/ppermute | solution.py:14
  72.6 9.0 %copy-start.6 = (f32[8,16,256]{2,1,0:T(8,128)S(1)}, f32[8,16,256]{2,1,0:T(8,128)}, u32[]{:S(2)}) copy-start(f32[8,16,256]{2,1,0:T(8,128)} %get-tuple-element.26) | copy-start | bytes 393220
  72.6 9.0 %copy-start.7 = (f32[8,16,256]{2,1,0:T(8,128)S(1)}, f32[8,16,256]{2,1,0:T(8,128)}, u32[]{:S(2)}) copy-start(f32[8,16,256]{2,1,0:T(8,128)} %get-tuple-element.24) | copy-start | bytes 393220
  74.7 6.1 %collective-permute-start.14 = (f32[8,1,256]{2,1,0:T(1,128)S(1)}, f32[8,1,256]{2,1,0:T(1,128)S(1)}, u32[]{:S(2)}, u32[]{:S(2)}) collective-permute-start(f32[8,1,256]{2,1,0:T(1,128)S(1)} %get-tuple-element.41), channel_id=1, source_target_pairs={{1,0},{2,1},{3,2},{4,3},{5,4},{6,5},{7,6},{9,8},{10,9},{11,10},{12... | collective-permute-start | bytes 24584 | tf_op jit(solution)/shard_map/ppermute | solution.py:17
  76.0 5.6 %collective-permute-start.15 = (f32[8,1,256]{2,1,0:T(1,128)S(1)}, f32[8,1,256]{2,1,0:T(1,128)S(1)}, u32[]{:S(2)}, u32[]{:S(2)}) collective-permute-start(f32[8,1,256]{2,1,0:T(1,128)S(1)} %get-tuple-element.42), channel_id=1, source_target_pairs={{0,1},{1,2},{2,3},{3,4},{4,5},{5,6},{6,7},{8,9},{9,10},{10,11},{11... | collective-permute-start | bytes 24584 | tf_op jit(solution)/shard_map/ppermute | solution.py:14
  84.6 13.3 %all-to-all-start.2 = ((f32[8,2,256]{2,1,0:T(2,128)}), f32[8,2,256]{2,1,0:T(2,128)S(1)}, u32[]{:S(2)}, u32[]{:S(2)}) async-start(f32[8,2,256]{2,1,0:T(2,128)} %fusion.60), calls=%async_computation.2 | async-start | bytes 32768 | tf_op jit(solution)/shard_map/all_to_all | solution.py:109
  97.9 8.9 %all-to-all-start.1 = ((f32[8,2,256]{2,1,0:T(2,128)}), f32[8,2,256]{2,1,0:T(2,128)S(1)}, u32[]{:S(2)}, u32[]{:S(2)}) async-start(f32[8,2,256]{2,1,0:T(2,128)} %fusion.61), calls=%async_computation.1 | async-start | bytes 32768 | tf_op jit(solution)/shard_map/all_to_all | solution.py:108
where the time goes:
time: 125 us; the launch traced here: 124 us
  starting transfers between devices  61.5 us (49%)
  other arithmetic  19.3 us (15%)
  blocking collectives  16.7 us (13%)
  waiting for transfers between devices  12.9 us (10%)
  local copies, waits for them, and re-layouts  12.3 us (10%)
  between operations  1.49 us (1%)
    ppermute x8, starting transfers between devices, padded_2(): lax.ppermute(lax.slice_in_dim(block, block.shape[dim] - width, None, axis...  33.8 us
    psum x1, blocking collectives, on_device(): total_grad, total_illum = lax.psum((grad_rounds, illum_rounds), 'shot')  16.7 us
    ppermute x8, starting transfers between devices, padded_2(): lax.ppermute(lax.slice_in_dim(block, 0, width, axis=dim), axis, backward)  10.3 us
    all_to_all x1, starting transfers between devices, on_device(): lax.all_to_all(to_owner(illumination), 'box', split_axis=0, concat_axis=0...  7.69 us
    all_to_all x1, starting transfers between devices, on_device(): lax.all_to_all(outgoing, 'box', split_axis=0, concat_axis=0, tiled=True)  6.34 us
    all_to_all x1, waiting for transfers between devices, on_device(): lax.all_to_all(to_owner(gradient), 'box', split_axis=0, concat_axis=0, ti...  5.55 us
    all_to_all x1, waiting for transfers between devices, on_device(): lax.all_to_all(to_owner(illumination), 'box', split_axis=0, concat_axis=0...  5 us
    scatter-add x4, other arithmetic, on_device(): next_u.at[shot_lane, column, source_depth]  3.7 us
  transfers between devices with their start and end apart: 19, of which 5 were waited for; matrix products, arithmetic and copies ran while one was open for 16% of the time, Pallas kernels for 0%

commit v1 on v0

v1 whole, which is shorter than its diff:
```python
import functools

import jax
import jax.numpy as jnp
from jax import lax
from jax.experimental import pallas as pl
from jax.experimental.pallas import tpu as pltpu
from jax.sharding import PartitionSpec as P

damping = 1.0
LANES = 128
MARGIN = 8
STEPS = 4
HALO = (
    ("un", 0, 7),
    ("up", 0, 6),
    ("bn", 0, 7),
    ("bp", 0, 6),
    ("un", 1, 4),
    ("up", 1, 3),
    ("qn", 0, 4),
    ("qn", 1, 4),
    ("qp", 0, 3),
    ("qp", 1, 3),
)
HALO_TILES = sum(count for _, _, count in HALO)
SPEED_TILE = HALO_TILES
META_TILE = HALO_TILES + 2
PACK_TILES = HALO_TILES + 3
VMEM = pltpu.VMEM
SMEM = pltpu.SMEM


def lane_iota():
    return lax.broadcasted_iota(jnp.int32, (8, LANES), 1)


def pack_kernel(
    first, rec, un, up, bn, bp, qn, qp, speed, obs, refl, pack_a, pack_b, image_out, *, owners
):
    columns, depth = speed.shape[1], speed.shape[2]
    rounds = refl.shape[0]
    tiles = columns // 2
    position = lax.axis_index("box")
    even = lax.rem(position, 2) == 0
    refs = {"un": un, "up": up, "bn": bn, "bp": bp, "qn": qn, "qp": qp}

    for target in range(owners):
        low_tile = first[0] + tiles * target - 3
        r0 = lax.div(low_tile - position + 2 * owners - 1, owners) - 1
        for slot in range(2):
            r = jnp.clip(r0 + slot, 0, rounds - 1)
            image_out[target, 2 * slot : 2 * slot + 2, :] = refl[r, 0, :, 0:LANES]

    def put(tile, left, right):
        pack_a[tile] = jnp.where(even, right, left)
        pack_b[tile] = jnp.where(even, left, right)

    tile = 0
    for name, half, count in HALO:
        part = slice(half * LANES, (half + 1) * LANES)
        low = jnp.swapaxes(refs[name][0, :, 0:8, part], 0, 1)
        high = jnp.swapaxes(refs[name][0, :, columns - 8 : columns, part], 0, 1)
        for j in range(1, count + 1):
            put(tile, low[j - 1], high[8 - j])
            tile += 1
    for half in range(2):
        part = slice(half * LANES, (half + 1) * LANES)
        put(SPEED_TILE + half, speed[0, 0:8, part], speed[0, columns - 8 : columns, part])

    lane = lane_iota()
    count = rec.shape[1]

    def meta(right):
        out = jnp.zeros((8, LANES), jnp.float32)
        for k in range(2):
            r = count - 1 - k if right else k
            for t in range(STEPS):
                value = jnp.broadcast_to(obs[0, :, t, r : r + 1], (8, LANES))
                out = jnp.where(lane == 2 * t + k, value, out)
            column = lax.div(rec[0, r], depth) - position * columns
            distance = columns - column if right else column + 1
            code = distance * depth + lax.rem(rec[0, r], depth)
            out = jnp.where(lane == 2 * STEPS + k, code.astype(jnp.float32), out)
        return out

    put(META_TILE, meta(False), meta(True))


def wave_kernel(
    first,
    sources,
    rec,
    un,
    up,
    bn,
    bp,
    qn,
    qp,
    speed,
    obs,
    wavelet,
    pack_a,
    pack_b,
    image_in,
    out,
    u0,
    u1,
    b0,
    b1,
    q0,
    q1,
    vel,
    img,
    acc,
    *,
    owners,
    groups,
):
    columns, depth = speed.shape[1], speed.shape[2]
    tiles = columns // 2
    position = lax.axis_index("box")
    even = lax.rem(position, 2) == 0
    lane = lane_iota()
    first_lane = lane == 0
    last_lane = lane == LANES - 1
    zero = jnp.zeros((8, LANES), jnp.float32)
    halves = (slice(0, LANES), slice(LANES, 2 * LANES))
    scratch = {"un": u0, "up": u1, "bn": b0, "bp": b1, "qn": q0, "qp": q1}

    for name, ref in (("un", un), ("up", up), ("qn", qn), ("qp", qp)):
        for c in range(0, columns, 8):
            scratch[name][MARGIN + c : MARGIN + c + 8] = jnp.swapaxes(ref[0, :, c : c + 8, :], 0, 1)
    for name, ref in (("bn", bn), ("bp", bp)):
        for c in range(0, columns, 8):
            scratch[name][MARGIN + c : MARGIN + c + 8] = jnp.swapaxes(
                ref[0, :, c : c + 8, 0:LANES], 0, 1
            )
    for c in range(columns):
        vel[MARGIN + c] = jnp.broadcast_to(speed[0, c : c + 1, :], (8, depth))

    def got(tile):
        a, b = pack_a[tile], pack_b[tile]
        return jnp.where(even, b, a), jnp.where(even, a, b)

    tile = 0
    for name, half, count in HALO:
        for j in range(1, count + 1):
            left, right = got(tile)
            scratch[name][MARGIN - j, :, halves[half]] = left
            scratch[name][MARGIN + columns - 1 + j, :, halves[half]] = right
            tile += 1
    for half, count in ((0, 6), (1, 3)):
        left, right = got(SPEED_TILE + half)
        for j in range(1, count + 1):
            vel[MARGIN - j, :, halves[half]] = jnp.broadcast_to(left[8 - j : 9 - j], (8, LANES))
            vel[MARGIN + columns - 1 + j, :, halves[half]] = jnp.broadcast_to(
                right[j - 1 : j], (8, LANES)
            )
    meta_left, meta_right = got(META_TILE)

    low_tile = first[0] + tiles * position - 3 + owners
    for m in range(tiles + 6):
        owner = lax.rem(low_tile + m, owners)
        pair = image_in[owner, 2 * (m // owners) : 2 * (m // owners) + 2, :]
        for w in range(2):
            img[MARGIN - 6 + 2 * m + w] = jnp.broadcast_to(pair[w : w + 1], (8, LANES))

    shot = lax.broadcasted_iota(jnp.int32, (8, LANES), 0)
    cell = jnp.zeros((8, LANES), jnp.int32)
    for s in range(8):
        cell = jnp.where(shot == s, sources[0, s] - position * columns * depth, cell)
    cell = cell - lane
    pulses = [jnp.broadcast_to(wavelet[0, :, t : t + 1], (8, LANES)) for t in range(STEPS)]

    def receiver(c):
        if c < 0 or c >= columns:
            j = -c if c < 0 else c - columns + 1
            meta = meta_left if c < 0 else meta_right
            k = (j - 1) // 2
            lane_of = 2 * STEPS + k
            code = jnp.broadcast_to(meta[:, lane_of : lane_of + 1], (8, LANES))
            mask = code == (lane + j * depth).astype(jnp.float32)
            return mask, lambda t: jnp.broadcast_to(
                meta[:, 2 * t + k : 2 * t + k + 1], (8, LANES)
            )
        r = c // 2
        here = rec[0, r] - (position * columns + c) * depth
        mask = lane == here
        return mask, lambda t: jnp.broadcast_to(obs[0, :, t, r : r + 1], (8, LANES))

    def up_down(xs):
        rolled_up = [pltpu.roll(x, 1, 1) for x in xs]
        rolled_down = [pltpu.roll(x, LANES - 1, 1) for x in xs]
        if len(xs) == 1:
            return [jnp.where(first_lane, 0.0, rolled_up[0]) + rolled_down[0]]
        return [
            jnp.where(first_lane, 0.0, rolled_up[0])
            + jnp.where(last_lane, rolled_down[1], rolled_down[0]),
            jnp.where(first_lane, rolled_up[0], rolled_up[1])
            + jnp.where(last_lane, 0.0, rolled_down[1]),
        ]

    def lap(ref, e, count):
        mid = [ref[e, :, halves[h]] for h in range(count)]
        depthwise = up_down(mid)
        return mid, [
            ref[e - 1, :, halves[h]] + ref[e + 1, :, halves[h]] + depthwise[h] - 4.0 * mid[h]
            for h in range(count)
        ]

    new_u, old_u, new_b, old_b = u0, u1, b0, b1
    misfits = []
    for t in range(STEPS):
        wide, narrow = 6 - t, 3 - t
        for c in range(-wide, columns + wide):
            e = MARGIN + c
            count = 2 if -narrow <= c < columns + narrow else 1
            mid, laps = lap(new_u, e, count)
            for h in range(count):
                hit = cell == c * depth + h * LANES
                a = vel[e, :, halves[h]] * laps[h] + jnp.where(hit, pulses[t], 0.0)
                acc[t, e, :, halves[h]] = a
                old_u[e, :, halves[h]] = 2.0 * mid[h] - old_u[e, :, halves[h]] + a
            (mid_b,), (lap_b,) = lap(new_b, e, 1)
            old_b[e] = (
                2.0 * mid_b
                - old_b[e]
                + vel[e, :, halves[0]] * lap_b
                + img[e] * acc[t, e, :, halves[0]]
            )
        new_u, old_u = old_u, new_u
        new_b, old_b = old_b, new_b
        part = {}
        for c in range(-t, columns + t):
            mask, recorded = receiver(c)
            part[c] = jnp.where(mask, new_b[MARGIN + c] - recorded(t), 0.0)
        misfits.append(part)

    grad = [[zero, zero] for _ in range(columns)]
    new_q, old_q = q0, q1
    for t in reversed(range(STEPS)):
        for c in range(-t, columns + t):
            e = MARGIN + c
            mid, laps = lap(new_q, e, 2)
            for h in range(2):
                q = 2.0 * mid[h] - old_q[e, :, halves[h]] + vel[e, :, halves[h]] * laps[h]
                if h == 0:
                    q = q + misfits[t][c]
                old_q[e, :, halves[h]] = q
                if 0 <= c < columns:
                    grad[c][h] = grad[c][h] + q * acc[t, e, :, halves[h]]
        new_q, old_q = old_q, new_q

    start = jnp.full((1, LANES), first[0].astype(jnp.float32))
    for k in range(tiles):
        owner = lax.rem(first[0] + tiles * position + k, owners)
        rows = []
        for h in range(2):
            for w in range(2):
                rows.append(jnp.sum(grad[2 * k + w][h], axis=0, keepdims=True))
        for h in range(2):
            for w in range(2):
                e = MARGIN + 2 * k + w
                total = zero
                for t in range(STEPS):
                    a = acc[t, e, :, halves[h]]
                    total = total + a * a
                rows.append(jnp.sum(total, axis=0, keepdims=True))
        for group in range(groups):
            for i, row in enumerate(rows):
                out[group * owners + owner, :, i * LANES : (i + 1) * LANES] = row
            out[group * owners + owner, :, 8 * LANES : 9 * LANES] = start


def join_kernel(received, migrated, total, *, owners, groups):
    position = lax.axis_index("box")
    total[...] = jnp.zeros_like(total)
    for group in range(groups):
        start = received[group * owners, 0, 8 * LANES].astype(jnp.int32)
        base = lax.div(start - position + owners - 1, owners)
        for p in range(owners):
            total[base + p] = total[base + p] + received[group * owners + p, :, 0 : 8 * LANES]
    for r in range(migrated.shape[0]):
        grad = total[r, :, 0 : 4 * LANES]
        illum = total[r, :, 4 * LANES : 8 * LANES]
        image = grad / jnp.sqrt(illum + damping)
        for h in range(2):
            for w in range(2):
                i = 2 * h + w
                migrated[r, 0, w : w + 1, h * LANES : (h + 1) * LANES] = image[
                    :, i * LANES : (i + 1) * LANES
                ]


def on_device(
    u_prev,
    u_now,
    born_prev,
    born_now,
    adj_after,
    adj_last,
    velocity,
    wavelet,
    sources,
    receivers,
    observed,
    first_tile,
    reflectivity,
):
    owners = lax.axis_size("box")
    groups = lax.axis_size("shot")
    columns, depth = velocity.shape[1], velocity.shape[2]
    rounds = reflectivity.shape[0]
    smem, vmem = pl.BlockSpec(memory_space=SMEM), pl.BlockSpec(memory_space=VMEM)
    f32 = jnp.float32
    params = pltpu.CompilerParams(vmem_limit_bytes=48 * 1024 * 1024)
    fields = (u_now, u_prev, born_now, born_prev, adj_last, adj_after)

    pack = jax.ShapeDtypeStruct((PACK_TILES, 8, LANES), f32)
    send_a, send_b, image_out = pl.pallas_call(
        functools.partial(pack_kernel, owners=owners),
        out_shape=(pack, pack, jax.ShapeDtypeStruct((owners, 4, LANES), f32)),
        in_specs=[smem] * 2 + [vmem] * 9,
        out_specs=(vmem,) * 3,
        compiler_params=params,
        name="pack",
    )(first_tile, receivers, *fields, velocity, observed, reflectivity)

    image_in = lax.all_to_all(image_out, "box", split_axis=0, concat_axis=0, tiled=True)
    swap_a = [(i, i ^ 1) for i in range(owners)]
    swap_b = [(i, i + 1 if i % 2 else i - 1) for i in range(1, owners - 1)]
    got_a = lax.ppermute(send_a, "box", swap_a)
    got_b = lax.ppermute(send_b, "box", swap_b)

    ext = columns + 2 * MARGIN
    out = pl.pallas_call(
        functools.partial(wave_kernel, owners=owners, groups=groups),
        out_shape=jax.ShapeDtypeStruct((groups * owners, 1, 9 * LANES), f32),
        in_specs=[smem] * 3 + [vmem] * 12,
        out_specs=vmem,
        scratch_shapes=[
            VMEM((ext, 8, depth), f32),
            VMEM((ext, 8, depth), f32),
            VMEM((ext, 8, LANES), f32),
            VMEM((ext, 8, LANES), f32),
            VMEM((ext, 8, depth), f32),
            VMEM((ext, 8, depth), f32),
            VMEM((ext, 8, depth), f32),
            VMEM((ext, 8, LANES), f32),
            VMEM((STEPS, ext, 8, depth), f32),
        ],
        compiler_params=params,
        name="waves",
    )(
        first_tile,
        sources,
        receivers,
        *fields,
        velocity,
        observed,
        wavelet,
        got_a,
        got_b,
        image_in,
    )

    received = lax.all_to_all(out, ("shot", "box"), split_axis=0, concat_axis=0, tiled=True)
    return pl.pallas_call(
        functools.partial(join_kernel, owners=owners, groups=groups),
        out_shape=jax.ShapeDtypeStruct(reflectivity.shape, f32),
        in_specs=[vmem],
        out_specs=vmem,
        scratch_shapes=[VMEM((rounds, 1, 8 * LANES), f32)],
        compiler_params=params,
        name="join",
    )(received)


def solution(mesh):
    return jax.shard_map(
        on_device,
        mesh=mesh,
        in_specs=(
            P("shot", None, "box", None),
            P("shot", None, "box", None),
            P("shot", None, "box", None),
            P("shot", None, "box", None),
            P("shot", None, "box", None),
            P("shot", None, "box", None),
            P("shot", "box", None),
            P("shot", None, None),
            P("shot", None),
            P("shot", "box"),
            P("shot", None, None, "box"),
            P("shot"),
            P(None, "box", None, None),
        ),
        out_specs=P(None, "box", None, None),
        check_vma=False,
    )
```

time: 125 us -> 38.5 us (0.31)
  starting transfers between devices: 61.5 us -> 8.8 us
  other arithmetic: 19.3 us -> 0 us
  waiting for transfers between devices: 12.9 us -> 5.56 us
  blocking collectives: 16.7 us -> 11 us
  local copies, waits for them, and re-layouts: 12.3 us -> 7.72 us
  Pallas kernels: 0 us -> 4.09 us
    ppermute x16 -> x2, starting transfers between devices: 44.2 us -> 1.11 us  [the longest x1 0.66 us: on_device(): got_b = lax.ppermute(send_b, 'box', swap_b)]
    psum x1 -> x0, blocking collectives: 16.7 us -> none  [on_device(): total_grad, total_illum = lax.psum((grad_rounds, illum_rounds), 'shot')]
    all_to_all x0 -> x1, blocking collectives: none -> 11 us  [on_device(): lax.all_to_all(out, ('shot', 'box'), split_axis=0, concat_axis=0, tiled=T...]
    all_to_all x3 -> x1, starting transfers between devices: 17.4 us -> 7.68 us  [on_device(): lax.all_to_all(image_out, 'box', split_axis=0, concat_axis=0, tiled=True)]
    scatter-add x8 -> x0, other arithmetic: 7.11 us -> none  [the longest x4 3.7 us: on_device(): next_u.at[shot_lane, column, source_depth]]
    unnamed x21 -> x41, local copies, waits for them, and re-layouts: 0.77 us -> 7.72 us
    all_to_all x3 -> x1, waiting for transfers between devices: 10.5 us -> 5.55 us  [on_device(): lax.all_to_all(image_out, 'box', split_axis=0, concat_axis=0, tiled=True)]
    add x10 -> x0, local copies, waits for them, and re-layouts: 4.95 us -> none  [the longest x4 2.46 us: on_device(): 2.0 * newer_b - older_b + speed_slab * lap_all[shot_count:]]
  transfers between devices with their start and end apart: 19 -> 3, of which waited for: 5 -> 1; matrix products, arithmetic and copies ran while one was open for 16% -> 0% of each run, Pallas kernels for 0% -> 0%
where the time goes in v1:
time: 38.5 us; the launch traced here: 38 us
  blocking collectives  11 us (29%)
  starting transfers between devices  8.8 us (23%)
  local copies, waits for them, and re-layouts  7.72 us (20%)
  waiting for transfers between devices  5.56 us (14%)
  Pallas kernels  4.09 us (11%)
  between operations  0.83 us (2%)
    all_to_all x1, blocking collectives, on_device(): lax.all_to_all(out, ('shot', 'box'), split_axis=0, concat_axis=0, tiled=T...  11 us
    unnamed x41, local copies, waits for them, and re-layouts  7.72 us
    all_to_all x1, starting transfers between devices, on_device(): lax.all_to_all(image_out, 'box', split_axis=0, concat_axis=0, tiled=True)  7.68 us
    all_to_all x1, waiting for transfers between devices, on_device(): lax.all_to_all(image_out, 'box', split_axis=0, concat_axis=0, tiled=True)  5.55 us
    pallas_call x1, Pallas kernels, on_device(): pl.pallas_call(functools.partial(wave_kernel, owners=owners, groups=group...  2.03 us
    pallas_call x1, Pallas kernels, on_device(): pl.pallas_call(functools.partial(pack_kernel, owners=owners), out_shape=(...  1.35 us
  transfers between devices with their start and end apart: 3, of which 1 were waited for; matrix products, arithmetic and copies ran while one was open for 0% of the time, Pallas kernels for 0%

profile of v1, /device:TPU:0, one launch (start us, length us, event | category | flops | bytes accessed | tf_op | source)
XLA Modules:
  0.0 38.0 jit_solution(2926659413028355495)
XLA Ops:
  0.0 0.0 copy-start.17
  0.7 0.0 copy-done.17
  0.7 0.0 copy-start
  0.7 0.9 %copy-done = f32[1,8,16,256]{3,2,1,0:T(8,128)S(1)} copy-done((f32[1,8,16,256]{3,2,1,0:T(8,128)S(1)}, f32[1,8,16,256]{3,2,1,0:T(8,128)}, u32[]{:S(2)}) %copy-start) | copy-done | bytes 131096
  1.6 0.0 copy-start.2
  1.6 0.9 %copy-done.2 = f32[1,8,16,256]{3,2,1,0:T(8,128)S(1)} copy-done((f32[1,8,16,256]{3,2,1,0:T(8,128)S(1)}, f32[1,8,16,256]{3,2,1,0:T(8,128)}, u32[]{:S(2)}) %copy-start.2) | copy-done | bytes 131096
  2.5 0.0 copy-start.4
  2.5 0.9 %copy-done.4 = f32[1,8,16,256]{3,2,1,0:T(8,128)S(1)} copy-done((f32[1,8,16,256]{3,2,1,0:T(8,128)S(1)}, f32[1,8,16,256]{3,2,1,0:T(8,128)}, u32[]{:S(2)}) %copy-start.4) | copy-done | bytes 131096
  3.4 0.0 copy-start.6
  3.4 0.9 %copy-done.6 = f32[1,8,16,256]{3,2,1,0:T(8,128)S(1)} copy-done((f32[1,8,16,256]{3,2,1,0:T(8,128)S(1)}, f32[1,8,16,256]{3,2,1,0:T(8,128)}, u32[]{:S(2)}) %copy-start.6) | copy-done | bytes 131096
  4.3 0.0 copy-start.8
  4.3 0.9 %copy-done.8 = f32[1,8,16,256]{3,2,1,0:T(8,128)S(1)} copy-done((f32[1,8,16,256]{3,2,1,0:T(8,128)S(1)}, f32[1,8,16,256]{3,2,1,0:T(8,128)}, u32[]{:S(2)}) %copy-start.8) | copy-done | bytes 131096
  5.2 0.0 copy-start.10
  5.2 0.9 %copy-done.10 = f32[1,8,16,256]{3,2,1,0:T(8,128)S(1)} copy-done((f32[1,8,16,256]{3,2,1,0:T(8,128)S(1)}, f32[1,8,16,256]{3,2,1,0:T(8,128)}, u32[]{:S(2)}) %copy-start.10) | copy-done | bytes 131096
  6.1 0.0 copy-start.12
  6.1 0.7 %copy-done.12 = f32[1,16,256]{2,1,0:T(8,128)S(1)} copy-done((f32[1,16,256]{2,1,0:T(8,128)S(1)}, f32[1,16,256]{2,1,0:T(8,128)}, u32[]{:S(2)}) %copy-start.12) | copy-done | bytes 16408
  6.8 0.0 copy-start.14
  6.8 0.7 %copy-done.14 = f32[1,8,4,8]{3,2,1,0:T(4,128)S(1)} copy-done((f32[1,8,4,8]{3,2,1,0:T(4,128)S(1)}, f32[1,8,4,8]{3,2,1,0:T(4,128)}, u32[]{:S(2)}) %copy-start.14) | copy-done | bytes 1048
  7.5 0.0 copy-start.16
  7.5 0.7 %copy-done.16 = f32[12,1,2,256]{3,2,1,0:T(2,128)S(1)} copy-done((f32[12,1,2,256]{3,2,1,0:T(2,128)S(1)}, f32[12,1,2,256]{3,2,1,0:T(2,128)}, u32[]{:S(2)}) %copy-start.16) | copy-done | bytes 24600
  8.3 0.0 copy-start.19
  8.3 0.0 copy-start.1
  8.3 0.0 copy-start.3
  8.3 0.0 copy-start.5
  8.3 0.0 copy-start.7
  8.3 0.0 copy-start.9
  8.3 0.0 copy-start.11
  8.3 1.4 %pack.1 = (f32[50,8,128]{2,1,0:T(8,128)S(1)}, f32[50,8,128]{2,1,0:T(8,128)S(1)}, f32[8,4,128]{2,1,0:T(4,128)}) custom-call(s32[1]{0:T(128)S(6)} %copy.15.first, s32[1,8]{1,0:T(1,128)S(1)} %copy-done.17, f32[1,8,16,256]{3,2,1,0:T(8,128)S(1)} %copy-done, f32[1,8,16,256]{3,2,1,0:T(8,128)S(1)} %copy-done.2, f32[1,8,16,256]{3,2,1,0:T(8,128)S(1)} %copy-done.4, ...), custom_call_target="tpu_custom_call" | custom-call | tf_op jit(solution)/shard_map/pack/pallas_call | solution.py:321
  9.7 0.5 %collective-permute-start = (f32[50,8,128]{2,1,0:T(8,128)S(1)}, f32[50,8,128]{2,1,0:T(8,128)S(1)}, u32[]{:S(2)}, u32[]{:S(2)}) collective-permute-start(f32[50,8,128]{2,1,0:T(8,128)S(1)} %get-tuple-element.8), channel_id=1, source_target_pairs={{0,1},{1,0},{2,3},{3,2},{4,5},{5,4},{6,7},{7,6},{8,9},{9,8},{10,11... | collective-permute-start | bytes 614408 | tf_op jit(solution)/shard_map/ppermute | solution.py:333
  10.1 0.7 %collective-permute-start.1 = (f32[50,8,128]{2,1,0:T(8,128)S(1)}, f32[50,8,128]{2,1,0:T(8,128)S(1)}, u32[]{:S(2)}, u32[]{:S(2)}) collective-permute-start(f32[50,8,128]{2,1,0:T(8,128)S(1)} %get-tuple-element.9), channel_id=1, source_target_pairs={{1,2},{2,1},{3,4},{4,3},{5,6},{6,5},{9,10},{10,9},{11,12},{12,11},... | collective-permute-start | bytes 614408 | tf_op jit(solution)/shard_map/ppermute | solution.py:334
  10.8 0.0 copy-start.13
  10.8 0.0 copy-start.15
  10.8 7.7 %all-to-all-start = ((f32[8,4,128]{2,1,0:T(4,128)}), f32[8,4,128]{2,1,0:T(4,128)S(1)}, u32[]{:S(2)}, u32[]{:S(2)}) async-start(f32[8,4,128]{2,1,0:T(4,128)} %get-tuple-element.10), calls=%async_computation | async-start | bytes 32768 | tf_op jit(solution)/shard_map/all_to_all | solution.py:330
  18.5 0.0 copy-done.19
  18.5 0.0 copy-start.18
  18.5 0.1 copy.14.wavelet
  18.6 5.6 %all-to-all-done.image_in = f32[8,4,128]{2,1,0:T(4,128)S(1)} async-done(((f32[8,4,128]{2,1,0:T(4,128)}), f32[8,4,128]{2,1,0:T(4,128)S(1)}, u32[]{:S(2)}, u32[]{:S(2)}) %all-to-all-start) | async-done | bytes 16416 | tf_op jit(solution)/shard_map/all_to_all | solution.py:330
  24.2 0.0 collective-permute-done.pack_a
  24.2 0.0 collective-permute-done.1.pack_b
  24.2 0.0 copy-done.1
  24.2 0.0 copy-done.3
  24.2 0.0 copy-done.5
  24.2 0.0 copy-done.7
  24.2 0.0 copy-done.9
  24.2 0.0 copy-done.11
  24.2 0.0 copy-done.13
  24.2 0.0 copy-done.15
  24.2 0.0 copy-done.18
  24.3 2.0 %waves.1 = f32[32,1,1152]{2,1,0:T(1,128)S(1)} custom-call(s32[1]{0:T(128)S(6)} %copy.15.first, s32[1,8]{1,0:T(1,128)S(1)} %copy-done.18, s32[1,8]{1,0:T(1,128)S(1)} %copy-done.17, f32[1,8,16,256]{3,2,1,0:T(8,128)S(1)} %copy-done.1, f32[1,8,16,256]{3,2,1,0:T(8,128)S(1)} %copy-done.3, f32[1,8,16,256]{3,2,1,0:T(8,128)S(1)} %copy-done.5, ...), custom_call_target="tpu_custom_call" | custom-call | tf_op jit(solution)/shard_map/waves/pallas_call | solution.py:337
  26.3 11.0 %all_to_all.10.received = f32[32,1,1152]{2,1,0:T(1,128)S(1)} all-to-all(f32[32,1,1152]{2,1,0:T(1,128)S(1)} %waves.1), channel_id=1, replica_groups=mesh['shot'=4,'box'=8] {'shot','box'}, dimensions={0} | all-to-all | bytes 294912 | tf_op jit(solution)/shard_map/all_to_all | solution.py:368
  37.3 0.7 %join.1 = f32[12,1,2,256]{3,2,1,0:T(2,128)} custom-call(f32[32,1,1152]{2,1,0:T(1,128)S(1)} %all_to_all.10.received), custom_call_target="tpu_custom_call" | custom-call | tf_op jit(solution)/shard_map/join/pallas_call | solution.py:369
Async XLA Ops:
  0.0 0.7 %copy-start.17 = (s32[1,8]{1,0:T(1,128)S(1)}, s32[1,8]{1,0:T(1,128)}, u32[]{:S(2)}) copy-start(s32[1,8]{1,0:T(1,128)} %rec.3) | copy-start | bytes 100
  0.7 0.9 %copy-start = (f32[1,8,16,256]{3,2,1,0:T(8,128)S(1)}, f32[1,8,16,256]{3,2,1,0:T(8,128)}, u32[]{:S(2)}) copy-start(f32[1,8,16,256]{3,2,1,0:T(8,128)} %un.3) | copy-start | bytes 393220
  1.6 0.9 %copy-start.2 = (f32[1,8,16,256]{3,2,1,0:T(8,128)S(1)}, f32[1,8,16,256]{3,2,1,0:T(8,128)}, u32[]{:S(2)}) copy-start(f32[1,8,16,256]{3,2,1,0:T(8,128)} %up.3) | copy-start | bytes 393220
  2.5 0.9 %copy-start.4 = (f32[1,8,16,256]{3,2,1,0:T(8,128)S(1)}, f32[1,8,16,256]{3,2,1,0:T(8,128)}, u32[]{:S(2)}) copy-start(f32[1,8,16,256]{3,2,1,0:T(8,128)} %bn.3) | copy-start | bytes 393220
  3.4 0.9 %copy-start.6 = (f32[1,8,16,256]{3,2,1,0:T(8,128)S(1)}, f32[1,8,16,256]{3,2,1,0:T(8,128)}, u32[]{:S(2)}) copy-start(f32[1,8,16,256]{3,2,1,0:T(8,128)} %bp.3) | copy-start | bytes 393220
  4.3 0.9 %copy-start.8 = (f32[1,8,16,256]{3,2,1,0:T(8,128)S(1)}, f32[1,8,16,256]{3,2,1,0:T(8,128)}, u32[]{:S(2)}) copy-start(f32[1,8,16,256]{3,2,1,0:T(8,128)} %qn.3) | copy-start | bytes 393220
  5.2 0.9 %copy-start.10 = (f32[1,8,16,256]{3,2,1,0:T(8,128)S(1)}, f32[1,8,16,256]{3,2,1,0:T(8,128)}, u32[]{:S(2)}) copy-start(f32[1,8,16,256]{3,2,1,0:T(8,128)} %qp.3) | copy-start | bytes 393220
  6.1 0.7 %copy-start.12 = (f32[1,16,256]{2,1,0:T(8,128)S(1)}, f32[1,16,256]{2,1,0:T(8,128)}, u32[]{:S(2)}) copy-start(f32[1,16,256]{2,1,0:T(8,128)} %speed.3) | copy-start | bytes 49156
  6.8 0.7 %copy-start.14 = (f32[1,8,4,8]{3,2,1,0:T(4,128)S(1)}, f32[1,8,4,8]{3,2,1,0:T(4,128)}, u32[]{:S(2)}) copy-start(f32[1,8,4,8]{3,2,1,0:T(4,128)} %obs.3) | copy-start | bytes 3076
  7.5 0.7 %copy-start.16 = (f32[12,1,2,256]{3,2,1,0:T(2,128)S(1)}, f32[12,1,2,256]{3,2,1,0:T(2,128)}, u32[]{:S(2)}) copy-start(f32[12,1,2,256]{3,2,1,0:T(2,128)} %refl.1) | copy-start | bytes 73732
  8.3 10.2 %copy-start.19 = (f32[1,8,4]{1,2,0:T(4,128)S(1)}, f32[1,8,4]{1,2,0:T(4,128)}, u32[]{:S(2)}) copy-start(f32[1,8,4]{1,2,0:T(4,128)} %param.20) | copy-start | bytes 388
  8.3 15.9 %copy-start.1 = (f32[1,8,16,256]{3,2,1,0:T(8,128)S(1)}, f32[1,8,16,256]{3,2,1,0:T(8,128)}, u32[]{:S(2)}) copy-start(f32[1,8,16,256]{3,2,1,0:T(8,128)} %un.3) | copy-start | bytes 393220
  8.3 15.9 %copy-start.3 = (f32[1,8,16,256]{3,2,1,0:T(8,128)S(1)}, f32[1,8,16,256]{3,2,1,0:T(8,128)}, u32[]{:S(2)}) copy-start(f32[1,8,16,256]{3,2,1,0:T(8,128)} %up.3) | copy-start | bytes 393220
  8.3 15.9 %copy-start.5 = (f32[1,8,16,256]{3,2,1,0:T(8,128)S(1)}, f32[1,8,16,256]{3,2,1,0:T(8,128)}, u32[]{:S(2)}) copy-start(f32[1,8,16,256]{3,2,1,0:T(8,128)} %bn.3) | copy-start | bytes 393220
  8.3 15.9 %copy-start.7 = (f32[1,8,16,256]{3,2,1,0:T(8,128)S(1)}, f32[1,8,16,256]{3,2,1,0:T(8,128)}, u32[]{:S(2)}) copy-start(f32[1,8,16,256]{3,2,1,0:T(8,128)} %bp.3) | copy-start | bytes 393220
  8.3 15.9 %copy-start.9 = (f32[1,8,16,256]{3,2,1,0:T(8,128)S(1)}, f32[1,8,16,256]{3,2,1,0:T(8,128)}, u32[]{:S(2)}) copy-start(f32[1,8,16,256]{3,2,1,0:T(8,128)} %qn.3) | copy-start | bytes 393220
  8.3 15.9 %copy-start.11 = (f32[1,8,16,256]{3,2,1,0:T(8,128)S(1)}, f32[1,8,16,256]{3,2,1,0:T(8,128)}, u32[]{:S(2)}) copy-start(f32[1,8,16,256]{3,2,1,0:T(8,128)} %qp.3) | copy-start | bytes 393220
  9.7 14.5 %collective-permute-start = (f32[50,8,128]{2,1,0:T(8,128)S(1)}, f32[50,8,128]{2,1,0:T(8,128)S(1)}, u32[]{:S(2)}, u32[]{:S(2)}) collective-permute-start(f32[50,8,128]{2,1,0:T(8,128)S(1)} %get-tuple-element.8), channel_id=1, source_target_pairs={{0,1},{1,0},{2,3},{3,2},{4,5},{5,4},{6,7},{7,6},{8,9},{9,8},{10,11... | collective-permute-start | bytes 614408 | tf_op jit(solution)/shard_map/ppermute | solution.py:333
  10.1 14.0 %collective-permute-start.1 = (f32[50,8,128]{2,1,0:T(8,128)S(1)}, f32[50,8,128]{2,1,0:T(8,128)S(1)}, u32[]{:S(2)}, u32[]{:S(2)}) collective-permute-start(f32[50,8,128]{2,1,0:T(8,128)S(1)} %get-tuple-element.9), channel_id=1, source_target_pairs={{1,2},{2,1},{3,4},{4,3},{5,6},{6,5},{9,10},{10,9},{11,12},{12,11},... | collective-permute-start | bytes 614408 | tf_op jit(solution)/shard_map/ppermute | solution.py:334
  10.8 13.4 %copy-start.13 = (f32[1,16,256]{2,1,0:T(8,128)S(1)}, f32[1,16,256]{2,1,0:T(8,128)}, u32[]{:S(2)}) copy-start(f32[1,16,256]{2,1,0:T(8,128)} %speed.3) | copy-start | bytes 49156
  10.8 13.4 %copy-start.15 = (f32[1,8,4,8]{3,2,1,0:T(4,128)S(1)}, f32[1,8,4,8]{3,2,1,0:T(4,128)}, u32[]{:S(2)}) copy-start(f32[1,8,4,8]{3,2,1,0:T(4,128)} %obs.3) | copy-start | bytes 3076
  10.8 13.3 %all-to-all-start = ((f32[8,4,128]{2,1,0:T(4,128)}), f32[8,4,128]{2,1,0:T(4,128)S(1)}, u32[]{:S(2)}, u32[]{:S(2)}) async-start(f32[8,4,128]{2,1,0:T(4,128)} %get-tuple-element.10), calls=%async_computation | async-start | bytes 32768 | tf_op jit(solution)/shard_map/all_to_all | solution.py:330
  18.5 5.7 %copy-start.18 = (s32[1,8]{1,0:T(1,128)S(1)}, s32[1,8]{1,0:T(1,128)}, u32[]{:S(2)}) copy-start(s32[1,8]{1,0:T(1,128)} %sources.1) | copy-start | bytes 100

commit v2 on v1

v2 whole, which is shorter than its diff:
```python
import functools

import jax
import jax.numpy as jnp
from jax import lax
from jax.experimental import pallas as pl
from jax.experimental.pallas import tpu as pltpu
from jax.sharding import PartitionSpec as P

damping = 1.0
LANES = 128
MARGIN = 8
STEPS = 4
HALO = (
    ("un", 0, 7),
    ("up", 0, 6),
    ("bn", 0, 7),
    ("bp", 0, 6),
    ("un", 1, 4),
    ("up", 1, 3),
    ("qn", 0, 4),
    ("qn", 1, 4),
    ("qp", 0, 3),
    ("qp", 1, 3),
)
HALO_TILES = sum(count for _, _, count in HALO)
SPEED_TILE = HALO_TILES
META_TILE = HALO_TILES + 2
PACK_TILES = HALO_TILES + 3
VMEM = pltpu.VMEM
SMEM = pltpu.SMEM


def lane_iota():
    return lax.broadcasted_iota(jnp.int32, (8, LANES), 1)


def pack_kernel(
    first_any,
    rec_any,
    un,
    up,
    bn,
    bp,
    qn,
    qp,
    speed_any,
    obs_any,
    refl_any,
    pack_a,
    pack_b,
    image_out,
    first,
    rec,
    refl,
    wide,
    near,
    speed,
    obs,
    sems,
):
    columns, depth = un.shape[2], un.shape[3]
    position = lax.axis_index("box")
    even = lax.rem(position, 2) == 0
    edges = (pl.ds(0, 8), pl.ds(columns - 8, 8))
    wides = {"un": 0, "up": 1, "qn": 2, "qp": 3}
    nears = {"bn": 0, "bp": 1}
    moves = [(first_any, first), (rec_any, rec), (obs_any, obs), (refl_any, refl)]
    for side in range(2):
        for name, ref in (("un", un), ("up", up), ("qn", qn), ("qp", qp)):
            moves.append((ref.at[0, :, edges[side], :], wide.at[side, wides[name]]))
        for name, ref in (("bn", bn), ("bp", bp)):
            moves.append((ref.at[0, :, edges[side], pl.ds(0, LANES)], near.at[side, nears[name]]))
        moves.append((speed_any.at[0, edges[side], :], speed.at[side]))
    copies = [pltpu.make_async_copy(*move, sems.at[i]) for i, move in enumerate(moves)]
    for copy in copies:
        copy.start()
    for copy in copies:
        copy.wait()

    owners = image_out.shape[0]
    for target in range(owners):
        low_tile = first[0] + (columns // 2) * target - 3
        r0 = lax.div(low_tile - position + 2 * owners - 1, owners) - 1
        for slot in range(2):
            r = jnp.clip(r0 + slot, 0, refl.shape[0] - 1)
            image_out[target, 2 * slot : 2 * slot + 2, :] = refl[r, 0, :, 0:LANES]

    def put(tile, left, right):
        pack_a[tile] = jnp.where(even, right, left)
        pack_b[tile] = jnp.where(even, left, right)

    tile = 0
    for name, half, count in HALO:
        part = slice(half * LANES, (half + 1) * LANES)
        if name in nears:
            low, high = (near[side, nears[name]] for side in range(2))
        else:
            low, high = (wide[side, wides[name], :, :, part] for side in range(2))
        low, high = jnp.swapaxes(low, 0, 1), jnp.swapaxes(high, 0, 1)
        for j in range(1, count + 1):
            put(tile, low[j - 1], high[8 - j])
            tile += 1
    for half in range(2):
        part = slice(half * LANES, (half + 1) * LANES)
        put(SPEED_TILE + half, speed[0, :, part], speed[1, :, part])

    lane = lane_iota()
    count = rec.shape[1]

    def meta(right):
        out = jnp.zeros((8, LANES), jnp.float32)
        for k in range(2):
            r = count - 1 - k if right else k
            for t in range(STEPS):
                value = jnp.broadcast_to(obs[0, :, t, r : r + 1], (8, LANES))
                out = jnp.where(lane == 2 * t + k, value, out)
            column = lax.div(rec[0, r], depth) - position * columns
            distance = columns - column if right else column + 1
            code = distance * depth + lax.rem(rec[0, r], depth)
            out = jnp.where(lane == 2 * STEPS + k, code.astype(jnp.float32), out)
        return out

    put(META_TILE, meta(False), meta(True))


def depthwise(xs, first_lane, last_lane):
    rolled_up = [pltpu.roll(x, 1, 1) for x in xs]
    rolled_down = [pltpu.roll(x, LANES - 1, 1) for x in xs]
    if len(xs) == 1:
        return [
            jnp.where(first_lane, 0.0, rolled_up[0]) + jnp.where(last_lane, 0.0, rolled_down[0])
        ]
    return [
        jnp.where(first_lane, 0.0, rolled_up[0])
        + jnp.where(last_lane, rolled_down[1], rolled_down[0]),
        jnp.where(first_lane, rolled_up[0], rolled_up[1])
        + jnp.where(last_lane, 0.0, rolled_down[1]),
    ]


def lap(ref, e, count, edges):
    parts = [slice(h * LANES, (h + 1) * LANES) for h in range(count)]
    mid = [ref[e, :, part] for part in parts]
    along = depthwise(mid, *edges)
    return mid, [
        ref[e - 1, :, parts[h]] + ref[e + 1, :, parts[h]] + along[h] - 4.0 * mid[h]
        for h in range(count)
    ]


def homogeneous_kernel(
    sources,
    un,
    up,
    bn,
    bp,
    qn,
    qp,
    speed,
    wavelet,
    pack_a,
    pack_b,
    acc,
    b0,
    b1,
    near_speed,
    meta,
    rows_out,
    u0,
    u1,
    q0,
    q1,
    vel,
    late,
):
    columns, depth = speed.shape[1], speed.shape[2]
    position = lax.axis_index("box")
    even = lax.rem(position, 2) == 0
    has_left = position > 0
    has_right = position < lax.axis_size("box") - 1
    lane = lane_iota()
    edges = lane == 0, lane == LANES - 1
    zero = jnp.zeros((8, LANES), jnp.float32)
    halves = (slice(0, LANES), slice(LANES, 2 * LANES))
    scratch = {"un": u0, "up": u1, "bn": b0, "bp": b1, "qn": q0, "qp": q1}

    for name, ref in (("un", un), ("up", up), ("qn", qn), ("qp", qp)):
        for c in range(0, columns, 8):
            scratch[name][MARGIN + c : MARGIN + c + 8] = jnp.swapaxes(ref[0, :, c : c + 8, :], 0, 1)
    for name, ref in (("bn", bn), ("bp", bp)):
        for c in range(0, columns, 8):
            scratch[name][MARGIN + c : MARGIN + c + 8] = jnp.swapaxes(
                ref[0, :, c : c + 8, 0:LANES], 0, 1
            )
    for c in range(columns):
        vel[MARGIN + c] = jnp.broadcast_to(speed[0, c : c + 1, :], (8, depth))

    def got(tile):
        a, b = pack_a[tile], pack_b[tile]
        left, right = jnp.where(even, b, a), jnp.where(even, a, b)
        return jnp.where(has_left, left, 0.0), jnp.where(has_right, right, 0.0)

    tile = 0
    for name, half, count in HALO:
        for j in range(1, count + 1):
            left, right = got(tile)
            scratch[name][MARGIN - j, :, halves[half]] = left
            scratch[name][MARGIN + columns - 1 + j, :, halves[half]] = right
            tile += 1
    for half, count in ((0, 6), (1, 3)):
        left, right = got(SPEED_TILE + half)
        for j in range(1, count + 1):
            vel[MARGIN - j, :, halves[half]] = jnp.broadcast_to(left[8 - j : 9 - j], (8, LANES))
            vel[MARGIN + columns - 1 + j, :, halves[half]] = jnp.broadcast_to(
                right[j - 1 : j], (8, LANES)
            )
    meta_left, meta_right = got(META_TILE)
    meta[0] = meta_left
    meta[1] = meta_right
    for c in range(-6, columns + 6):
        near_speed[MARGIN + c] = vel[MARGIN + c, :, halves[0]]

    shot = lax.broadcasted_iota(jnp.int32, (8, LANES), 0)
    cell = jnp.zeros((8, LANES), jnp.int32)
    for s in range(8):
        cell = jnp.where(shot == s, sources[0, s] - position * columns * depth, cell)
    cell = cell - lane
    pulses = [jnp.broadcast_to(wavelet[0, :, t : t + 1], (8, LANES)) for t in range(STEPS)]

    new_u, old_u = u0, u1
    illum = [[zero, zero] for _ in range(columns)]
    for t in range(STEPS):
        wide, narrow = 6 - t, 3 - t
        for c in range(-wide, columns + wide):
            e = MARGIN + c
            count = 2 if -narrow <= c < columns + narrow else 1
            mid, laps = lap(new_u, e, count, edges)
            for h in range(count):
                hit = cell == c * depth + h * LANES
                a = vel[e, :, halves[h]] * laps[h] + jnp.where(hit, pulses[t], 0.0)
                if h == 0:
                    acc[t, e] = a
                elif 0 <= c < columns:
                    late[t, c] = a
                old_u[e, :, halves[h]] = 2.0 * mid[h] - old_u[e, :, halves[h]] + a
                if 0 <= c < columns:
                    illum[c][h] = illum[c][h] + a * a
        new_u, old_u = old_u, new_u

    grad = [[zero, zero] for _ in range(columns)]
    new_q, old_q = q0, q1
    for t in reversed(range(STEPS)):
        for c in range(-t, columns + t):
            e = MARGIN + c
            mid, laps = lap(new_q, e, 2, edges)
            for h in range(2):
                q = 2.0 * mid[h] - old_q[e, :, halves[h]] + vel[e, :, halves[h]] * laps[h]
                old_q[e, :, halves[h]] = q
                if 0 <= c < columns:
                    a = late[t, c] if h else acc[t, e]
                    grad[c][h] = grad[c][h] + q * a
        new_q, old_q = old_q, new_q

    for k in range(columns // 2):
        i = 0
        for sums in (grad, illum):
            for h in range(2):
                for w in range(2):
                    rows_out[k, :, i * LANES : (i + 1) * LANES] = jnp.sum(
                        sums[2 * k + w][h], axis=0, keepdims=True
                    )
                    i += 1


def scattered_kernel(
    first,
    rec,
    acc,
    b0_in,
    b1_in,
    speed,
    meta,
    rows_in,
    obs,
    image_in,
    out,
    b0,
    b1,
    q0,
    q1,
    img,
    *,
    owners,
    groups,
    depth,
):
    columns = 2 * rows_in.shape[0]
    tiles = columns // 2
    position = lax.axis_index("box")
    lane = lane_iota()
    edges = lane == 0, lane == LANES - 1
    zero = jnp.zeros((8, LANES), jnp.float32)

    low_tile = first[0] + tiles * position - 3 + owners
    for m in range(tiles + 6):
        owner = lax.rem(low_tile + m, owners)
        slot = 2 * (m // owners)
        pair = image_in[owner, slot : slot + 2, :]
        for w in range(2):
            img[MARGIN - 6 + 2 * m + w] = jnp.broadcast_to(pair[w : w + 1], (8, LANES))

    def receiver(c):
        if c < 0 or c >= columns:
            j = -c if c < 0 else c - columns + 1
            side = meta[0] if c < 0 else meta[1]
            k = (j - 1) // 2
            lane_of = 2 * STEPS + k
            code = jnp.broadcast_to(side[:, lane_of : lane_of + 1], (8, LANES))
            mask = code == (lane + j * depth).astype(jnp.float32)
            return mask, lambda t: jnp.broadcast_to(
                side[:, 2 * t + k : 2 * t + k + 1], (8, LANES)
            )
        r = c // 2
        here = rec[0, r] - (position * columns + c) * depth
        return lane == here, lambda t: jnp.broadcast_to(obs[0, :, t, r : r + 1], (8, LANES))

    misfits = []
    new_b, old_b, spare = b0_in, b1_in, [b0, b1]
    for t in range(STEPS):
        next_b = spare[t % 2]
        for c in range(t - 6, columns + 6 - t):
            e = MARGIN + c
            (mid,), (laps,) = lap(new_b, e, 1, edges)
            next_b[e] = 2.0 * mid - old_b[e] + speed[e] * laps + img[e] * acc[t, e]
        old_b, new_b = new_b, next_b
        part = {}
        for c in range(-t, columns + t):
            mask, recorded = receiver(c)
            part[c] = jnp.where(mask, new_b[MARGIN + c] - recorded(t), 0.0)
        misfits.append(part)

    grad = [zero] * columns
    new_q, old_q = q0, q1
    for t in reversed(range(STEPS)):
        for c in range(-t, columns + t):
            e = MARGIN + c
            q = misfits[t][c]
            if t < STEPS - 1:
                (mid,), (laps,) = lap(new_q, e, 1, edges)
                q = q + 2.0 * mid + speed[e] * laps
            if t < STEPS - 2:
                q = q - old_q[e]
            old_q[e] = q
            if 0 <= c < columns:
                grad[c] = grad[c] + q * acc[t, e]
        new_q, old_q = old_q, new_q

    start = jnp.full((1, LANES), first[0].astype(jnp.float32))
    for k in range(tiles):
        owner = lax.rem(first[0] + tiles * position + k, owners)
        rows = rows_in[k]
        near = [jnp.sum(grad[2 * k + w], axis=0, keepdims=True) for w in range(2)]
        for group in range(groups):
            to = group * owners + owner
            out[to, :, 2 * LANES : 8 * LANES] = rows[:, 2 * LANES :]
            for w in range(2):
                part = slice(w * LANES, (w + 1) * LANES)
                out[to, :, part] = rows[:, part] + near[w]
            out[to, :, 8 * LANES : 9 * LANES] = start


def join_kernel(received, migrated, total, *, owners, groups):
    position = lax.axis_index("box")
    total[...] = jnp.zeros_like(total)
    for group in range(groups):
        start = received[group * owners, 0, 8 * LANES].astype(jnp.int32)
        base = lax.div(start - position + owners - 1, owners)
        for p in range(owners):
            total[base + p] = total[base + p] + received[group * owners + p, :, 0 : 8 * LANES]
    for r in range(migrated.shape[0]):
        grad = total[r, :, 0 : 4 * LANES]
        illum = total[r, :, 4 * LANES : 8 * LANES]
        image = grad / jnp.sqrt(illum + damping)
        for h in range(2):
            for w in range(2):
                i = 2 * h + w
                migrated[r, 0, w : w + 1, h * LANES : (h + 1) * LANES] = image[
                    :, i * LANES : (i + 1) * LANES
                ]


def on_device(
    u_prev,
    u_now,
    born_prev,
    born_now,
    adj_after,
    adj_last,
    velocity,
    wavelet,
    sources,
    receivers,
    observed,
    first_tile,
    reflectivity,
):
    owners = lax.axis_size("box")
    groups = lax.axis_size("shot")
    columns, depth = velocity.shape[1], velocity.shape[2]
    rounds = reflectivity.shape[0]
    smem, vmem = pl.BlockSpec(memory_space=SMEM), pl.BlockSpec(memory_space=VMEM)
    anywhere = pl.BlockSpec(memory_space=pl.ANY)
    f32 = jnp.float32
    params = pltpu.CompilerParams(vmem_limit_bytes=32 * 1024 * 1024)
    params_hbm = pltpu.CompilerParams(vmem_limit_bytes=60 * 1024 * 1024)
    fields = (u_now, u_prev, born_now, born_prev, adj_last, adj_after)

    pack = jax.ShapeDtypeStruct((PACK_TILES, 8, LANES), f32)
    send_a, send_b, image_out = pl.pallas_call(
        pack_kernel,
        out_shape=(pack, pack, jax.ShapeDtypeStruct((owners, 4, LANES), f32)),
        in_specs=[anywhere] * 11,
        out_specs=(vmem,) * 3,
        scratch_shapes=[
            SMEM(first_tile.shape, jnp.int32),
            SMEM(receivers.shape, jnp.int32),
            VMEM(reflectivity.shape, f32),
            VMEM((2, 4, 8, 8, depth), f32),
            VMEM((2, 2, 8, 8, LANES), f32),
            VMEM((2, 8, depth), f32),
            VMEM(observed.shape, f32),
            pltpu.SemaphoreType.DMA((18,)),
        ],
        compiler_params=params_hbm,
        name="pack",
    )(first_tile, receivers, *fields, velocity, observed, reflectivity)

    ends = (0, owners - 1)
    swap_a = [(i, i ^ 1) for i in range(owners)]
    swap_b = [
        (g * owners + i, (g ^ 1) * owners + i if i in ends else g * owners + (i + 1 if i % 2 else i - 1))
        for g in range(groups)
        for i in range(owners)
    ]
    got_a = lax.ppermute(send_a, "box", swap_a)
    got_b = lax.ppermute(send_b, ("shot", "box"), swap_b)
    image_in = lax.all_to_all(image_out, "box", split_axis=0, concat_axis=0, tiled=True)

    ext = columns + 2 * MARGIN
    shape = jax.ShapeDtypeStruct
    acc, b0, b1, near_speed, meta, rows = pl.pallas_call(
        homogeneous_kernel,
        out_shape=(
            shape((STEPS, ext, 8, LANES), f32),
            shape((ext, 8, LANES), f32),
            shape((ext, 8, LANES), f32),
            shape((ext, 8, LANES), f32),
            shape((2, 8, LANES), f32),
            shape((columns // 2, 1, 8 * LANES), f32),
        ),
        in_specs=[smem] + [vmem] * 10,
        out_specs=(vmem,) * 6,
        scratch_shapes=[VMEM((ext, 8, depth), f32)] * 5 + [VMEM((STEPS, columns, 8, LANES), f32)],
        compiler_params=params,
        name="homogeneous",
    )(sources, *fields, velocity, wavelet, got_a, got_b)
    out = pl.pallas_call(
        functools.partial(scattered_kernel, owners=owners, groups=groups, depth=depth),
        out_shape=shape((groups * owners, 1, 9 * LANES), f32),
        in_specs=[smem] * 2 + [vmem] * 8,
        out_specs=vmem,
        scratch_shapes=[VMEM((ext, 8, LANES), f32)] * 5,
        compiler_params=params,
        name="scattered",
    )(
        first_tile,
        receivers,
        acc,
        b0,
        b1,
        near_speed,
        meta,
        rows,
        observed,
        image_in,
    )

    received = lax.all_to_all(out, ("shot", "box"), split_axis=0, concat_axis=0, tiled=True)
    return pl.pallas_call(
        functools.partial(join_kernel, owners=owners, groups=groups),
        out_shape=jax.ShapeDtypeStruct(reflectivity.shape, f32),
        in_specs=[vmem],
        out_specs=vmem,
        scratch_shapes=[VMEM((rounds, 1, 8 * LANES), f32)],
        compiler_params=params,
        name="join",
    )(received)


def solution(mesh):
    return jax.shard_map(
        on_device,
        mesh=mesh,
        in_specs=(
            P("shot", None, "box", None),
            P("shot", None, "box", None),
            P("shot", None, "box", None),
            P("shot", None, "box", None),
            P("shot", None, "box", None),
            P("shot", None, "box", None),
            P("shot", "box", None),
            P("shot", None, None),
            P("shot", None),
            P("shot", "box"),
            P("shot", None, None, "box"),
            P("shot"),
            P(None, "box", None, None),
        ),
        out_specs=P(None, "box", None, None),
        check_vma=False,
    )
```

time: 38.5 us -> 30 us (0.78)
  local copies, waits for them, and re-layouts: 7.72 us -> 1.27 us
  waiting for transfers between devices: 5.56 us -> 3.53 us
  Pallas kernels: 4.09 us -> 6.06 us
  starting transfers between devices: 8.8 us -> 7.85 us
  blocking collectives: 11 us -> 10.2 us
    unnamed x41 -> x23, local copies, waits for them, and re-layouts: 7.72 us -> 1.27 us
    all_to_all x1, starting transfers between devices: 7.68 us -> 4.77 us  [on_device(): lax.all_to_all(image_out, 'box', split_axis=0, concat_axis=0, tiled=True)]
    all_to_all x1, waiting for transfers between devices: 5.55 us -> 3.53 us  [on_device(): lax.all_to_all(image_out, 'box', split_axis=0, concat_axis=0, tiled=True)]
    pallas_call x2 -> x3, Pallas kernels: 3.38 us -> 5.35 us  [the longest x1 2.38 us: on_device(): pl.pallas_call(pack_kernel, out_shape=(pack, pack, jax.ShapeDtypeStruct((...]
    ppermute x1, starting transfers between devices: 0.66 us -> 2.56 us  [on_device(): got_b = lax.ppermute(send_b, ('shot', 'box'), swap_b)]
    all_to_all x1, blocking collectives: 11 us -> 10.2 us  [on_device(): lax.all_to_all(out, ('shot', 'box'), split_axis=0, concat_axis=0, tiled=T...]
  transfers between devices with their start and end apart: 3 -> 3, of which waited for: 1 -> 1; matrix products, arithmetic and copies ran while one was open for 0% -> 0% of each run, Pallas kernels for 0% -> 5%
where the time goes in v2:
time: 30 us; the launch traced here: 29.7 us
  blocking collectives  10.2 us (34%)
  starting transfers between devices  7.85 us (26%)
  Pallas kernels  6.06 us (20%)
  waiting for transfers between devices  3.53 us (12%)
  local copies, waits for them, and re-layouts  1.27 us (4%)
  between operations  0.79 us (3%)
    all_to_all x1, blocking collectives, on_device(): lax.all_to_all(out, ('shot', 'box'), split_axis=0, concat_axis=0, tiled=T...  10.2 us
    all_to_all x1, starting transfers between devices, on_device(): lax.all_to_all(image_out, 'box', split_axis=0, concat_axis=0, tiled=True)  4.77 us
    all_to_all x1, waiting for transfers between devices, on_device(): lax.all_to_all(image_out, 'box', split_axis=0, concat_axis=0, tiled=True)  3.53 us
    ppermute x1, starting transfers between devices, on_device(): got_b = lax.ppermute(send_b, ('shot', 'box'), swap_b)  2.56 us
    pallas_call x1, Pallas kernels, on_device(): pl.pallas_call(pack_kernel, out_shape=(pack, pack, jax.ShapeDtypeStruct((...  2.38 us
    pallas_call x1, Pallas kernels, on_device(): pl.pallas_call(functools.partial(scattered_kernel, owners=owners, groups=...  1.52 us
    pallas_call x1, Pallas kernels, on_device(): pl.pallas_call(homogeneous_kernel, out_shape=(shape((STEPS, ext, 8, LANES...  1.45 us
    unnamed x23, local copies, waits for them, and re-layouts  1.27 us
  transfers between devices with their start and end apart: 3, of which 1 were waited for; matrix products, arithmetic and copies ran while one was open for 0% of the time, Pallas kernels for 5%

profile of v2, /device:TPU:0, one launch (start us, length us, event | category | flops | bytes accessed | tf_op | source)
XLA Modules:
  0.0 29.7 jit_solution(1405339950975485907)
XLA Ops:
  0.7 0.0 copy-start
  0.7 0.0 copy-start.1
  0.7 0.0 copy-start.2
  0.7 0.0 copy-start.3
  0.7 0.0 copy-start.4
  0.7 0.0 copy-start.5
  0.7 2.4 %pack.1 = (f32[50,8,128]{2,1,0:T(8,128)}, f32[50,8,128]{2,1,0:T(8,128)}, f32[8,4,128]{2,1,0:T(4,128)}) custom-call(s32[1]{0:T(128)S(6)} %copy.15.first_any.first, s32[1,8]{1,0:T(1,128)} %rec.1, f32[1,8,16,256]{3,2,1,0:T(8,128)} %un.3, f32[1,8,16,256]{3,2,1,0:T(8,128)} %up.3, f32[1,8,16,256]{3,2,1,0:T(8,128)} %bn.3, f32[1,8,16,256]{3,2,1,0:T(8,128)} %bp.3, ...), custom_call_target="tpu_custom_call" | custom-call | tf_op jit(solution)/shard_map/pack/pallas_call | solution.py:420
  3.1 0.5 %collective-permute-start = (f32[50,8,128]{2,1,0:T(8,128)}, f32[50,8,128]{2,1,0:T(8,128)S(1)}, u32[]{:S(2)}, u32[]{:S(2)}) collective-permute-start(f32[50,8,128]{2,1,0:T(8,128)} %get-tuple-element.14), channel_id=1, source_target_pairs={{0,1},{1,0},{2,3},{3,2},{4,5},{5,4},{6,7},{7,6},{8,9},{9,8},{10,11... | collective-permute-start | bytes 614408 | tf_op jit(solution)/shard_map/ppermute | solution.py:446
  3.6 2.6 %collective-permute-start.1 = (f32[50,8,128]{2,1,0:T(8,128)}, f32[50,8,128]{2,1,0:T(8,128)S(1)}, u32[]{:S(2)}, u32[]{:S(2)}) collective-permute-start(f32[50,8,128]{2,1,0:T(8,128)} %get-tuple-element.15), channel_id=1, source_target_pairs={{0,8},{1,2},{2,1},{3,4},{4,3},{5,6},{6,5},{7,15},{8,0},{9,10},{10,... | collective-permute-start | bytes 614408 | tf_op jit(solution)/shard_map/ppermute | solution.py:447
  6.2 0.0 copy-start.10
  6.2 0.0 copy-start.6
  6.2 4.8 %all-to-all-start = ((f32[8,4,128]{2,1,0:T(4,128)}), f32[8,4,128]{2,1,0:T(4,128)S(1)}, u32[]{:S(2)}, u32[]{:S(2)}) async-start(f32[8,4,128]{2,1,0:T(4,128)} %get-tuple-element.22), calls=%async_computation | async-start | bytes 32768 | tf_op jit(solution)/shard_map/all_to_all | solution.py:448
  11.0 0.0 copy-done.10
  11.0 0.0 copy-start.9
  11.0 0.1 copy.14.wavelet
  11.1 0.0 collective-permute-done.pack_a
  11.1 0.0 collective-permute-done.1.pack_b
  11.1 0.0 copy-done
  11.1 0.0 copy-done.1
  11.1 0.0 copy-done.2
  11.1 0.0 copy-done.3
  11.1 0.0 copy-done.4
  11.1 0.0 copy-done.5
  11.1 0.0 copy-done.6
  11.1 0.5 %copy-done.9 = s32[1,8]{1,0:T(1,128)S(1)} copy-done((s32[1,8]{1,0:T(1,128)S(1)}, s32[1,8]{1,0:T(1,128)}, u32[]{:S(2)}) %copy-start.9) | copy-done | bytes 56
  11.6 0.0 copy-start.7
  11.6 1.5 %homogeneous.1 = (f32[4,32,8,128]{3,2,1,0:T(8,128)S(1)}, f32[32,8,128]{2,1,0:T(8,128)S(1)}, f32[32,8,128]{2,1,0:T(8,128)S(1)}, f32[32,8,128]{2,1,0:T(8,128)S(1)}...) custom-call(s32[1,8]{1,0:T(1,128)S(1)} %copy-done.9, f32[1,8,16,256]{3,2,1,0:T(8,128)S(1)} %copy-done, ...), custom_call_target="tpu_custom_call" | custom-call | tf_op jit(solution)/shard_map/homogeneous/pallas_call | solution.py:452
  13.1 3.5 %all-to-all-done.image_in = f32[8,4,128]{2,1,0:T(4,128)S(1)} async-done(((f32[8,4,128]{2,1,0:T(4,128)}), f32[8,4,128]{2,1,0:T(4,128)S(1)}, u32[]{:S(2)}, u32[]{:S(2)}) %all-to-all-start) | async-done | bytes 16416 | tf_op jit(solution)/shard_map/all_to_all | solution.py:448
  16.6 0.0 copy-start.8
  16.6 0.0 copy-done.7
  16.6 0.7 %copy-done.8 = s32[1,8]{1,0:T(1,128)S(1)} copy-done((s32[1,8]{1,0:T(1,128)S(1)}, s32[1,8]{1,0:T(1,128)}, u32[]{:S(2)}) %copy-start.8) | copy-done | bytes 56
  17.3 1.5 %scattered.1 = f32[32,1,1152]{2,1,0:T(1,128)S(1)} custom-call(s32[1]{0:T(128)S(6)} %copy.15.first_any.first, s32[1,8]{1,0:T(1,128)S(1)} %copy-done.8, f32[4,32,8,128]{3,2,1,0:T(8,128)S(1)} %get-tuple-element.16.acc, f32[32,8,128]{2,1,0:T(8,128)S(1)} %get-tuple-element.17.b0_in, f32[32,8,128]{2,1,0:T(8,128)S(1)} %get-tuple-element.18.b1_in, ...), custom_call_target="tpu_custom_call" | custom-call | tf_op jit(solution)/shard_map/scattered/pallas_call | solution.py:468
  18.8 10.2 %all_to_all.10.received = f32[32,1,1152]{2,1,0:T(1,128)S(1)} all-to-all(f32[32,1,1152]{2,1,0:T(1,128)S(1)} %scattered.1), channel_id=1, replica_groups=mesh['shot'=4,'box'=8] {'shot','box'}, dimensions={0} | all-to-all | bytes 294912 | tf_op jit(solution)/shard_map/all_to_all | solution.py:489
  29.0 0.7 %join.1 = f32[12,1,2,256]{3,2,1,0:T(2,128)} custom-call(f32[32,1,1152]{2,1,0:T(1,128)S(1)} %all_to_all.10.received), custom_call_target="tpu_custom_call" | custom-call | tf_op jit(solution)/shard_map/join/pallas_call | solution.py:490
Async XLA Ops:
  0.7 10.4 %copy-start = (f32[1,8,16,256]{3,2,1,0:T(8,128)S(1)}, f32[1,8,16,256]{3,2,1,0:T(8,128)}, u32[]{:S(2)}) copy-start(f32[1,8,16,256]{3,2,1,0:T(8,128)} %un.3) | copy-start | bytes 393220
  0.7 10.4 %copy-start.1 = (f32[1,8,16,256]{3,2,1,0:T(8,128)S(1)}, f32[1,8,16,256]{3,2,1,0:T(8,128)}, u32[]{:S(2)}) copy-start(f32[1,8,16,256]{3,2,1,0:T(8,128)} %up.3) | copy-start | bytes 393220
  0.7 10.4 %copy-start.2 = (f32[1,8,16,256]{3,2,1,0:T(8,128)S(1)}, f32[1,8,16,256]{3,2,1,0:T(8,128)}, u32[]{:S(2)}) copy-start(f32[1,8,16,256]{3,2,1,0:T(8,128)} %bn.3) | copy-start | bytes 393220
  0.7 10.4 %copy-start.3 = (f32[1,8,16,256]{3,2,1,0:T(8,128)S(1)}, f32[1,8,16,256]{3,2,1,0:T(8,128)}, u32[]{:S(2)}) copy-start(f32[1,8,16,256]{3,2,1,0:T(8,128)} %bp.3) | copy-start | bytes 393220
  0.7 10.4 %copy-start.4 = (f32[1,8,16,256]{3,2,1,0:T(8,128)S(1)}, f32[1,8,16,256]{3,2,1,0:T(8,128)}, u32[]{:S(2)}) copy-start(f32[1,8,16,256]{3,2,1,0:T(8,128)} %qn.3) | copy-start | bytes 393220
  0.7 10.4 %copy-start.5 = (f32[1,8,16,256]{3,2,1,0:T(8,128)S(1)}, f32[1,8,16,256]{3,2,1,0:T(8,128)}, u32[]{:S(2)}) copy-start(f32[1,8,16,256]{3,2,1,0:T(8,128)} %qp.3) | copy-start | bytes 393220
  3.1 8.0 %collective-permute-start = (f32[50,8,128]{2,1,0:T(8,128)}, f32[50,8,128]{2,1,0:T(8,128)S(1)}, u32[]{:S(2)}, u32[]{:S(2)}) collective-permute-start(f32[50,8,128]{2,1,0:T(8,128)} %get-tuple-element.14), channel_id=1, source_target_pairs={{0,1},{1,0},{2,3},{3,2},{4,5},{5,4},{6,7},{7,6},{8,9},{9,8},{10,11... | collective-permute-start | bytes 614408 | tf_op jit(solution)/shard_map/ppermute | solution.py:446
  3.6 7.4 %collective-permute-start.1 = (f32[50,8,128]{2,1,0:T(8,128)}, f32[50,8,128]{2,1,0:T(8,128)S(1)}, u32[]{:S(2)}, u32[]{:S(2)}) collective-permute-start(f32[50,8,128]{2,1,0:T(8,128)} %get-tuple-element.15), channel_id=1, source_target_pairs={{0,8},{1,2},{2,1},{3,4},{4,3},{5,6},{6,5},{7,15},{8,0},{9,10},{10,... | collective-permute-start | bytes 614408 | tf_op jit(solution)/shard_map/ppermute | solution.py:447
  6.2 4.8 %copy-start.10 = (f32[1,8,4]{1,2,0:T(4,128)S(1)}, f32[1,8,4]{1,2,0:T(4,128)}, u32[]{:S(2)}) copy-start(f32[1,8,4]{1,2,0:T(4,128)} %param.20) | copy-start | bytes 388
  6.2 4.9 %copy-start.6 = (f32[1,16,256]{2,1,0:T(8,128)S(1)}, f32[1,16,256]{2,1,0:T(8,128)}, u32[]{:S(2)}) copy-start(f32[1,16,256]{2,1,0:T(8,128)} %speed.1) | copy-start | bytes 49156
  6.2 10.4 %all-to-all-start = ((f32[8,4,128]{2,1,0:T(4,128)}), f32[8,4,128]{2,1,0:T(4,128)S(1)}, u32[]{:S(2)}, u32[]{:S(2)}) async-start(f32[8,4,128]{2,1,0:T(4,128)} %get-tuple-element.22), calls=%async_computation | async-start | bytes 32768 | tf_op jit(solution)/shard_map/all_to_all | solution.py:448
  11.0 0.7 %copy-start.9 = (s32[1,8]{1,0:T(1,128)S(1)}, s32[1,8]{1,0:T(1,128)}, u32[]{:S(2)}) copy-start(s32[1,8]{1,0:T(1,128)} %sources.1) | copy-start | bytes 100
  11.6 5.0 %copy-start.7 = (f32[1,8,4,8]{3,2,1,0:T(4,128)S(1)}, f32[1,8,4,8]{3,2,1,0:T(4,128)}, u32[]{:S(2)}) copy-start(f32[1,8,4,8]{3,2,1,0:T(4,128)} %obs.1) | copy-start | bytes 3076
  16.6 0.7 %copy-start.8 = (s32[1,8]{1,0:T(1,128)S(1)}, s32[1,8]{1,0:T(1,128)}, u32[]{:S(2)}) copy-start(s32[1,8]{1,0:T(1,128)} %rec.1) | copy-start | bytes 100

commit v3 on v2

--- a/solution.py
+++ b/solution.py
@@ -35,8 +35,25 @@
     return lax.broadcasted_iota(jnp.int32, (8, LANES), 1)
 
 
+def choose_kernel(first, own, other, info_in, info, *picks, columns):
+    info[...] = info_in[...]
+    info[0] = jnp.full((8, LANES), first[0])
+    position = lax.axis_index("box")
+    owners = 2 * len(picks)
+    rounds = own.shape[0]
+    for i, pick in enumerate(picks):
+        target = position ^ (2 * i)
+        low_tile = first[0] + (columns // 2) * target - 3
+        for core, tiles in enumerate((own, other)):
+            owner = position ^ core
+            r0 = lax.div(low_tile - owner + 2 * owners - 1, owners) - 1
+            for slot in range(2):
+                r = jnp.clip(r0 + slot, 0, rounds - 1)
+                pick[core, 2 * slot : 2 * slot + 2, :] = tiles[r, 0, :, 0:LANES]
+
+
 def pack_kernel(
-    first_any,
+    sources_any,
     rec_any,
     un,
     up,
@@ -46,13 +63,11 @@
     qp,
     speed_any,
     obs_any,
-    refl_any,
     pack_a,
     pack_b,
-    image_out,
-    first,
+    info,
+    sources,
     rec,
-    refl,
     wide,
     near,
     speed,
@@ -62,51 +77,73 @@
     columns, depth = un.shape[2], un.shape[3]
     position = lax.axis_index("box")
     even = lax.rem(position, 2) == 0
+    lane = lane_iota()
+    row = lax.broadcasted_iota(jnp.int32, (8, LANES), 0)
     edges = (pl.ds(0, 8), pl.ds(columns - 8, 8))
     wides = {"un": 0, "up": 1, "qn": 2, "qp": 3}
     nears = {"bn": 0, "bp": 1}
-    moves = [(first_any, first), (rec_any, rec), (obs_any, obs), (refl_any, refl)]
-    for side in range(2):
-        for name, ref in (("un", un), ("up", up), ("qn", qn), ("qp", qp)):
-            moves.append((ref.at[0, :, edges[side], :], wide.at[side, wides[name]]))
-        for name, ref in (("bn", bn), ("bp", bp)):
-            moves.append((ref.at[0, :, edges[side], pl.ds(0, LANES)], near.at[side, nears[name]]))
-        moves.append((speed_any.at[0, edges[side], :], speed.at[side]))
-    copies = [pltpu.make_async_copy(*move, sems.at[i]) for i, move in enumerate(moves)]
-    for copy in copies:
-        copy.start()
-    for copy in copies:
-        copy.wait()
-
-    owners = image_out.shape[0]
-    for target in range(owners):
-        low_tile = first[0] + (columns // 2) * target - 3
-        r0 = lax.div(low_tile - position + 2 * owners - 1, owners) - 1
-        for slot in range(2):
-            r = jnp.clip(r0 + slot, 0, refl.shape[0] - 1)
-            image_out[target, 2 * slot : 2 * slot + 2, :] = refl[r, 0, :, 0:LANES]
+    fields = {"un": un, "up": up, "bn": bn, "bp": bp, "qn": qn, "qp": qp}
+
+    moves = [[(sources_any, sources), (rec_any, rec)]]
+    for name, ref in fields.items():
+        group = []
+        for side in range(2):
+            if name in wides:
+                group.append((ref.at[0, :, edges[side], :], wide.at[side, wides[name]]))
+            else:
+                source = ref.at[0, :, edges[side], pl.ds(0, LANES)]
+                group.append((source, near.at[side, nears[name]]))
+        moves.append(group)
+    moves.append([(speed_any.at[0, edges[side], :], speed.at[side]) for side in range(2)])
+    moves[-1].append((obs_any, obs))
+    copies, i = [], 0
+    for group in moves:
+        copies.append([])
+        for move in group:
+            copies[-1].append(pltpu.make_async_copy(*move, sems.at[i]))
+            copies[-1][-1].start()
+            i += 1
+
+    def arrive(group):
+        for copy in copies[group]:
+            copy.wait()
+
+    arrive(0)
+    own_cell = position * columns * depth
+    info[0] = jnp.zeros((8, LANES), jnp.int32)
+    cell = jnp.zeros((8, LANES), jnp.int32)
+    for s in range(8):
+        cell = jnp.where(row == s, sources[0, s] - own_cell, cell)
+    info[1] = cell
+    count = rec.shape[1]
+    for block in range(0, count, 8):
+        cell = jnp.zeros((8, LANES), jnp.int32)
+        for r in range(min(8, count - block)):
+            cell = jnp.where(row == r, rec[0, block + r] - own_cell, cell)
+        info[2 + block // 8] = cell
 
     def put(tile, left, right):
         pack_a[tile] = jnp.where(even, right, left)
         pack_b[tile] = jnp.where(even, left, right)
 
-    tile = 0
-    for name, half, count in HALO:
+    arrived, tile = set(), 0
+    for name, half, width in HALO:
+        if name not in arrived:
+            arrive(1 + list(fields).index(name))
+            arrived.add(name)
         part = slice(half * LANES, (half + 1) * LANES)
         if name in nears:
             low, high = (near[side, nears[name]] for side in range(2))
         else:
             low, high = (wide[side, wides[name], :, :, part] for side in range(2))
         low, high = jnp.swapaxes(low, 0, 1), jnp.swapaxes(high, 0, 1)
-        for j in range(1, count + 1):
+        for j in range(1, width + 1):
             put(tile, low[j - 1], high[8 - j])
             tile += 1
+    arrive(1 + len(fields))
     for half in range(2):
         part = slice(half * LANES, (half + 1) * LANES)
         put(SPEED_TILE + half, speed[0, :, part], speed[1, :, part])
-
-    lane = lane_iota()
-    count = rec.shape[1]
 
     def meta(right):
         out = jnp.zeros((8, LANES), jnp.float32)
@@ -150,7 +187,7 @@
 
 
 def homogeneous_kernel(
-    sources,
+    info,
     un,
     up,
     bn,
@@ -158,32 +195,39 @@
     qn,
     qp,
     speed,
+    obs,
     wavelet,
     pack_a,
     pack_b,
     acc,
+    near_speed,
+    hit_out,
+    ahead,
+    out,
+    u0,
+    u1,
     b0,
     b1,
-    near_speed,
-    meta,
-    rows_out,
-    u0,
-    u1,
     q0,
     q1,
     vel,
     late,
+    *,
+    owners,
+    groups,
 ):
     columns, depth = speed.shape[1], speed.shape[2]
+    tiles = columns // 2
     position = lax.axis_index("box")
     even = lax.rem(position, 2) == 0
     has_left = position > 0
-    has_right = position < lax.axis_size("box") - 1
+    has_right = position < owners - 1
     lane = lane_iota()
     edges = lane == 0, lane == LANES - 1
     zero = jnp.zeros((8, LANES), jnp.float32)
     halves = (slice(0, LANES), slice(LANES, 2 * LANES))
     scratch = {"un": u0, "up": u1, "bn": b0, "bp": b1, "qn": q0, "qp": q1}
+    first = info[0, 0, 0]
 
     for name, ref in (("un", un), ("up", up), ("qn", qn), ("qp", qp)):
         for c in range(0, columns, 8):
@@ -215,19 +259,12 @@
             vel[MARGIN + columns - 1 + j, :, halves[half]] = jnp.broadcast_to(
                 right[j - 1 : j], (8, LANES)
             )
-    meta_left, meta_right = got(META_TILE)
-    meta[0] = meta_left
-    meta[1] = meta_right
+    meta = got(META_TILE)
     for c in range(-6, columns + 6):
         near_speed[MARGIN + c] = vel[MARGIN + c, :, halves[0]]
 
-    shot = lax.broadcasted_iota(jnp.int32, (8, LANES), 0)
-    cell = jnp.zeros((8, LANES), jnp.int32)
-    for s in range(8):
-        cell = jnp.where(shot == s, sources[0, s] - position * columns * depth, cell)
-    cell = cell - lane
+    cell = info[1] - lane
     pulses = [jnp.broadcast_to(wavelet[0, :, t : t + 1], (8, LANES)) for t in range(STEPS)]
-
     new_u, old_u = u0, u1
     illum = [[zero, zero] for _ in range(columns)]
     for t in range(STEPS):
@@ -248,6 +285,35 @@
                     illum[c][h] = illum[c][h] + a * a
         new_u, old_u = old_u, new_u
 
+    reach = STEPS - 1
+    recorded = {}
+    for c in range(-reach, columns + reach):
+        if 0 <= c < columns:
+            r = c // 2
+            here = jnp.broadcast_to(info[2 + r // 8, r % 8 : r % 8 + 1, :], (8, LANES))
+            hit = lane == here - c * depth
+            columns_of = [obs[0, :, t, r : r + 1] for t in range(STEPS)]
+        else:
+            j = -c if c < 0 else c - columns + 1
+            side, k = meta[0] if c < 0 else meta[1], (j - 1) // 2
+            code = jnp.broadcast_to(side[:, 2 * STEPS + k : 2 * STEPS + k + 1], (8, LANES))
+            hit = code == (lane + j * depth).astype(jnp.float32)
+            columns_of = [side[:, 2 * t + k : 2 * t + k + 1] for t in range(STEPS)]
+        hit_out[reach + c] = jnp.where(hit, 1.0, 0.0)
+        recorded[c] = columns_of
+    new_b, old_b = b0, b1
+    for t in range(STEPS):
+        wide = 2 * reach - t
+        for c in range(-wide, columns + wide):
+            e = MARGIN + c
+            (mid,), (laps,) = lap(new_b, e, 1, edges)
+            b = 2.0 * mid - old_b[e] + vel[e, :, halves[0]] * laps
+            old_b[e] = b
+            if -t <= c < columns + t:
+                value = jnp.broadcast_to(recorded[c][t], (8, LANES))
+                ahead[t, reach + c] = hit_out[reach + c] * (b - value)
+        new_b, old_b = old_b, new_b
+
     grad = [[zero, zero] for _ in range(columns)]
     new_q, old_q = q0, q1
     for t in reversed(range(STEPS)):
@@ -262,83 +328,72 @@
                     grad[c][h] = grad[c][h] + q * a
         new_q, old_q = old_q, new_q
 
-    for k in range(columns // 2):
+    start = jnp.full((1, LANES), first.astype(jnp.float32))
+    for k in range(tiles):
+        owner = lax.rem(first + tiles * position + k, owners)
         i = 0
         for sums in (grad, illum):
             for h in range(2):
                 for w in range(2):
-                    rows_out[k, :, i * LANES : (i + 1) * LANES] = jnp.sum(
-                        sums[2 * k + w][h], axis=0, keepdims=True
-                    )
+                    total = jnp.sum(sums[2 * k + w][h], axis=0, keepdims=True)
+                    for group in range(groups):
+                        out[group * owners + owner, :, i * LANES : (i + 1) * LANES] = total
                     i += 1
+        for group in range(groups):
+            out[group * owners + owner, :, 8 * LANES : 9 * LANES] = start
 
 
 def scattered_kernel(
-    first,
-    rec,
+    info,
     acc,
-    b0_in,
-    b1_in,
     speed,
-    meta,
-    rows_in,
-    obs,
-    image_in,
-    out,
-    b0,
-    b1,
-    q0,
-    q1,
-    img,
-    *,
+    hit,
+    ahead,
+    *refs,
     owners,
     groups,
-    depth,
 ):
-    columns = 2 * rows_in.shape[0]
+    images, (_, out, b0, b1, q0, q1, img) = refs[: owners // 2], refs[owners // 2 :]
+    reach = STEPS - 1
+    columns = hit.shape[0] - 2 * reach
     tiles = columns // 2
     position = lax.axis_index("box")
     lane = lane_iota()
     edges = lane == 0, lane == LANES - 1
     zero = jnp.zeros((8, LANES), jnp.float32)
-
-    low_tile = first[0] + tiles * position - 3 + owners
+    first = info[0, 0, 0]
+
+    low_tile = first + tiles * position - 3 + owners
     for m in range(tiles + 6):
-        owner = lax.rem(low_tile + m, owners)
-        slot = 2 * (m // owners)
-        pair = image_in[owner, slot : slot + 2, :]
+        apart = lax.rem(low_tile + m, owners) ^ position
+        chips, core = lax.div(apart, 2), lax.rem(apart, 2)
+        part = slice(2 * (m // owners), 2 * (m // owners) + 2)
+        pair = images[0][core, part, :]
+        for i in range(1, owners // 2):
+            pair = jnp.where(chips == i, images[i][core, part, :], pair)
         for w in range(2):
             img[MARGIN - 6 + 2 * m + w] = jnp.broadcast_to(pair[w : w + 1], (8, LANES))
 
-    def receiver(c):
-        if c < 0 or c >= columns:
-            j = -c if c < 0 else c - columns + 1
-            side = meta[0] if c < 0 else meta[1]
-            k = (j - 1) // 2
-            lane_of = 2 * STEPS + k
-            code = jnp.broadcast_to(side[:, lane_of : lane_of + 1], (8, LANES))
-            mask = code == (lane + j * depth).astype(jnp.float32)
-            return mask, lambda t: jnp.broadcast_to(
-                side[:, 2 * t + k : 2 * t + k + 1], (8, LANES)
-            )
-        r = c // 2
-        here = rec[0, r] - (position * columns + c) * depth
-        return lane == here, lambda t: jnp.broadcast_to(obs[0, :, t, r : r + 1], (8, LANES))
-
     misfits = []
-    new_b, old_b, spare = b0_in, b1_in, [b0, b1]
+    new_b, old_b = b0, b1
     for t in range(STEPS):
-        next_b = spare[t % 2]
-        for c in range(t - 6, columns + 6 - t):
+        wide = 2 * reach - t
+        for c in range(-wide, columns + wide):
             e = MARGIN + c
-            (mid,), (laps,) = lap(new_b, e, 1, edges)
-            next_b[e] = 2.0 * mid - old_b[e] + speed[e] * laps + img[e] * acc[t, e]
-        old_b, new_b = new_b, next_b
-        part = {}
-        for c in range(-t, columns + t):
-            mask, recorded = receiver(c)
-            part[c] = jnp.where(mask, new_b[MARGIN + c] - recorded(t), 0.0)
-        misfits.append(part)
+            b = img[e] * acc[t, e]
+            if t > 0:
+                (mid,), (laps,) = lap(new_b, e, 1, edges)
+                b = b + 2.0 * mid + speed[e] * laps
+            if t > 1:
+                b = b - old_b[e]
+            old_b[e] = b
+        new_b, old_b = old_b, new_b
+        misfits.append(
+            {
+                c: hit[reach + c] * new_b[MARGIN + c] + ahead[t, reach + c]
+                for c in range(-t, columns + t)
+            }
+        )
 
     grad = [zero] * columns
     new_q, old_q = q0, q1
@@ -356,18 +411,13 @@
                 grad[c] = grad[c] + q * acc[t, e]
         new_q, old_q = old_q, new_q
 
-    start = jnp.full((1, LANES), first[0].astype(jnp.float32))
     for k in range(tiles):
-        owner = lax.rem(first[0] + tiles * position + k, owners)
-        rows = rows_in[k]
-        near = [jnp.sum(grad[2 * k + w], axis=0, keepdims=True) for w in range(2)]
-        for group in range(groups):
-            to = group * owners + owner
-            out[to, :, 2 * LANES : 8 * LANES] = rows[:, 2 * LANES :]
-            for w in range(2):
-                part = slice(w * LANES, (w + 1) * LANES)
-                out[to, :, part] = rows[:, part] + near[w]
-            out[to, :, 8 * LANES : 9 * LANES] = start
+        owner = lax.rem(first + tiles * position + k, owners)
+        for w in range(2):
+            part = slice(w * LANES, (w + 1) * LANES)
+            total = out[owner, :, part] + jnp.sum(grad[2 * k + w], axis=0, keepdims=True)
+            for group in range(groups):
+                out[group * owners + owner, :, part] = total
 
 
 def join_kernel(received, migrated, total, *, owners, groups):
@@ -409,33 +459,38 @@
     groups = lax.axis_size("shot")
     columns, depth = velocity.shape[1], velocity.shape[2]
     rounds = reflectivity.shape[0]
-    smem, vmem = pl.BlockSpec(memory_space=SMEM), pl.BlockSpec(memory_space=VMEM)
+    vmem = pl.BlockSpec(memory_space=VMEM)
     anywhere = pl.BlockSpec(memory_space=pl.ANY)
     f32 = jnp.float32
-    params = pltpu.CompilerParams(vmem_limit_bytes=32 * 1024 * 1024)
-    params_hbm = pltpu.CompilerParams(vmem_limit_bytes=60 * 1024 * 1024)
+    params = pltpu.CompilerParams(vmem_limit_bytes=24 * 1024 * 1024)
+    params_hbm = pltpu.CompilerParams(vmem_limit_bytes=24 * 1024 * 1024)
     fields = (u_now, u_prev, born_now, born_prev, adj_last, adj_after)
 
-    pack = jax.ShapeDtypeStruct((PACK_TILES, 8, LANES), f32)
-    send_a, send_b, image_out = pl.pallas_call(
+    shape = jax.ShapeDtypeStruct
+    pack = VMEM((PACK_TILES, 8, LANES), f32)
+    blocks = 2 + pl.cdiv(receivers.shape[1], 8)
+    pack_from = (sources, receivers, *fields, velocity, observed)
+    send_a, send_b, info = pl.pallas_call(
         pack_kernel,
-        out_shape=(pack, pack, jax.ShapeDtypeStruct((owners, 4, LANES), f32)),
-        in_specs=[anywhere] * 11,
+        out_shape=(
+            pack,
+            pack,
+            VMEM((blocks, 8, LANES), jnp.int32),
+        ),
+        in_specs=[anywhere] * 10,
         out_specs=(vmem,) * 3,
         scratch_shapes=[
-            SMEM(first_tile.shape, jnp.int32),
+            SMEM(sources.shape, jnp.int32),
             SMEM(receivers.shape, jnp.int32),
-            VMEM(reflectivity.shape, f32),
             VMEM((2, 4, 8, 8, depth), f32),
             VMEM((2, 2, 8, 8, LANES), f32),
             VMEM((2, 8, depth), f32),
             VMEM(observed.shape, f32),
-            pltpu.SemaphoreType.DMA((18,)),
+            pltpu.SemaphoreType.DMA((17,)),
         ],
         compiler_params=params_hbm,
         name="pack",
-    )(first_tile, receivers, *fields, velocity, observed, reflectivity)
-
+    )(*(pltpu.with_memory_space_constraint(x, pltpu.HBM) for x in pack_from))
     ends = (0, owners - 1)
     swap_a = [(i, i ^ 1) for i in range(owners)]
     swap_b = [
@@ -445,46 +500,52 @@
     ]
     got_a = lax.ppermute(send_a, "box", swap_a)
     got_b = lax.ppermute(send_b, ("shot", "box"), swap_b)
-    image_in = lax.all_to_all(image_out, "box", split_axis=0, concat_axis=0, tiled=True)
+    other_image = lax.ppermute(reflectivity, "box", swap_a)
+    info, *picks = pl.pallas_call(
+        functools.partial(choose_kernel, columns=columns),
+        out_shape=(VMEM((blocks, 8, LANES), jnp.int32),)
+        + (VMEM((2, 4, LANES), f32),) * (owners // 2),
+        in_specs=[pl.BlockSpec(memory_space=SMEM)] + [vmem] * 3,
+        out_specs=(vmem,) * (1 + owners // 2),
+        compiler_params=params,
+        name="choose",
+    )(first_tile, reflectivity, other_image, info)
+    images = [picks[0]] + [
+        lax.ppermute(picks[i], "box", [(j, j ^ (2 * i)) for j in range(owners)])
+        for i in range(1, owners // 2)
+    ]
 
     ext = columns + 2 * MARGIN
-    shape = jax.ShapeDtypeStruct
-    acc, b0, b1, near_speed, meta, rows = pl.pallas_call(
-        homogeneous_kernel,
+    near = columns + 2 * (STEPS - 1)
+    payload = shape((groups * owners, 1, 9 * LANES), f32)
+    acc, near_speed, hit, ahead, part = pl.pallas_call(
+        functools.partial(homogeneous_kernel, owners=owners, groups=groups),
         out_shape=(
             shape((STEPS, ext, 8, LANES), f32),
             shape((ext, 8, LANES), f32),
-            shape((ext, 8, LANES), f32),
-            shape((ext, 8, LANES), f32),
-            shape((2, 8, LANES), f32),
-            shape((columns // 2, 1, 8 * LANES), f32),
+            shape((near, 8, LANES), f32),
+            shape((STEPS, near, 8, LANES), f32),
+            payload,
         ),
-        in_specs=[smem] + [vmem] * 10,
-        out_specs=(vmem,) * 6,
-        scratch_shapes=[VMEM((ext, 8, depth), f32)] * 5 + [VMEM((STEPS, columns, 8, LANES), f32)],
+        in_specs=[vmem] * 12,
+        out_specs=(vmem,) * 5,
+        scratch_shapes=[VMEM((ext, 8, depth), f32)] * 2
+        + [VMEM((ext, 8, LANES), f32)] * 2
+        + [VMEM((ext, 8, depth), f32)] * 3
+        + [VMEM((STEPS, columns, 8, LANES), f32)],
         compiler_params=params,
         name="homogeneous",
-    )(sources, *fields, velocity, wavelet, got_a, got_b)
+    )(info, *fields, velocity, observed, wavelet, got_a, got_b)
     out = pl.pallas_call(
-        functools.partial(scattered_kernel, owners=owners, groups=groups, depth=depth),
-        out_shape=shape((groups * owners, 1, 9 * LANES), f32),
-        in_specs=[smem] * 2 + [vmem] * 8,
+        functools.partial(scattered_kernel, owners=owners, groups=groups),
+        out_shape=payload,
+        in_specs=[vmem] * (6 + len(images)),
         out_specs=vmem,
         scratch_shapes=[VMEM((ext, 8, LANES), f32)] * 5,
+        input_output_aliases={5 + len(images): 0},
         compiler_params=params,
         name="scattered",
-    )(
-        first_tile,
-        receivers,
-        acc,
-        b0,
-        b1,
-        near_speed,
-        meta,
-        rows,
-        observed,
-        image_in,
-    )
+    )(info, acc, near_speed, hit, ahead, *images, part)
 
     received = lax.all_to_all(out, ("shot", "box"), split_axis=0, concat_axis=0, tiled=True)
     return pl.pallas_call(

time: 30 us -> 27.5 us (0.917)
  Pallas kernels: 6.06 us -> 4.8 us
  local copies, waits for them, and re-layouts: 1.27 us -> 0.12 us
  blocking collectives: 10.2 us -> 10.6 us
    all_to_all x1 -> x0, starting transfers between devices: 4.77 us -> none  [on_device(): lax.all_to_all(image_out, 'box', split_axis=0, concat_axis=0, tiled=True)]
    ppermute x0 -> x4, starting transfers between devices: none -> 4.65 us  [the longest x3 4.45 us: on_device(): lax.ppermute(picks[i], 'box', [(j, j ^ 2 * i) for j in range(owners)])]
    all_to_all x1 -> x0, waiting for transfers between devices: 3.53 us -> none  [on_device(): lax.all_to_all(image_out, 'box', split_axis=0, concat_axis=0, tiled=True)]
    ppermute x0 -> x4, waiting for transfers between devices: none -> 3.24 us  [the longest x3 2.9 us: on_device(): lax.ppermute(picks[i], 'box', [(j, j ^ 2 * i) for j in range(owners)])]
    unnamed x23 -> x21, local copies, waits for them, and re-layouts: 1.27 us -> 0.12 us
    pallas_call x1, Pallas kernels: 1.52 us -> 0.59 us  [on_device(): pl.pallas_call(functools.partial(scattered_kernel, owners=owners, groups=...]
    all_to_all x1, blocking collectives: 10.2 us -> 10.6 us  [on_device(): lax.all_to_all(out, ('shot', 'box'), split_axis=0, concat_axis=0, tiled=T...]
    pallas_call x2 -> x3, Pallas kernels: 3.83 us -> 3.5 us  [the longest x1 1.9 us: on_device(): pl.pallas_call(functools.partial(homogeneous_kernel, owners=owners, group...]
  transfers between devices with their start and end apart: 3 -> 6, of which waited for: 1 -> 2; matrix products, arithmetic and copies ran while one was open for 0% -> 0% of each run, Pallas kernels for 5% -> 7%
where the time goes in v3:
time: 27.5 us; the launch traced here: 27.4 us
  blocking collectives  10.6 us (39%)
  starting transfers between devices  7.76 us (28%)
  Pallas kernels  4.8 us (17%)
  waiting for transfers between devices  3.24 us (12%)
  between operations  0.79 us (3%)
    all_to_all x1, blocking collectives, on_device(): lax.all_to_all(out, ('shot', 'box'), split_axis=0, concat_axis=0, tiled=T...  10.6 us
    ppermute x3, starting transfers between devices, on_device(): lax.ppermute(picks[i], 'box', [(j, j ^ 2 * i) for j in range(owners)])  4.45 us
    ppermute x3, waiting for transfers between devices, on_device(): lax.ppermute(picks[i], 'box', [(j, j ^ 2 * i) for j in range(owners)])  2.9 us
    ppermute x1, starting transfers between devices, on_device(): got_b = lax.ppermute(send_b, ('shot', 'box'), swap_b)  2.56 us
    pallas_call x1, Pallas kernels, on_device(): pl.pallas_call(functools.partial(homogeneous_kernel, owners=owners, group...  1.9 us
    pallas_call x1, Pallas kernels, on_device(): pl.pallas_call(pack_kernel, out_shape=(pack, pack, VMEM((blocks, 8, LANES...  1.57 us
    pallas_call x1, Pallas kernels, on_device(): pl.pallas_call(functools.partial(join_kernel, owners=owners, groups=group...  0.71 us
    pallas_call x1, Pallas kernels, on_device(): pl.pallas_call(functools.partial(scattered_kernel, owners=owners, groups=...  0.59 us
  transfers between devices with their start and end apart: 6, of which 2 were waited for; matrix products, arithmetic and copies ran while one was open for 0% of the time, Pallas kernels for 7%

profile of v3, /device:TPU:0, one launch (start us, length us, event | category | flops | bytes accessed | tf_op | source)
XLA Modules:
  0.0 27.4 jit_solution(7210312167977051776)
XLA Ops:
  0.0 0.0 copy-start.8
  0.0 0.0 copy-start
  0.0 0.0 copy-start.1
  0.0 0.0 copy-start.2
  0.0 0.0 copy-start.3
  0.0 0.0 copy-start.4
  0.0 0.0 copy-start.5
  0.0 1.6 %pack.1 = (f32[50,8,128]{2,1,0:T(8,128)S(1)}, f32[50,8,128]{2,1,0:T(8,128)S(1)}, s32[3,8,128]{2,1,0:T(8,128)S(1)}) custom-call(s32[1,8]{1,0:T(1,128)} %sources_any.1, s32[1,8]{1,0:T(1,128)} %rec_any.1, f32[1,8,16,256]{3,2,1,0:T(8,128)} %un.3, f32[1,8,16,256]{3,2,1,0:T(8,128)} %up.3, f32[1,8,16,256]{3,2,1,0:T(8,128)} %bn.3, f32[1,8,16,256]{3,2,1,0:T(8,128)} %bp.3, ...), custom_call_target="tpu_custom_call" | custom-call | tf_op jit(solution)/shard_map/pack/pallas_call | solution.py:473
  1.6 0.5 %collective-permute-start.1 = (f32[50,8,128]{2,1,0:T(8,128)S(1)}, f32[50,8,128]{2,1,0:T(8,128)S(1)}, u32[]{:S(2)}, u32[]{:S(2)}) collective-permute-start(f32[50,8,128]{2,1,0:T(8,128)S(1)} %get-tuple-element.20), channel_id=1, source_target_pairs={{0,1},{1,0},{2,3},{3,2},{4,5},{5,4},{6,7},{7,6},{8,9},{9,8},{10,11... | collective-permute-start | bytes 614408 | tf_op jit(solution)/shard_map/ppermute | solution.py:501
  2.2 2.6 %collective-permute-start.2 = (f32[50,8,128]{2,1,0:T(8,128)S(1)}, f32[50,8,128]{2,1,0:T(8,128)S(1)}, u32[]{:S(2)}, u32[]{:S(2)}) collective-permute-start(f32[50,8,128]{2,1,0:T(8,128)S(1)} %get-tuple-element.21), channel_id=1, source_target_pairs={{0,8},{1,2},{2,1},{3,4},{4,3},{5,6},{6,5},{7,15},{8,0},{9,10},{10,... | collective-permute-start | bytes 614408 | tf_op jit(solution)/shard_map/ppermute | solution.py:502
  4.7 0.0 copy-done.8
  4.7 0.2 collective-permute-start
  5.6 0.3 %collective-permute-done.other = f32[12,1,2,256]{3,2,1,0:T(2,128)S(1)} collective-permute-done((f32[12,1,2,256]{3,2,1,0:T(2,128)S(1)}, f32[12,1,2,256]{3,2,1,0:T(2,128)S(1)}, u32[]{:S(2)}, u32[]{:S(2)}) %collective-permute-start) | collective-permute-done | bytes 24608 | tf_op jit(solution)/shard_map/ppermute | solution.py:503
  5.9 0.0 copy-start.6
  5.9 0.0 copy-start.7
  6.0 0.0 copy-start.9
  6.0 1.5 %collective-permute-start.3 = (f32[2,4,128]{2,1,0:T(4,128)S(1)}, f32[2,4,128]{2,1,0:T(4,128)S(1)}, u32[]{:S(2)}, u32[]{:S(2)}) collective-permute-start(f32[2,4,128]{2,1,0:T(4,128)S(1)} %get-tuple-element.27), channel_id=1, source_target_pairs={{0,2},{1,3},{2,0},{3,1},{4,6},{5,7},{6,4},{7,5},{8,10},{9,11},{10,... | collective-permute-start | bytes 12296 | tf_op jit(solution)/shard_map/ppermute | solution.py:514
  7.5 2.5 %collective-permute-start.4 = (f32[2,4,128]{2,1,0:T(4,128)S(1)}, f32[2,4,128]{2,1,0:T(4,128)S(1)}, u32[]{:S(2)}, u32[]{:S(2)}) collective-permute-start(f32[2,4,128]{2,1,0:T(4,128)S(1)} %get-tuple-element.28), channel_id=1, source_target_pairs={{0,4},{1,5},{2,6},{3,7},{4,0},{5,1},{6,2},{7,3},{8,12},{9,13},{10,... | collective-permute-start | bytes 12296 | tf_op jit(solution)/shard_map/ppermute | solution.py:514
  10.0 0.4 %collective-permute-start.5 = (f32[2,4,128]{2,1,0:T(4,128)S(1)}, f32[2,4,128]{2,1,0:T(4,128)S(1)}, u32[]{:S(2)}, u32[]{:S(2)}) collective-permute-start(f32[2,4,128]{2,1,0:T(4,128)S(1)} %get-tuple-element.29), channel_id=1, source_target_pairs={{0,6},{1,7},{2,4},{3,5},{4,2},{5,3},{6,0},{7,1},{8,14},{9,15},{10,... | collective-permute-start | bytes 12296 | tf_op jit(solution)/shard_map/ppermute | solution.py:514
  10.4 0.0 copy-done.9
  10.4 0.1 copy.15.wavelet
  10.5 0.0 collective-permute-done.1.pack_a
  10.5 0.0 collective-permute-done.2.pack_b
  10.5 0.0 copy-done
  10.5 0.0 copy-done.1
  10.5 0.0 copy-done.2
  10.5 0.0 copy-done.3
  10.6 0.0 copy-done.4
  10.6 0.0 copy-done.5
  10.6 0.0 copy-done.6
  10.6 0.0 copy-done.7
  10.6 1.9 %homogeneous.1 = (f32[4,32,8,128]{3,2,1,0:T(8,128)S(1)}, f32[32,8,128]{2,1,0:T(8,128)S(1)}, f32[22,8,128]{2,1,0:T(8,128)S(1)}, f32[4,22,8,128]{3,2,1,0:T(8,128)S(1)}, f32[32,1,1152]{2,1,0:T(1,128)S(1)}) custom-call(s32[3,8,128]{2,1,0:T(8,128)S(1)} %get-tuple-element.19.info, f32[1,8,16,256]{3,2,1,0:T(8,128)S(1)} %copy-done, f32[1,8,16,256]{3,2,1,0:T(8,128)S(1)} %copy-done.1, ...), custom_call_target="tpu_custom_call" | custom-call | tf_op jit(solution)/shard_map/homogeneous/pallas_call | solution.py:521
  12.5 0.0 collective-permute-done.3.refs_1_
  12.5 0.0 collective-permute-done.4.refs_2_
  12.5 2.9 %collective-permute-done.5.refs_3_ = f32[2,4,128]{2,1,0:T(4,128)S(1)} collective-permute-done((f32[2,4,128]{2,1,0:T(4,128)S(1)}, f32[2,4,128]{2,1,0:T(4,128)S(1)}, u32[]{:S(2)}, u32[]{:S(2)}) %collective-permute-start.5) | collective-permute-done | bytes 4128 | tf_op jit(solution)/shard_map/ppermute | solution.py:514
  15.4 0.6 %scattered.1 = f32[32,1,1152]{2,1,0:T(1,128)S(1)} custom-call(s32[3,8,128]{2,1,0:T(8,128)S(1)} %get-tuple-element.19.info, f32[4,32,8,128]{3,2,1,0:T(8,128)S(1)} %get-tuple-element.22.acc, f32[32,8,128]{2,1,0:T(8,128)S(1)} %get-tuple-element.23.speed, f32[22,8,128]{2,1,0:T(8,128)S(1)} %get-tuple-element.24.hit, ...), custom_call_target="tpu_custom_call", output_to_operand_aliasing={{}: (9, {})} | custom-call | tf_op jit(solution)/shard_map/scattered/pallas_call | solution.py:539
  16.0 10.6 %all_to_all.5.received = f32[32,1,1152]{2,1,0:T(1,128)S(1)} all-to-all(f32[32,1,1152]{2,1,0:T(1,128)S(1)} %scattered.1), channel_id=1, replica_groups=mesh['shot'=4,'box'=8] {'shot','box'}, dimensions={0} | all-to-all | bytes 294912 | tf_op jit(solution)/shard_map/all_to_all | solution.py:550
  26.7 0.7 %join.1 = f32[12,1,2,256]{3,2,1,0:T(2,128)} custom-call(f32[32,1,1152]{2,1,0:T(1,128)S(1)} %all_to_all.5.received), custom_call_target="tpu_custom_call" | custom-call | tf_op jit(solution)/shard_map/join/pallas_call | solution.py:551
  (1 shorter events, 0.0 us)
Async XLA Ops:
  0.0 4.7 %copy-start.8 = (f32[12,1,2,256]{3,2,1,0:T(2,128)S(1)}, f32[12,1,2,256]{3,2,1,0:T(2,128)}, u32[]{:S(2)}) copy-start(f32[12,1,2,256]{3,2,1,0:T(2,128)} %own.1) | copy-start | bytes 73732
  0.0 10.5 %copy-start = (f32[1,8,16,256]{3,2,1,0:T(8,128)S(1)}, f32[1,8,16,256]{3,2,1,0:T(8,128)}, u32[]{:S(2)}) copy-start(f32[1,8,16,256]{3,2,1,0:T(8,128)} %un.3) | copy-start | bytes 393220
  0.0 10.5 %copy-start.1 = (f32[1,8,16,256]{3,2,1,0:T(8,128)S(1)}, f32[1,8,16,256]{3,2,1,0:T(8,128)}, u32[]{:S(2)}) copy-start(f32[1,8,16,256]{3,2,1,0:T(8,128)} %up.3) | copy-start | bytes 393220
  0.0 10.5 %copy-start.2 = (f32[1,8,16,256]{3,2,1,0:T(8,128)S(1)}, f32[1,8,16,256]{3,2,1,0:T(8,128)}, u32[]{:S(2)}) copy-start(f32[1,8,16,256]{3,2,1,0:T(8,128)} %bn.3) | copy-start | bytes 393220
  0.0 10.5 %copy-start.3 = (f32[1,8,16,256]{3,2,1,0:T(8,128)S(1)}, f32[1,8,16,256]{3,2,1,0:T(8,128)}, u32[]{:S(2)}) copy-start(f32[1,8,16,256]{3,2,1,0:T(8,128)} %bp.3) | copy-start | bytes 393220
  0.0 10.5 %copy-start.4 = (f32[1,8,16,256]{3,2,1,0:T(8,128)S(1)}, f32[1,8,16,256]{3,2,1,0:T(8,128)}, u32[]{:S(2)}) copy-start(f32[1,8,16,256]{3,2,1,0:T(8,128)} %qn.3) | copy-start | bytes 393220
  0.0 10.5 %copy-start.5 = (f32[1,8,16,256]{3,2,1,0:T(8,128)S(1)}, f32[1,8,16,256]{3,2,1,0:T(8,128)}, u32[]{:S(2)}) copy-start(f32[1,8,16,256]{3,2,1,0:T(8,128)} %qp.3) | copy-start | bytes 393220
  1.6 8.9 %collective-permute-start.1 = (f32[50,8,128]{2,1,0:T(8,128)S(1)}, f32[50,8,128]{2,1,0:T(8,128)S(1)}, u32[]{:S(2)}, u32[]{:S(2)}) collective-permute-start(f32[50,8,128]{2,1,0:T(8,128)S(1)} %get-tuple-element.20), channel_id=1, source_target_pairs={{0,1},{1,0},{2,3},{3,2},{4,5},{5,4},{6,7},{7,6},{8,9},{9,8},{10,11... | collective-permute-start | bytes 614408 | tf_op jit(solution)/shard_map/ppermute | solution.py:501
  2.2 8.4 %collective-permute-start.2 = (f32[50,8,128]{2,1,0:T(8,128)S(1)}, f32[50,8,128]{2,1,0:T(8,128)S(1)}, u32[]{:S(2)}, u32[]{:S(2)}) collective-permute-start(f32[50,8,128]{2,1,0:T(8,128)S(1)} %get-tuple-element.21), channel_id=1, source_target_pairs={{0,8},{1,2},{2,1},{3,4},{4,3},{5,6},{6,5},{7,15},{8,0},{9,10},{10,... | collective-permute-start | bytes 614408 | tf_op jit(solution)/shard_map/ppermute | solution.py:502
  4.7 1.2 %collective-permute-start = (f32[12,1,2,256]{3,2,1,0:T(2,128)S(1)}, f32[12,1,2,256]{3,2,1,0:T(2,128)S(1)}, u32[]{:S(2)}, u32[]{:S(2)}) collective-permute-start(f32[12,1,2,256]{3,2,1,0:T(2,128)S(1)} %copy-done.8), channel_id=1, source_target_pairs={{0,1},{1,0},{2,3},{3,2},{4,5},{5,4},{6,7},{7,6},{8,9},{9,8},{10,11... | collective-permute-start | bytes 73736 | tf_op jit(solution)/shard_map/ppermute | solution.py:503
  5.9 4.7 %copy-start.6 = (f32[1,16,256]{2,1,0:T(8,128)S(1)}, f32[1,16,256]{2,1,0:T(8,128)}, u32[]{:S(2)}) copy-start(f32[1,16,256]{2,1,0:T(8,128)} %speed.1) | copy-start | bytes 49156
  5.9 4.7 %copy-start.7 = (f32[1,8,4,8]{3,2,1,0:T(4,128)S(1)}, f32[1,8,4,8]{3,2,1,0:T(4,128)}, u32[]{:S(2)}) copy-start(f32[1,8,4,8]{3,2,1,0:T(4,128)} %obs.1) | copy-start | bytes 3076
  6.0 4.5 %copy-start.9 = (f32[1,8,4]{1,2,0:T(4,128)S(1)}, f32[1,8,4]{1,2,0:T(4,128)}, u32[]{:S(2)}) copy-start(f32[1,8,4]{1,2,0:T(4,128)} %param.20) | copy-start | bytes 388
  6.0 6.5 %collective-permute-start.3 = (f32[2,4,128]{2,1,0:T(4,128)S(1)}, f32[2,4,128]{2,1,0:T(4,128)S(1)}, u32[]{:S(2)}, u32[]{:S(2)}) collective-permute-start(f32[2,4,128]{2,1,0:T(4,128)S(1)} %get-tuple-element.27), channel_id=1, source_target_pairs={{0,2},{1,3},{2,0},{3,1},{4,6},{5,7},{6,4},{7,5},{8,10},{9,11},{10,... | collective-permute-start | bytes 12296 | tf_op jit(solution)/shard_map/ppermute | solution.py:514
  7.5 5.0 %collective-permute-start.4 = (f32[2,4,128]{2,1,0:T(4,128)S(1)}, f32[2,4,128]{2,1,0:T(4,128)S(1)}, u32[]{:S(2)}, u32[]{:S(2)}) collective-permute-start(f32[2,4,128]{2,1,0:T(4,128)S(1)} %get-tuple-element.28), channel_id=1, source_target_pairs={{0,4},{1,5},{2,6},{3,7},{4,0},{5,1},{6,2},{7,3},{8,12},{9,13},{10,... | collective-permute-start | bytes 12296 | tf_op jit(solution)/shard_map/ppermute | solution.py:514
  10.0 5.4 %collective-permute-start.5 = (f32[2,4,128]{2,1,0:T(4,128)S(1)}, f32[2,4,128]{2,1,0:T(4,128)S(1)}, u32[]{:S(2)}, u32[]{:S(2)}) collective-permute-start(f32[2,4,128]{2,1,0:T(4,128)S(1)} %get-tuple-element.29), channel_id=1, source_target_pairs={{0,6},{1,7},{2,4},{3,5},{4,2},{5,3},{6,0},{7,1},{8,14},{9,15},{10,... | collective-permute-start | bytes 12296 | tf_op jit(solution)/shard_map/ppermute | solution.py:514

commit v4 on v3

--- a/solution.py
+++ b/solution.py
@@ -31,25 +31,35 @@
 SMEM = pltpu.SMEM
 
 
+def partner_bits(i):
+    return 2 * i + 1 if i else 0
+
+
 def lane_iota():
     return lax.broadcasted_iota(jnp.int32, (8, LANES), 1)
 
 
-def choose_kernel(first, own, other, info_in, info, *picks, columns):
+def choose_kernel(first, own, pack_a, info_in, info, *picks, columns):
     info[...] = info_in[...]
     info[0] = jnp.full((8, LANES), first[0])
+    start = first[0]
     position = lax.axis_index("box")
     owners = 2 * len(picks)
     rounds = own.shape[0]
     for i, pick in enumerate(picks):
-        target = position ^ (2 * i)
-        low_tile = first[0] + (columns // 2) * target - 3
-        for core, tiles in enumerate((own, other)):
+        target = position ^ partner_bits(i)
+        low_tile = start + (columns // 2) * target - 3
+        for core in range(2):
             owner = position ^ core
             r0 = lax.div(low_tile - owner + 2 * owners - 1, owners) - 1
             for slot in range(2):
                 r = jnp.clip(r0 + slot, 0, rounds - 1)
-                pick[core, 2 * slot : 2 * slot + 2, :] = tiles[r, 0, :, 0:LANES]
+                if core == 0:
+                    tile = own[r, 0, :, 0:LANES]
+                else:
+                    row = pl.multiple_of(2 * lax.rem(r, 4), 2)
+                    tile = pack_a[PACK_TILES + lax.div(r, 4), pl.ds(row, 2), :]
+                pick[core, 2 * slot : 2 * slot + 2, :] = tile
 
 
 def pack_kernel(
@@ -63,11 +73,13 @@
     qp,
     speed_any,
     obs_any,
+    refl_any,
     pack_a,
     pack_b,
     info,
     sources,
     rec,
+    refl,
     wide,
     near,
     speed,
@@ -96,6 +108,7 @@
         moves.append(group)
     moves.append([(speed_any.at[0, edges[side], :], speed.at[side]) for side in range(2)])
     moves[-1].append((obs_any, obs))
+    moves.append([(refl_any, refl)])
     copies, i = [], 0
     for group in moves:
         copies.append([])
@@ -108,7 +121,8 @@
         for copy in copies[group]:
             copy.wait()
 
-    arrive(0)
+    for group in range(len(copies)):
+        arrive(group)
     own_cell = position * columns * depth
     info[0] = jnp.zeros((8, LANES), jnp.int32)
     cell = jnp.zeros((8, LANES), jnp.int32)
@@ -116,49 +130,78 @@
         cell = jnp.where(row == s, sources[0, s] - own_cell, cell)
     info[1] = cell
     count = rec.shape[1]
+    edge_receivers = (0, 1, count - 1, count - 2)
     for block in range(0, count, 8):
         cell = jnp.zeros((8, LANES), jnp.int32)
         for r in range(min(8, count - block)):
             cell = jnp.where(row == r, rec[0, block + r] - own_cell, cell)
         info[2 + block // 8] = cell
 
-    def put(tile, left, right):
-        pack_a[tile] = jnp.where(even, right, left)
-        pack_b[tile] = jnp.where(even, left, right)
-
-    arrived, tile = set(), 0
-    for name, half, width in HALO:
-        if name not in arrived:
-            arrive(1 + list(fields).index(name))
-            arrived.add(name)
-        part = slice(half * LANES, (half + 1) * LANES)
-        if name in nears:
-            low, high = (near[side, nears[name]] for side in range(2))
-        else:
-            low, high = (wide[side, wides[name], :, :, part] for side in range(2))
-        low, high = jnp.swapaxes(low, 0, 1), jnp.swapaxes(high, 0, 1)
-        for j in range(1, width + 1):
-            put(tile, low[j - 1], high[8 - j])
-            tile += 1
-    arrive(1 + len(fields))
-    for half in range(2):
-        part = slice(half * LANES, (half + 1) * LANES)
-        put(SPEED_TILE + half, speed[0, :, part], speed[1, :, part])
-
-    def meta(right):
+    def send(low_to, high_to):
+        def put(tile, low, high):
+            if low_to is not None:
+                low_to[tile] = low
+            if high_to is not None:
+                high_to[tile] = high
+
+        tile = 0
+        for name, half, width in HALO:
+            part = slice(half * LANES, (half + 1) * LANES)
+            if name in nears:
+                low, high = (near[side, nears[name]] for side in range(2))
+            else:
+                low, high = (wide[side, wides[name], :, :, part] for side in range(2))
+            low, high = jnp.swapaxes(low, 0, 1), jnp.swapaxes(high, 0, 1)
+            for j in range(1, width + 1):
+                put(tile, low[j - 1], high[8 - j])
+                tile += 1
+        for half in range(2):
+            part = slice(half * LANES, (half + 1) * LANES)
+            put(SPEED_TILE + half, speed[0, :, part], speed[1, :, part])
+        put(META_TILE, meta[0], meta[1])
+
+    recorded = []
+    for t in range(STEPS):
+        at = obs[0, :, t, :]
+        recorded.append([jnp.broadcast_to(at[:, r : r + 1], (8, LANES)) for r in edge_receivers])
+    meta = []
+    for side in range(2):
         out = jnp.zeros((8, LANES), jnp.float32)
         for k in range(2):
-            r = count - 1 - k if right else k
+            r = edge_receivers[2 * side + k]
             for t in range(STEPS):
-                value = jnp.broadcast_to(obs[0, :, t, r : r + 1], (8, LANES))
-                out = jnp.where(lane == 2 * t + k, value, out)
+                out = jnp.where(lane == 2 * t + k, recorded[t][2 * side + k], out)
             column = lax.div(rec[0, r], depth) - position * columns
-            distance = columns - column if right else column + 1
+            distance = columns - column if side else column + 1
             code = distance * depth + lax.rem(rec[0, r], depth)
             out = jnp.where(lane == 2 * STEPS + k, code.astype(jnp.float32), out)
-        return out
-
-    put(META_TILE, meta(False), meta(True))
+        meta.append(out)
+
+    is_end = jnp.logical_or(position == 0, position == lax.axis_size("box") - 1)
+
+    @pl.when(jnp.logical_and(even, jnp.logical_not(is_end)))
+    def _():
+        send(pack_b, pack_a)
+
+    @pl.when(jnp.logical_and(jnp.logical_not(even), jnp.logical_not(is_end)))
+    def _():
+        send(pack_a, pack_b)
+
+    @pl.when(is_end)
+    def _():
+        pack_b[...] = jnp.zeros_like(pack_b)
+
+    @pl.when(jnp.logical_and(even, is_end))
+    def _():
+        send(None, pack_a)
+
+    @pl.when(jnp.logical_and(jnp.logical_not(even), is_end))
+    def _():
+        send(pack_a, None)
+
+    for r in range(refl.shape[0]):
+        row = 2 * (r % 4)
+        pack_a[PACK_TILES + r // 4, row : row + 2, :] = refl[r, 0, :, 0:LANES]
 
 
 def depthwise(xs, first_lane, last_lane):
@@ -210,8 +253,12 @@
     b1,
     q0,
     q1,
+    q2,
+    q3,
+    q4,
     vel,
     late,
+    metas,
     *,
     owners,
     groups,
@@ -220,11 +267,8 @@
     tiles = columns // 2
     position = lax.axis_index("box")
     even = lax.rem(position, 2) == 0
-    has_left = position > 0
-    has_right = position < owners - 1
     lane = lane_iota()
     edges = lane == 0, lane == LANES - 1
-    zero = jnp.zeros((8, LANES), jnp.float32)
     halves = (slice(0, LANES), slice(LANES, 2 * LANES))
     scratch = {"un": u0, "up": u1, "bn": b0, "bp": b1, "qn": q0, "qp": q1}
     first = info[0, 0, 0]
@@ -239,34 +283,41 @@
             )
     for c in range(columns):
         vel[MARGIN + c] = jnp.broadcast_to(speed[0, c : c + 1, :], (8, depth))
-
-    def got(tile):
-        a, b = pack_a[tile], pack_b[tile]
-        left, right = jnp.where(even, b, a), jnp.where(even, a, b)
-        return jnp.where(has_left, left, 0.0), jnp.where(has_right, right, 0.0)
-
-    tile = 0
-    for name, half, count in HALO:
-        for j in range(1, count + 1):
-            left, right = got(tile)
-            scratch[name][MARGIN - j, :, halves[half]] = left
-            scratch[name][MARGIN + columns - 1 + j, :, halves[half]] = right
-            tile += 1
-    for half, count in ((0, 6), (1, 3)):
-        left, right = got(SPEED_TILE + half)
-        for j in range(1, count + 1):
-            vel[MARGIN - j, :, halves[half]] = jnp.broadcast_to(left[8 - j : 9 - j], (8, LANES))
-            vel[MARGIN + columns - 1 + j, :, halves[half]] = jnp.broadcast_to(
-                right[j - 1 : j], (8, LANES)
-            )
-    meta = got(META_TILE)
-    for c in range(-6, columns + 6):
         near_speed[MARGIN + c] = vel[MARGIN + c, :, halves[0]]
+
+    def receive(left, right):
+        tile = 0
+        for name, half, count in HALO:
+            for j in range(1, count + 1):
+                scratch[name][MARGIN - j, :, halves[half]] = left[tile]
+                scratch[name][MARGIN + columns - 1 + j, :, halves[half]] = right[tile]
+                tile += 1
+        for half, count in ((0, 6), (1, 3)):
+            for j in range(1, count + 1):
+                for e, v in (
+                    (MARGIN - j, left[SPEED_TILE + half, 8 - j : 9 - j, :]),
+                    (MARGIN + columns - 1 + j, right[SPEED_TILE + half, j - 1 : j, :]),
+                ):
+                    v = jnp.broadcast_to(v, (8, LANES))
+                    vel[e, :, halves[half]] = v
+                    if half == 0:
+                        near_speed[e] = v
+        metas[0] = left[META_TILE]
+        metas[1] = right[META_TILE]
+
+    @pl.when(even)
+    def _():
+        receive(pack_b, pack_a)
+
+    @pl.when(jnp.logical_not(even))
+    def _():
+        receive(pack_a, pack_b)
+
+    meta = metas[0], metas[1]
 
     cell = info[1] - lane
     pulses = [jnp.broadcast_to(wavelet[0, :, t : t + 1], (8, LANES)) for t in range(STEPS)]
     new_u, old_u = u0, u1
-    illum = [[zero, zero] for _ in range(columns)]
     for t in range(STEPS):
         wide, narrow = 6 - t, 3 - t
         for c in range(-wide, columns + wide):
@@ -280,27 +331,34 @@
                     acc[t, e] = a
                 elif 0 <= c < columns:
                     late[t, c] = a
-                old_u[e, :, halves[h]] = 2.0 * mid[h] - old_u[e, :, halves[h]] + a
-                if 0 <= c < columns:
-                    illum[c][h] = illum[c][h] + a * a
+                if t < STEPS - 1:
+                    old_u[e, :, halves[h]] = 2.0 * mid[h] - old_u[e, :, halves[h]] + a
         new_u, old_u = old_u, new_u
 
     reach = STEPS - 1
     recorded = {}
+    own_obs = [obs[0, :, t, :] for t in range(STEPS)]
     for c in range(-reach, columns + reach):
         if 0 <= c < columns:
             r = c // 2
             here = jnp.broadcast_to(info[2 + r // 8, r % 8 : r % 8 + 1, :], (8, LANES))
             hit = lane == here - c * depth
-            columns_of = [obs[0, :, t, r : r + 1] for t in range(STEPS)]
+            if c % 2 == 0:
+                pair = [jnp.broadcast_to(at[:, r : r + 1], (8, LANES)) for at in own_obs]
+            recorded[c] = pair
         else:
             j = -c if c < 0 else c - columns + 1
             side, k = meta[0] if c < 0 else meta[1], (j - 1) // 2
             code = jnp.broadcast_to(side[:, 2 * STEPS + k : 2 * STEPS + k + 1], (8, LANES))
             hit = code == (lane + j * depth).astype(jnp.float32)
-            columns_of = [side[:, 2 * t + k : 2 * t + k + 1] for t in range(STEPS)]
+            recorded[c] = [
+                jnp.broadcast_to(side[:, 2 * t + k : 2 * t + k + 1], (8, LANES))
+                for t in range(STEPS)
+            ]
         hit_out[reach + c] = jnp.where(hit, 1.0, 0.0)
-        recorded[c] = columns_of
+        for t in range(STEPS):
+            if -t <= c < columns + t:
+                ahead[t, reach + c] = recorded[c][t]
     new_b, old_b = b0, b1
     for t in range(STEPS):
         wide = 2 * reach - t
@@ -308,37 +366,43 @@
             e = MARGIN + c
             (mid,), (laps,) = lap(new_b, e, 1, edges)
             b = 2.0 * mid - old_b[e] + vel[e, :, halves[0]] * laps
-            old_b[e] = b
+            if t < STEPS - 1:
+                old_b[e] = b
             if -t <= c < columns + t:
-                value = jnp.broadcast_to(recorded[c][t], (8, LANES))
-                ahead[t, reach + c] = hit_out[reach + c] * (b - value)
+                ahead[t, reach + c] = hit_out[reach + c] * (b - ahead[t, reach + c])
         new_b, old_b = old_b, new_b
 
-    grad = [[zero, zero] for _ in range(columns)]
-    new_q, old_q = q0, q1
-    for t in reversed(range(STEPS)):
+    newer, older = q0, q1
+    for t, q_t in zip(reversed(range(STEPS)), (q2, q3, q4, q1)):
         for c in range(-t, columns + t):
             e = MARGIN + c
-            mid, laps = lap(new_q, e, 2, edges)
+            mid, laps = lap(newer, e, 2, edges)
             for h in range(2):
-                q = 2.0 * mid[h] - old_q[e, :, halves[h]] + vel[e, :, halves[h]] * laps[h]
-                old_q[e, :, halves[h]] = q
-                if 0 <= c < columns:
-                    a = late[t, c] if h else acc[t, e]
-                    grad[c][h] = grad[c][h] + q * a
-        new_q, old_q = old_q, new_q
+                q_t[e, :, halves[h]] = (
+                    2.0 * mid[h] - older[e, :, halves[h]] + vel[e, :, halves[h]] * laps[h]
+                )
+        newer, older = q_t, newer
+    adjoint = (q1, q4, q3, q2)
 
     start = jnp.full((1, LANES), first.astype(jnp.float32))
     for k in range(tiles):
         owner = lax.rem(first + tiles * position + k, owners)
-        i = 0
-        for sums in (grad, illum):
-            for h in range(2):
-                for w in range(2):
-                    total = jnp.sum(sums[2 * k + w][h], axis=0, keepdims=True)
-                    for group in range(groups):
-                        out[group * owners + owner, :, i * LANES : (i + 1) * LANES] = total
-                    i += 1
+        grads, illums = [], []
+        for h in range(2):
+            for w in range(2):
+                c = 2 * k + w
+                grad = illum = None
+                for t in range(STEPS):
+                    a = late[t, c] if h else acc[t, MARGIN + c]
+                    g = adjoint[t][MARGIN + c, :, halves[h]] * a
+                    grad = g if grad is None else grad + g
+                    illum = a * a if illum is None else illum + a * a
+                grads.append(grad)
+                illums.append(illum)
+        for i, total in enumerate(grads + illums):
+            total = jnp.sum(total, axis=0, keepdims=True)
+            for group in range(groups):
+                out[group * owners + owner, :, i * LANES : (i + 1) * LANES] = total
         for group in range(groups):
             out[group * owners + owner, :, 8 * LANES : 9 * LANES] = start
 
@@ -353,14 +417,13 @@
     owners,
     groups,
 ):
-    images, (_, out, b0, b1, q0, q1, img) = refs[: owners // 2], refs[owners // 2 :]
+    images, (_, out, b0, b1, q0, q1, q2, q3, img) = refs[: owners // 2], refs[owners // 2 :]
     reach = STEPS - 1
     columns = hit.shape[0] - 2 * reach
     tiles = columns // 2
     position = lax.axis_index("box")
     lane = lane_iota()
     edges = lane == 0, lane == LANES - 1
-    zero = jnp.zeros((8, LANES), jnp.float32)
     first = info[0, 0, 0]
 
     low_tile = first + tiles * position - 3 + owners
@@ -370,7 +433,8 @@
         part = slice(2 * (m // owners), 2 * (m // owners) + 2)
         pair = images[0][core, part, :]
         for i in range(1, owners // 2):
-            pair = jnp.where(chips == i, images[i][core, part, :], pair)
+            other = 1 - core if partner_bits(i) % 2 else core
+            pair = jnp.where(chips == i, images[i][other, part, :], pair)
         for w in range(2):
             img[MARGIN - 6 + 2 * m + w] = jnp.broadcast_to(pair[w : w + 1], (8, LANES))
 
@@ -395,27 +459,29 @@
             }
         )
 
-    grad = [zero] * columns
-    new_q, old_q = q0, q1
-    for t in reversed(range(STEPS)):
+    newer = older = None
+    for t, q_t in zip(reversed(range(STEPS)), (q0, q1, q2, q3)):
         for c in range(-t, columns + t):
             e = MARGIN + c
             q = misfits[t][c]
-            if t < STEPS - 1:
-                (mid,), (laps,) = lap(new_q, e, 1, edges)
+            if newer is not None:
+                (mid,), (laps,) = lap(newer, e, 1, edges)
                 q = q + 2.0 * mid + speed[e] * laps
-            if t < STEPS - 2:
-                q = q - old_q[e]
-            old_q[e] = q
-            if 0 <= c < columns:
-                grad[c] = grad[c] + q * acc[t, e]
-        new_q, old_q = old_q, new_q
+            if older is not None:
+                q = q - older[e]
+            q_t[e] = q
+        newer, older = q_t, newer
+    adjoint = (q3, q2, q1, q0)
 
     for k in range(tiles):
         owner = lax.rem(first + tiles * position + k, owners)
         for w in range(2):
+            e = MARGIN + 2 * k + w
             part = slice(w * LANES, (w + 1) * LANES)
-            total = out[owner, :, part] + jnp.sum(grad[2 * k + w], axis=0, keepdims=True)
+            grad = adjoint[0][e] * acc[0, e]
+            for t in range(1, STEPS):
+                grad = grad + adjoint[t][e] * acc[t, e]
+            total = out[owner, :, part] + jnp.sum(grad, axis=0, keepdims=True)
             for group in range(groups):
                 out[group * owners + owner, :, part] = total
 
@@ -467,26 +533,26 @@
     fields = (u_now, u_prev, born_now, born_prev, adj_last, adj_after)
 
     shape = jax.ShapeDtypeStruct
-    pack = VMEM((PACK_TILES, 8, LANES), f32)
     blocks = 2 + pl.cdiv(receivers.shape[1], 8)
-    pack_from = (sources, receivers, *fields, velocity, observed)
+    pack_from = (sources, receivers, *fields, velocity, observed, reflectivity)
     send_a, send_b, info = pl.pallas_call(
         pack_kernel,
         out_shape=(
-            pack,
-            pack,
+            VMEM((PACK_TILES + pl.cdiv(rounds, 4), 8, LANES), f32),
+            VMEM((PACK_TILES, 8, LANES), f32),
             VMEM((blocks, 8, LANES), jnp.int32),
         ),
-        in_specs=[anywhere] * 10,
+        in_specs=[anywhere] * 11,
         out_specs=(vmem,) * 3,
         scratch_shapes=[
             SMEM(sources.shape, jnp.int32),
             SMEM(receivers.shape, jnp.int32),
+            VMEM(reflectivity.shape, f32),
             VMEM((2, 4, 8, 8, depth), f32),
             VMEM((2, 2, 8, 8, LANES), f32),
             VMEM((2, 8, depth), f32),
             VMEM(observed.shape, f32),
-            pltpu.SemaphoreType.DMA((17,)),
+            pltpu.SemaphoreType.DMA((18,)),
         ],
         compiler_params=params_hbm,
         name="pack",
@@ -500,7 +566,6 @@
     ]
     got_a = lax.ppermute(send_a, "box", swap_a)
     got_b = lax.ppermute(send_b, ("shot", "box"), swap_b)
-    other_image = lax.ppermute(reflectivity, "box", swap_a)
     info, *picks = pl.pallas_call(
         functools.partial(choose_kernel, columns=columns),
         out_shape=(VMEM((blocks, 8, LANES), jnp.int32),)
@@ -509,11 +574,12 @@
         out_specs=(vmem,) * (1 + owners // 2),
         compiler_params=params,
         name="choose",
-    )(first_tile, reflectivity, other_image, info)
-    images = [picks[0]] + [
-        lax.ppermute(picks[i], "box", [(j, j ^ (2 * i)) for j in range(owners)])
-        for i in range(1, owners // 2)
-    ]
+    )(first_tile, reflectivity, got_a, info)
+    images = {0: picks[0]}
+    for i in reversed(range(1, owners // 2)):
+        pairs = [(j, j ^ partner_bits(i)) for j in range(owners)]
+        images[i] = lax.ppermute(picks[i], "box", pairs)
+    images = [images[i] for i in range(owners // 2)]
 
     ext = columns + 2 * MARGIN
     near = columns + 2 * (STEPS - 1)
@@ -531,8 +597,8 @@
         out_specs=(vmem,) * 5,
         scratch_shapes=[VMEM((ext, 8, depth), f32)] * 2
         + [VMEM((ext, 8, LANES), f32)] * 2
-        + [VMEM((ext, 8, depth), f32)] * 3
-        + [VMEM((STEPS, columns, 8, LANES), f32)],
+        + [VMEM((ext, 8, depth), f32)] * 6
+        + [VMEM((STEPS, columns, 8, LANES), f32), VMEM((2, 8, LANES), f32)],
         compiler_params=params,
         name="homogeneous",
     )(info, *fields, velocity, observed, wavelet, got_a, got_b)
@@ -541,7 +607,7 @@
         out_shape=payload,
         in_specs=[vmem] * (6 + len(images)),
         out_specs=vmem,
-        scratch_shapes=[VMEM((ext, 8, LANES), f32)] * 5,
+        scratch_shapes=[VMEM((ext, 8, LANES), f32)] * 7,
         input_output_aliases={5 + len(images): 0},
         compiler_params=params,
         name="scattered",

time: 27.5 us -> 26.3 us (0.956)
  waiting for transfers between devices: 3.24 us -> 2.28 us
  starting transfers between devices: 7.76 us -> 7.12 us
  blocking collectives: 10.6 us -> 11.2 us
    ppermute x4 -> x3, waiting for transfers between devices: 3.24 us -> 2.27 us  [on_device(): images[i] = lax.ppermute(picks[i], 'box', pairs)]
    ppermute x4 -> x3, starting transfers between devices: 4.65 us -> 4 us  [on_device(): images[i] = lax.ppermute(picks[i], 'box', pairs)]
    all_to_all x1, blocking collectives: 10.6 us -> 11.2 us  [on_device(): lax.all_to_all(out, ('shot', 'box'), split_axis=0, concat_axis=0, tiled=T...]
    pallas_call x1, Pallas kernels: 1.9 us -> 1.57 us  [on_device(): pl.pallas_call(functools.partial(homogeneous_kernel, owners=owners, group...]
  transfers between devices with their start and end apart: 6 -> 5, of which waited for: 2 -> 1; matrix products, arithmetic and copies ran while one was open for 0% -> 0% of each run, Pallas kernels for 7% -> 6%
where the time goes in v4:
time: 26.3 us; the launch traced here: 26.1 us
  blocking collectives  11.2 us (43%)
  starting transfers between devices  7.12 us (27%)
  Pallas kernels  4.59 us (17%)
  waiting for transfers between devices  2.28 us (9%)
  between operations  0.8 us (3%)
    all_to_all x1, blocking collectives, on_device(): lax.all_to_all(out, ('shot', 'box'), split_axis=0, concat_axis=0, tiled=T...  11.2 us
    ppermute x3, starting transfers between devices, on_device(): images[i] = lax.ppermute(picks[i], 'box', pairs)  4 us
    ppermute x1, starting transfers between devices, on_device(): got_b = lax.ppermute(send_b, ('shot', 'box'), swap_b)  2.54 us
    ppermute x3, waiting for transfers between devices, on_device(): images[i] = lax.ppermute(picks[i], 'box', pairs)  2.27 us
    pallas_call x1, Pallas kernels, on_device(): pl.pallas_call(pack_kernel, out_shape=(VMEM((PACK_TILES + pl.cdiv(rounds,...  1.64 us
    pallas_call x1, Pallas kernels, on_device(): pl.pallas_call(functools.partial(homogeneous_kernel, owners=owners, group...  1.57 us
    pallas_call x1, Pallas kernels, on_device(): pl.pallas_call(functools.partial(join_kernel, owners=owners, groups=group...  0.71 us
    pallas_call x1, Pallas kernels, on_device(): pl.pallas_call(functools.partial(scattered_kernel, owners=owners, groups=...  0.6 us
  transfers between devices with their start and end apart: 5, of which 1 were waited for; matrix products, arithmetic and copies ran while one was open for 0% of the time, Pallas kernels for 6%

profile of v4, /device:TPU:0, one launch (start us, length us, event | category | flops | bytes accessed | tf_op | source)
XLA Modules:
  0.0 26.1 jit_solution(13570291096591275544)
XLA Ops:
  0.0 0.0 copy-start.6
  0.0 0.0 copy-start.2
  0.0 0.0 copy-start.3
  0.0 0.0 copy-start.4
  0.0 0.0 copy-start.5
  0.0 0.0 copy-start.7
  0.0 0.0 copy-start.8
  0.0 1.6 %pack.1 = (f32[53,8,128]{2,1,0:T(8,128)S(1)}, f32[50,8,128]{2,1,0:T(8,128)S(1)}, s32[3,8,128]{2,1,0:T(8,128)S(1)}) custom-call(s32[1,8]{1,0:T(1,128)} %sources_any.1, s32[1,8]{1,0:T(1,128)} %rec_any.1, f32[1,8,16,256]{3,2,1,0:T(8,128)} %un.3, f32[1,8,16,256]{3,2,1,0:T(8,128)} %up.3, f32[1,8,16,256]{3,2,1,0:T(8,128)} %bn.3, f32[1,8,16,256]{3,2,1,0:T(8,128)} %bp.3, ...), custom_call_target="tpu_custom_call" | custom-call | tf_op jit(solution)/shard_map/pack/pallas_call | solution.py:538
  1.7 0.6 %collective-permute-start = (f32[53,8,128]{2,1,0:T(8,128)S(1)}, f32[53,8,128]{2,1,0:T(8,128)S(1)}, u32[]{:S(2)}, u32[]{:S(2)}) collective-permute-start(f32[53,8,128]{2,1,0:T(8,128)S(1)} %get-tuple-element.18), channel_id=1, source_target_pairs={{0,1},{1,0},{2,3},{3,2},{4,5},{5,4},{6,7},{7,6},{8,9},{9,8},{10,11... | collective-permute-start | bytes 651272 | tf_op jit(solution)/shard_map/ppermute | solution.py:567
  2.3 2.5 %collective-permute-start.1 = (f32[50,8,128]{2,1,0:T(8,128)S(1)}, f32[50,8,128]{2,1,0:T(8,128)S(1)}, u32[]{:S(2)}, u32[]{:S(2)}) collective-permute-start(f32[50,8,128]{2,1,0:T(8,128)S(1)} %get-tuple-element.21), channel_id=1, source_target_pairs={{0,8},{1,2},{2,1},{3,4},{4,3},{5,6},{6,5},{7,15},{8,0},{9,10},{10,... | collective-permute-start | bytes 614408 | tf_op jit(solution)/shard_map/ppermute | solution.py:568
  5.4 0.0 collective-permute-done.pack_a
  5.5 0.0 copy-start.9
  5.5 0.0 copy-done.6
  5.5 0.0 copy-start
  5.5 0.0 copy-start.1
  5.5 0.1 choose.1
  5.6 1.5 %collective-permute-start.2 = (f32[2,4,128]{2,1,0:T(4,128)S(1)}, f32[2,4,128]{2,1,0:T(4,128)S(1)}, u32[]{:S(2)}, u32[]{:S(2)}) collective-permute-start(f32[2,4,128]{2,1,0:T(4,128)S(1)} %get-tuple-element.27), channel_id=1, source_target_pairs={{0,3},{1,2},{2,1},{3,0},{4,7},{5,6},{6,5},{7,4},{8,11},{9,10},{10,... | collective-permute-start | bytes 12296 | tf_op jit(solution)/shard_map/ppermute | solution.py:581
  7.1 1.7 %collective-permute-start.3 = (f32[2,4,128]{2,1,0:T(4,128)S(1)}, f32[2,4,128]{2,1,0:T(4,128)S(1)}, u32[]{:S(2)}, u32[]{:S(2)}) collective-permute-start(f32[2,4,128]{2,1,0:T(4,128)S(1)} %get-tuple-element.28), channel_id=1, source_target_pairs={{0,5},{1,4},{2,7},{3,6},{4,1},{5,0},{6,3},{7,2},{8,13},{9,12},{10,... | collective-permute-start | bytes 12296 | tf_op jit(solution)/shard_map/ppermute | solution.py:581
  8.8 0.8 %collective-permute-start.4 = (f32[2,4,128]{2,1,0:T(4,128)S(1)}, f32[2,4,128]{2,1,0:T(4,128)S(1)}, u32[]{:S(2)}, u32[]{:S(2)}) collective-permute-start(f32[2,4,128]{2,1,0:T(4,128)S(1)} %get-tuple-element.29), channel_id=1, source_target_pairs={{0,7},{1,6},{2,5},{3,4},{4,3},{5,2},{6,1},{7,0},{8,15},{9,14},{10,... | collective-permute-start | bytes 12296 | tf_op jit(solution)/shard_map/ppermute | solution.py:581
  9.6 0.0 copy-done.9
  9.6 0.1 copy.15.wavelet
  9.7 0.0 collective-permute-done.1.pack_b
  9.7 0.0 copy-done.2
  9.7 0.0 copy-done.3
  9.7 0.0 copy-done.4
  9.7 0.0 copy-done.5
  9.7 0.0 copy-done.7
  9.7 0.0 copy-done.8
  9.7 0.0 copy-done
  9.7 0.0 copy-done.1
  9.7 1.6 %homogeneous.1 = (f32[4,32,8,128]{3,2,1,0:T(8,128)S(1)}, f32[32,8,128]{2,1,0:T(8,128)S(1)}, f32[22,8,128]{2,1,0:T(8,128)S(1)}, f32[4,22,8,128]{3,2,1,0:T(8,128)S(1)}, f32[32,1,1152]{2,1,0:T(1,128)S(1)}) custom-call(s32[3,8,128]{2,1,0:T(8,128)S(1)} %get-tuple-element.20.info, f32[1,8,16,256]{3,2,1,0:T(8,128)S(1)} %copy-done, f32[1,8,16,256]{3,2,1,0:T(8,128)S(1)} %copy-done.1, ...), custom_call_target="tpu_custom_call" | custom-call | tf_op jit(solution)/shard_map/homogeneous/pallas_call | solution.py:587
  11.3 0.0 collective-permute-done.2.refs_1_
  11.3 0.0 collective-permute-done.3.refs_2_
  11.3 2.3 %collective-permute-done.4.refs_3_ = f32[2,4,128]{2,1,0:T(4,128)S(1)} collective-permute-done((f32[2,4,128]{2,1,0:T(4,128)S(1)}, f32[2,4,128]{2,1,0:T(4,128)S(1)}, u32[]{:S(2)}, u32[]{:S(2)}) %collective-permute-start.4) | collective-permute-done | bytes 4128 | tf_op jit(solution)/shard_map/ppermute | solution.py:581
  13.6 0.6 %scattered.1 = f32[32,1,1152]{2,1,0:T(1,128)S(1)} custom-call(s32[3,8,128]{2,1,0:T(8,128)S(1)} %get-tuple-element.20.info, f32[4,32,8,128]{3,2,1,0:T(8,128)S(1)} %get-tuple-element.22.acc, f32[32,8,128]{2,1,0:T(8,128)S(1)} %get-tuple-element.23.speed, f32[22,8,128]{2,1,0:T(8,128)S(1)} %get-tuple-element.24.hit, ...), custom_call_target="tpu_custom_call", output_to_operand_aliasing={{}: (9, {})} | custom-call | tf_op jit(solution)/shard_map/scattered/pallas_call | solution.py:605
  14.2 11.2 %all_to_all.5.received = f32[32,1,1152]{2,1,0:T(1,128)S(1)} all-to-all(f32[32,1,1152]{2,1,0:T(1,128)S(1)} %scattered.1), channel_id=1, replica_groups=mesh['shot'=4,'box'=8] {'shot','box'}, dimensions={0} | all-to-all | bytes 294912 | tf_op jit(solution)/shard_map/all_to_all | solution.py:616
  25.4 0.7 %join.1 = f32[12,1,2,256]{3,2,1,0:T(2,128)} custom-call(f32[32,1,1152]{2,1,0:T(1,128)S(1)} %all_to_all.5.received), custom_call_target="tpu_custom_call" | custom-call | tf_op jit(solution)/shard_map/join/pallas_call | solution.py:617
Async XLA Ops:
  0.0 5.5 %copy-start.6 = (f32[12,1,2,256]{3,2,1,0:T(2,128)S(1)}, f32[12,1,2,256]{3,2,1,0:T(2,128)}, u32[]{:S(2)}) copy-start(f32[12,1,2,256]{3,2,1,0:T(2,128)} %own.1) | copy-start | bytes 73732
  0.0 9.7 %copy-start.2 = (f32[1,8,16,256]{3,2,1,0:T(8,128)S(1)}, f32[1,8,16,256]{3,2,1,0:T(8,128)}, u32[]{:S(2)}) copy-start(f32[1,8,16,256]{3,2,1,0:T(8,128)} %bn.3) | copy-start | bytes 393220
  0.0 9.7 %copy-start.3 = (f32[1,8,16,256]{3,2,1,0:T(8,128)S(1)}, f32[1,8,16,256]{3,2,1,0:T(8,128)}, u32[]{:S(2)}) copy-start(f32[1,8,16,256]{3,2,1,0:T(8,128)} %bp.3) | copy-start | bytes 393220
  0.0 9.7 %copy-start.4 = (f32[1,8,16,256]{3,2,1,0:T(8,128)S(1)}, f32[1,8,16,256]{3,2,1,0:T(8,128)}, u32[]{:S(2)}) copy-start(f32[1,8,16,256]{3,2,1,0:T(8,128)} %qn.3) | copy-start | bytes 393220
  0.0 9.7 %copy-start.5 = (f32[1,8,16,256]{3,2,1,0:T(8,128)S(1)}, f32[1,8,16,256]{3,2,1,0:T(8,128)}, u32[]{:S(2)}) copy-start(f32[1,8,16,256]{3,2,1,0:T(8,128)} %qp.3) | copy-start | bytes 393220
  0.0 9.7 %copy-start.7 = (f32[1,16,256]{2,1,0:T(8,128)S(1)}, f32[1,16,256]{2,1,0:T(8,128)}, u32[]{:S(2)}) copy-start(f32[1,16,256]{2,1,0:T(8,128)} %speed.1) | copy-start | bytes 49156
  0.0 9.7 %copy-start.8 = (f32[1,8,4,8]{3,2,1,0:T(4,128)S(1)}, f32[1,8,4,8]{3,2,1,0:T(4,128)}, u32[]{:S(2)}) copy-start(f32[1,8,4,8]{3,2,1,0:T(4,128)} %obs.1) | copy-start | bytes 3076
  1.7 3.8 %collective-permute-start = (f32[53,8,128]{2,1,0:T(8,128)S(1)}, f32[53,8,128]{2,1,0:T(8,128)S(1)}, u32[]{:S(2)}, u32[]{:S(2)}) collective-permute-start(f32[53,8,128]{2,1,0:T(8,128)S(1)} %get-tuple-element.18), channel_id=1, source_target_pairs={{0,1},{1,0},{2,3},{3,2},{4,5},{5,4},{6,7},{7,6},{8,9},{9,8},{10,11... | collective-permute-start | bytes 651272 | tf_op jit(solution)/shard_map/ppermute | solution.py:567
  2.3 7.4 %collective-permute-start.1 = (f32[50,8,128]{2,1,0:T(8,128)S(1)}, f32[50,8,128]{2,1,0:T(8,128)S(1)}, u32[]{:S(2)}, u32[]{:S(2)}) collective-permute-start(f32[50,8,128]{2,1,0:T(8,128)S(1)} %get-tuple-element.21), channel_id=1, source_target_pairs={{0,8},{1,2},{2,1},{3,4},{4,3},{5,6},{6,5},{7,15},{8,0},{9,10},{10,... | collective-permute-start | bytes 614408 | tf_op jit(solution)/shard_map/ppermute | solution.py:568
  5.5 4.1 %copy-start.9 = (f32[1,8,4]{1,2,0:T(4,128)S(1)}, f32[1,8,4]{1,2,0:T(4,128)}, u32[]{:S(2)}) copy-start(f32[1,8,4]{1,2,0:T(4,128)} %param.20) | copy-start | bytes 388
  5.5 4.2 %copy-start = (f32[1,8,16,256]{3,2,1,0:T(8,128)S(1)}, f32[1,8,16,256]{3,2,1,0:T(8,128)}, u32[]{:S(2)}) copy-start(f32[1,8,16,256]{3,2,1,0:T(8,128)} %un.3) | copy-start | bytes 393220
  5.5 4.2 %copy-start.1 = (f32[1,8,16,256]{3,2,1,0:T(8,128)S(1)}, f32[1,8,16,256]{3,2,1,0:T(8,128)}, u32[]{:S(2)}) copy-start(f32[1,8,16,256]{3,2,1,0:T(8,128)} %up.3) | copy-start | bytes 393220
  5.6 5.7 %collective-permute-start.2 = (f32[2,4,128]{2,1,0:T(4,128)S(1)}, f32[2,4,128]{2,1,0:T(4,128)S(1)}, u32[]{:S(2)}, u32[]{:S(2)}) collective-permute-start(f32[2,4,128]{2,1,0:T(4,128)S(1)} %get-tuple-element.27), channel_id=1, source_target_pairs={{0,3},{1,2},{2,1},{3,0},{4,7},{5,6},{6,5},{7,4},{8,11},{9,10},{10,... | collective-permute-start | bytes 12296 | tf_op jit(solution)/shard_map/ppermute | solution.py:581
  7.1 4.3 %collective-permute-start.3 = (f32[2,4,128]{2,1,0:T(4,128)S(1)}, f32[2,4,128]{2,1,0:T(4,128)S(1)}, u32[]{:S(2)}, u32[]{:S(2)}) collective-permute-start(f32[2,4,128]{2,1,0:T(4,128)S(1)} %get-tuple-element.28), channel_id=1, source_target_pairs={{0,5},{1,4},{2,7},{3,6},{4,1},{5,0},{6,3},{7,2},{8,13},{9,12},{10,... | collective-permute-start | bytes 12296 | tf_op jit(solution)/shard_map/ppermute | solution.py:581
  8.8 4.8 %collective-permute-start.4 = (f32[2,4,128]{2,1,0:T(4,128)S(1)}, f32[2,4,128]{2,1,0:T(4,128)S(1)}, u32[]{:S(2)}, u32[]{:S(2)}) collective-permute-start(f32[2,4,128]{2,1,0:T(4,128)S(1)} %get-tuple-element.29), channel_id=1, source_target_pairs={{0,7},{1,6},{2,5},{3,4},{4,3},{5,2},{6,1},{7,0},{8,15},{9,14},{10,... | collective-permute-start | bytes 12296 | tf_op jit(solution)/shard_map/ppermute | solution.py:581

commit v5 on v4

--- a/solution.py
+++ b/solution.py
@@ -12,10 +12,8 @@
 MARGIN = 8
 STEPS = 4
 HALO = (
-    ("un", 0, 7),
-    ("up", 0, 6),
-    ("bn", 0, 7),
-    ("bp", 0, 6),
+    ("un", 0, 4),
+    ("up", 0, 3),
     ("un", 1, 4),
     ("up", 1, 3),
     ("qn", 0, 4),
@@ -23,7 +21,17 @@
     ("qp", 0, 3),
     ("qp", 1, 3),
 )
-HALO_TILES = sum(count for _, _, count in HALO)
+NEAR = (
+    *(("bn", j, j < 7) for j in range(1, 8)),
+    *(("bp", j, j < 6) for j in range(1, 7)),
+    *(("un", j, j < 7) for j in range(5, 8)),
+    *(("up", j, j < 6) for j in range(4, 7)),
+)
+HALF = LANES // 2
+MORE = 4
+MORE_OF = [column for column in NEAR if column[2]]
+NEAR_TILE = sum(count for _, _, count in HALO)
+HALO_TILES = NEAR_TILE + (len(NEAR) + 1) // 2
 SPEED_TILE = HALO_TILES
 META_TILE = HALO_TILES + 2
 PACK_TILES = HALO_TILES + 3
@@ -65,25 +73,29 @@
 def pack_kernel(
     sources_any,
     rec_any,
+    un_any,
+    up_any,
+    bn_any,
+    bp_any,
+    qn_any,
+    qp_any,
+    speed_any,
+    obs_any,
+    refl_any,
+    pack_a,
+    pack_b,
+    info,
     un,
     up,
     bn,
     bp,
     qn,
     qp,
-    speed_any,
-    obs_any,
-    refl_any,
-    pack_a,
-    pack_b,
-    info,
+    speed,
+    obs,
+    refl,
     sources,
     rec,
-    refl,
-    wide,
-    near,
-    speed,
-    obs,
     sems,
 ):
     columns, depth = un.shape[2], un.shape[3]
@@ -91,38 +103,27 @@
     even = lax.rem(position, 2) == 0
     lane = lane_iota()
     row = lax.broadcasted_iota(jnp.int32, (8, LANES), 0)
-    edges = (pl.ds(0, 8), pl.ds(columns - 8, 8))
-    wides = {"un": 0, "up": 1, "qn": 2, "qp": 3}
-    nears = {"bn": 0, "bp": 1}
     fields = {"un": un, "up": up, "bn": bn, "bp": bp, "qn": qn, "qp": qp}
 
-    moves = [[(sources_any, sources), (rec_any, rec)]]
-    for name, ref in fields.items():
-        group = []
-        for side in range(2):
-            if name in wides:
-                group.append((ref.at[0, :, edges[side], :], wide.at[side, wides[name]]))
-            else:
-                source = ref.at[0, :, edges[side], pl.ds(0, LANES)]
-                group.append((source, near.at[side, nears[name]]))
-        moves.append(group)
-    moves.append([(speed_any.at[0, edges[side], :], speed.at[side]) for side in range(2)])
-    moves[-1].append((obs_any, obs))
-    moves.append([(refl_any, refl)])
-    copies, i = [], 0
-    for group in moves:
-        copies.append([])
-        for move in group:
-            copies[-1].append(pltpu.make_async_copy(*move, sems.at[i]))
-            copies[-1][-1].start()
-            i += 1
-
-    def arrive(group):
-        for copy in copies[group]:
-            copy.wait()
-
-    for group in range(len(copies)):
-        arrive(group)
+    small = ((sources_any, sources), (rec_any, rec), (obs_any, obs), (refl_any, refl))
+    near = (slice(None),) * 3 + (pl.ds(0, LANES),)
+    large = (
+        (un_any, un),
+        (up_any, up),
+        (bn_any.at[near], bn),
+        (bp_any.at[near], bp),
+        (qn_any, qn),
+        (qp_any, qp),
+        (speed_any, speed),
+    )
+    copies = [
+        pltpu.make_async_copy(*move, sems.at[i]) for i, move in enumerate(small + large)
+    ]
+    for copy in copies:
+        copy.start()
+    for copy in copies[: len(small)]:
+        copy.wait()
+
     own_cell = position * columns * depth
     info[0] = jnp.zeros((8, LANES), jnp.int32)
     cell = jnp.zeros((8, LANES), jnp.int32)
@@ -136,29 +137,6 @@
         for r in range(min(8, count - block)):
             cell = jnp.where(row == r, rec[0, block + r] - own_cell, cell)
         info[2 + block // 8] = cell
-
-    def send(low_to, high_to):
-        def put(tile, low, high):
-            if low_to is not None:
-                low_to[tile] = low
-            if high_to is not None:
-                high_to[tile] = high
-
-        tile = 0
-        for name, half, width in HALO:
-            part = slice(half * LANES, (half + 1) * LANES)
-            if name in nears:
-                low, high = (near[side, nears[name]] for side in range(2))
-            else:
-                low, high = (wide[side, wides[name], :, :, part] for side in range(2))
-            low, high = jnp.swapaxes(low, 0, 1), jnp.swapaxes(high, 0, 1)
-            for j in range(1, width + 1):
-                put(tile, low[j - 1], high[8 - j])
-                tile += 1
-        for half in range(2):
-            part = slice(half * LANES, (half + 1) * LANES)
-            put(SPEED_TILE + half, speed[0, :, part], speed[1, :, part])
-        put(META_TILE, meta[0], meta[1])
 
     recorded = []
     for t in range(STEPS):
@@ -177,6 +155,47 @@
             out = jnp.where(lane == 2 * STEPS + k, code.astype(jnp.float32), out)
         meta.append(out)
 
+    for r in range(refl.shape[0]):
+        at = 2 * (r % 4)
+        pack_a[PACK_TILES + r // 4, at : at + 2, :] = refl[r, 0, :, 0:LANES]
+    for copy in copies[len(small) :]:
+        copy.wait()
+
+    def send(low_to, high_to):
+        for side, to in ((0, low_to), (1, high_to)):
+            if to is None:
+                continue
+            edge = slice(columns - 8, columns) if side else slice(0, 8)
+            got = {}
+
+            def column(name, half, j):
+                if (name, half) not in got:
+                    part = slice(half * LANES, (half + 1) * LANES)
+                    got[name, half] = jnp.swapaxes(fields[name][0, :, edge, part], 0, 1)
+                return got[name, half][8 - j if side else j - 1]
+
+            tile = 0
+            for name, half, width in HALO:
+                for j in range(1, width + 1):
+                    to[tile] = column(name, half, j)
+                    tile += 1
+            for i in range(0, len(NEAR), 2):
+                out = column(NEAR[i][0], 0, NEAR[i][1])
+                if i + 1 < len(NEAR):
+                    other = column(NEAR[i + 1][0], 0, NEAR[i + 1][1])
+                    out = jnp.where(lane < HALF, out, pltpu.roll(other, HALF, 1))
+                else:
+                    for k, (name, j, _) in enumerate(MORE_OF):
+                        more = column(name, 0, j)
+                        if k:
+                            more = pltpu.roll(more, MORE * k, 1)
+                        out = jnp.where(lane < HALF + MORE * k, out, more)
+                to[tile] = out
+                tile += 1
+            for half in range(2):
+                to[SPEED_TILE + half] = speed[0, edge, half * LANES : (half + 1) * LANES]
+            to[META_TILE] = meta[side]
+
     is_end = jnp.logical_or(position == 0, position == lax.axis_size("box") - 1)
 
     @pl.when(jnp.logical_and(even, jnp.logical_not(is_end)))
@@ -198,10 +217,6 @@
     @pl.when(jnp.logical_and(jnp.logical_not(even), is_end))
     def _():
         send(pack_a, None)
-
-    for r in range(refl.shape[0]):
-        row = 2 * (r % 4)
-        pack_a[PACK_TILES + r // 4, row : row + 2, :] = refl[r, 0, :, 0:LANES]
 
 
 def depthwise(xs, first_lane, last_lane):
@@ -279,19 +294,34 @@
     for name, ref in (("bn", bn), ("bp", bp)):
         for c in range(0, columns, 8):
             scratch[name][MARGIN + c : MARGIN + c + 8] = jnp.swapaxes(
-                ref[0, :, c : c + 8, 0:LANES], 0, 1
+                ref[0, :, c : c + 8, :], 0, 1
             )
     for c in range(columns):
         vel[MARGIN + c] = jnp.broadcast_to(speed[0, c : c + 1, :], (8, depth))
         near_speed[MARGIN + c] = vel[MARGIN + c, :, halves[0]]
 
     def receive(left, right):
-        tile = 0
-        for name, half, count in HALO:
-            for j in range(1, count + 1):
-                scratch[name][MARGIN - j, :, halves[half]] = left[tile]
-                scratch[name][MARGIN + columns - 1 + j, :, halves[half]] = right[tile]
-                tile += 1
+        for side, pack in ((0, left), (1, right)):
+
+            def place(j):
+                return MARGIN + columns - 1 + j if side else MARGIN - j
+
+            tile = 0
+            for name, half, count in HALO:
+                for j in range(1, count + 1):
+                    scratch[name][place(j), :, halves[half]] = pack[tile]
+                    tile += 1
+            more = pack[NEAR_TILE + len(NEAR) // 2]
+            for i, column in enumerate(NEAR):
+                name, j, needs_more = column
+                value = pack[NEAR_TILE + i // 2]
+                if i % 2:
+                    value = pltpu.roll(value, HALF, 1)
+                if needs_more:
+                    k = MORE_OF.index(column)
+                    rest = pltpu.roll(more, LANES - MORE * k, 1) if k else more
+                    value = jnp.where(lane < HALF, value, rest)
+                scratch[name][place(j), :, halves[0]] = value
         for half, count in ((0, 6), (1, 3)):
             for j in range(1, count + 1):
                 for e, v in (
@@ -417,7 +447,8 @@
     owners,
     groups,
 ):
-    images, (_, out, b0, b1, q0, q1, q2, q3, img) = refs[: owners // 2], refs[owners // 2 :]
+    images = refs[: owners // 2][::-1]
+    _, out, b0, b1, q0, q1, q2, q3, img = refs[owners // 2 :]
     reach = STEPS - 1
     columns = hit.shape[0] - 2 * reach
     tiles = columns // 2
@@ -535,28 +566,29 @@
     shape = jax.ShapeDtypeStruct
     blocks = 2 + pl.cdiv(receivers.shape[1], 8)
     pack_from = (sources, receivers, *fields, velocity, observed, reflectivity)
-    send_a, send_b, info = pl.pallas_call(
+    near_field = (*u_now.shape[:-1], LANES)
+    kept = [near_field if i in (2, 3) else u_now.shape for i in range(6)]
+    kept += [velocity.shape, observed.shape, reflectivity.shape]
+    send_a, send_b, info, *kept = pl.pallas_call(
         pack_kernel,
         out_shape=(
             VMEM((PACK_TILES + pl.cdiv(rounds, 4), 8, LANES), f32),
             VMEM((PACK_TILES, 8, LANES), f32),
             VMEM((blocks, 8, LANES), jnp.int32),
+            *(VMEM(dims, f32) for dims in kept),
         ),
         in_specs=[anywhere] * 11,
-        out_specs=(vmem,) * 3,
+        out_specs=(vmem,) * 12,
         scratch_shapes=[
             SMEM(sources.shape, jnp.int32),
             SMEM(receivers.shape, jnp.int32),
-            VMEM(reflectivity.shape, f32),
-            VMEM((2, 4, 8, 8, depth), f32),
-            VMEM((2, 2, 8, 8, LANES), f32),
-            VMEM((2, 8, depth), f32),
-            VMEM(observed.shape, f32),
-            pltpu.SemaphoreType.DMA((18,)),
+            pltpu.SemaphoreType.DMA((11,)),
         ],
         compiler_params=params_hbm,
         name="pack",
     )(*(pltpu.with_memory_space_constraint(x, pltpu.HBM) for x in pack_from))
+    *kept, own_tiles = kept
+
     ends = (0, owners - 1)
     swap_a = [(i, i ^ 1) for i in range(owners)]
     swap_b = [
@@ -574,12 +606,12 @@
         out_specs=(vmem,) * (1 + owners // 2),
         compiler_params=params,
         name="choose",
-    )(first_tile, reflectivity, got_a, info)
+    )(first_tile, own_tiles, got_a, info)
     images = {0: picks[0]}
     for i in reversed(range(1, owners // 2)):
         pairs = [(j, j ^ partner_bits(i)) for j in range(owners)]
         images[i] = lax.ppermute(picks[i], "box", pairs)
-    images = [images[i] for i in range(owners // 2)]
+    images = [images[i] for i in reversed(range(owners // 2))]
 
     ext = columns + 2 * MARGIN
     near = columns + 2 * (STEPS - 1)
@@ -601,7 +633,7 @@
         + [VMEM((STEPS, columns, 8, LANES), f32), VMEM((2, 8, LANES), f32)],
         compiler_params=params,
         name="homogeneous",
-    )(info, *fields, velocity, observed, wavelet, got_a, got_b)
+    )(info, *kept, wavelet, got_a, got_b)
     out = pl.pallas_call(
         functools.partial(scattered_kernel, owners=owners, groups=groups),
         out_shape=payload,

time: 26.3 us -> 25.6 us (0.973)
  waiting for transfers between devices: 2.28 us -> 1.63 us
  blocking collectives: 11.2 us -> 11.5 us
    ppermute x3, waiting for transfers between devices: 2.27 us -> 1.62 us  [on_device(): images[i] = lax.ppermute(picks[i], 'box', pairs)]
    all_to_all x1, blocking collectives: 11.2 us -> 11.5 us  [on_device(): lax.all_to_all(out, ('shot', 'box'), split_axis=0, concat_axis=0, tiled=T...]
  transfers between devices with their start and end apart: 5 -> 5, of which waited for: 1 -> 1; matrix products, arithmetic and copies ran while one was open for 0% -> 0% of each run, Pallas kernels for 6% -> 7%
where the time goes in v5:
time: 25.6 us; the launch traced here: 25.5 us
  blocking collectives  11.5 us (45%)
  starting transfers between devices  7.07 us (28%)
  Pallas kernels  4.47 us (17%)
  waiting for transfers between devices  1.63 us (6%)
  between operations  0.71 us (3%)
    all_to_all x1, blocking collectives, on_device(): lax.all_to_all(out, ('shot', 'box'), split_axis=0, concat_axis=0, tiled=T...  11.5 us
    ppermute x3, starting transfers between devices, on_device(): images[i] = lax.ppermute(picks[i], 'box', pairs)  3.99 us
    ppermute x1, starting transfers between devices, on_device(): got_b = lax.ppermute(send_b, ('shot', 'box'), swap_b)  2.56 us
    pallas_call x1, Pallas kernels, on_device(): pl.pallas_call(functools.partial(homogeneous_kernel, owners=owners, group...  1.66 us
    ppermute x3, waiting for transfers between devices, on_device(): images[i] = lax.ppermute(picks[i], 'box', pairs)  1.62 us
    pallas_call x1, Pallas kernels, on_device(): pl.pallas_call(pack_kernel, out_shape=(VMEM((PACK_TILES + pl.cdiv(rounds,...  1.43 us
    pallas_call x1, Pallas kernels, on_device(): pl.pallas_call(functools.partial(join_kernel, owners=owners, groups=group...  0.71 us
    pallas_call x1, Pallas kernels, on_device(): pl.pallas_call(functools.partial(scattered_kernel, owners=owners, groups=...  0.6 us
  transfers between devices with their start and end apart: 5, of which 1 were waited for; matrix products, arithmetic and copies ran while one was open for 0% of the time, Pallas kernels for 7%

profile of v5, /device:TPU:0, one launch (start us, length us, event | category | flops | bytes accessed | tf_op | source)
XLA Modules:
  0.0 25.5 jit_solution(1482420143798764154)
XLA Ops:
  0.0 1.4 %pack.1 = (f32[44,8,128]{2,1,0:T(8,128)S(1)}, f32[41,8,128]{2,1,0:T(8,128)S(1)}, s32[3,8,128]{2,1,0:T(8,128)S(1)}, f32[1,8,16,256]{3,2,1,0:T(8,128)S(1)}, f32[1,...) custom-call(s32[1,8]{1,0:T(1,128)} %sources_any.1, ...), custom_call_target="tpu_custom_call" | custom-call | tf_op jit(solution)/shard_map/pack/pallas_call | solution.py:572
  1.4 0.5 %collective-permute-start = (f32[44,8,128]{2,1,0:T(8,128)S(1)}, f32[44,8,128]{2,1,0:T(8,128)S(1)}, u32[]{:S(2)}, u32[]{:S(2)}) collective-permute-start(f32[44,8,128]{2,1,0:T(8,128)S(1)} %get-tuple-element.28), channel_id=1, source_target_pairs={{0,1},{1,0},{2,3},{3,2},{4,5},{5,4},{6,7},{7,6},{8,9},{9,8},{10,11... | collective-permute-start | bytes 540680 | tf_op jit(solution)/shard_map/ppermute | solution.py:599
  2.0 2.6 %collective-permute-start.1 = (f32[41,8,128]{2,1,0:T(8,128)S(1)}, f32[41,8,128]{2,1,0:T(8,128)S(1)}, u32[]{:S(2)}, u32[]{:S(2)}) collective-permute-start(f32[41,8,128]{2,1,0:T(8,128)S(1)} %get-tuple-element.39), channel_id=1, source_target_pairs={{0,8},{1,2},{2,1},{3,4},{4,3},{5,6},{6,5},{7,15},{8,0},{9,10},{10,... | collective-permute-start | bytes 503816 | tf_op jit(solution)/shard_map/ppermute | solution.py:600
  5.2 0.0 collective-permute-done.pack_a
  5.2 0.1 choose.1
  5.3 0.0 copy-start
  5.3 3.4 %collective-permute-start.2 = (f32[2,4,128]{2,1,0:T(4,128)S(1)}, f32[2,4,128]{2,1,0:T(4,128)S(1)}, u32[]{:S(2)}, u32[]{:S(2)}) collective-permute-start(f32[2,4,128]{2,1,0:T(4,128)S(1)} %get-tuple-element.44), channel_id=1, source_target_pairs={{0,7},{1,6},{2,5},{3,4},{4,3},{5,2},{6,1},{7,0},{8,15},{9,14},{10,... | collective-permute-start | bytes 12296 | tf_op jit(solution)/shard_map/ppermute | solution.py:613
  8.7 0.0 collective-permute-start.3
  8.7 0.6 %collective-permute-start.4 = (f32[2,4,128]{2,1,0:T(4,128)S(1)}, f32[2,4,128]{2,1,0:T(4,128)S(1)}, u32[]{:S(2)}, u32[]{:S(2)}) collective-permute-start(f32[2,4,128]{2,1,0:T(4,128)S(1)} %get-tuple-element.46), channel_id=1, source_target_pairs={{0,3},{1,2},{2,1},{3,0},{4,7},{5,6},{6,5},{7,4},{8,11},{9,10},{10,... | collective-permute-start | bytes 12296 | tf_op jit(solution)/shard_map/ppermute | solution.py:613
  9.3 0.0 copy-done
  9.3 0.1 copy.15.wavelet
  9.3 0.0 collective-permute-done.1.pack_b
  9.3 1.7 %homogeneous.1 = (f32[4,32,8,128]{3,2,1,0:T(8,128)S(1)}, f32[32,8,128]{2,1,0:T(8,128)S(1)}, f32[22,8,128]{2,1,0:T(8,128)S(1)}, f32[4,22,8,128]{3,2,1,0:T(8,128)S(1)}, f32[32,1,1152]{2,1,0:T(1,128)S(1)}) custom-call(s32[3,8,128]{2,1,0:T(8,128)S(1)} %get-tuple-element.30.info, f32[1,8,16,256]{3,2,1,0:T(8,128)S(1)} %get-tuple-element.31.un, ...), custom_call_target="tpu_custom_call" | custom-call | tf_op jit(solution)/shard_map/homogeneous/pallas_call | solution.py:619
  11.0 0.0 collective-permute-done.2.refs_0_
  11.0 1.6 %collective-permute-done.3.refs_1_ = f32[2,4,128]{2,1,0:T(4,128)S(1)} collective-permute-done((f32[2,4,128]{2,1,0:T(4,128)S(1)}, f32[2,4,128]{2,1,0:T(4,128)S(1)}, u32[]{:S(2)}, u32[]{:S(2)}) %collective-permute-start.3) | collective-permute-done | bytes 4128 | tf_op jit(solution)/shard_map/ppermute | solution.py:613
  12.6 0.0 collective-permute-done.4.refs_2_
  12.6 0.6 %scattered.1 = f32[32,1,1152]{2,1,0:T(1,128)S(1)} custom-call(s32[3,8,128]{2,1,0:T(8,128)S(1)} %get-tuple-element.30.info, f32[4,32,8,128]{3,2,1,0:T(8,128)S(1)} %get-tuple-element.40.acc, f32[32,8,128]{2,1,0:T(8,128)S(1)} %get-tuple-element.41.speed, f32[22,8,128]{2,1,0:T(8,128)S(1)} %get-tuple-element.42.hit, ...), custom_call_target="tpu_custom_call", output_to_operand_aliasing={{}: (9, {})} | custom-call | tf_op jit(solution)/shard_map/scattered/pallas_call | solution.py:637
  13.2 11.5 %all_to_all.5.received = f32[32,1,1152]{2,1,0:T(1,128)S(1)} all-to-all(f32[32,1,1152]{2,1,0:T(1,128)S(1)} %scattered.1), channel_id=1, replica_groups=mesh['shot'=4,'box'=8] {'shot','box'}, dimensions={0} | all-to-all | bytes 294912 | tf_op jit(solution)/shard_map/all_to_all | solution.py:648
  24.8 0.7 %join.1 = f32[12,1,2,256]{3,2,1,0:T(2,128)} custom-call(f32[32,1,1152]{2,1,0:T(1,128)S(1)} %all_to_all.5.received), custom_call_target="tpu_custom_call" | custom-call | tf_op jit(solution)/shard_map/join/pallas_call | solution.py:649
Async XLA Ops:
  1.4 3.7 %collective-permute-start = (f32[44,8,128]{2,1,0:T(8,128)S(1)}, f32[44,8,128]{2,1,0:T(8,128)S(1)}, u32[]{:S(2)}, u32[]{:S(2)}) collective-permute-start(f32[44,8,128]{2,1,0:T(8,128)S(1)} %get-tuple-element.28), channel_id=1, source_target_pairs={{0,1},{1,0},{2,3},{3,2},{4,5},{5,4},{6,7},{7,6},{8,9},{9,8},{10,11... | collective-permute-start | bytes 540680 | tf_op jit(solution)/shard_map/ppermute | solution.py:599
  2.0 7.4 %collective-permute-start.1 = (f32[41,8,128]{2,1,0:T(8,128)S(1)}, f32[41,8,128]{2,1,0:T(8,128)S(1)}, u32[]{:S(2)}, u32[]{:S(2)}) collective-permute-start(f32[41,8,128]{2,1,0:T(8,128)S(1)} %get-tuple-element.39), channel_id=1, source_target_pairs={{0,8},{1,2},{2,1},{3,4},{4,3},{5,6},{6,5},{7,15},{8,0},{9,10},{10,... | collective-permute-start | bytes 503816 | tf_op jit(solution)/shard_map/ppermute | solution.py:600
  5.3 4.0 %copy-start = (f32[1,8,4]{1,2,0:T(4,128)S(1)}, f32[1,8,4]{1,2,0:T(4,128)}, u32[]{:S(2)}) copy-start(f32[1,8,4]{1,2,0:T(4,128)} %param.20) | copy-start | bytes 388
  5.3 5.7 %collective-permute-start.2 = (f32[2,4,128]{2,1,0:T(4,128)S(1)}, f32[2,4,128]{2,1,0:T(4,128)S(1)}, u32[]{:S(2)}, u32[]{:S(2)}) collective-permute-start(f32[2,4,128]{2,1,0:T(4,128)S(1)} %get-tuple-element.44), channel_id=1, source_target_pairs={{0,7},{1,6},{2,5},{3,4},{4,3},{5,2},{6,1},{7,0},{8,15},{9,14},{10,... | collective-permute-start | bytes 12296 | tf_op jit(solution)/shard_map/ppermute | solution.py:613
  8.7 3.9 %collective-permute-start.3 = (f32[2,4,128]{2,1,0:T(4,128)S(1)}, f32[2,4,128]{2,1,0:T(4,128)S(1)}, u32[]{:S(2)}, u32[]{:S(2)}) collective-permute-start(f32[2,4,128]{2,1,0:T(4,128)S(1)} %get-tuple-element.45), channel_id=1, source_target_pairs={{0,5},{1,4},{2,7},{3,6},{4,1},{5,0},{6,3},{7,2},{8,13},{9,12},{10,... | collective-permute-start | bytes 12296 | tf_op jit(solution)/shard_map/ppermute | solution.py:613
  8.7 3.9 %collective-permute-start.4 = (f32[2,4,128]{2,1,0:T(4,128)S(1)}, f32[2,4,128]{2,1,0:T(4,128)S(1)}, u32[]{:S(2)}, u32[]{:S(2)}) collective-permute-start(f32[2,4,128]{2,1,0:T(4,128)S(1)} %get-tuple-element.46), channel_id=1, source_target_pairs={{0,3},{1,2},{2,1},{3,0},{4,7},{5,6},{6,5},{7,4},{8,11},{9,10},{10,... | collective-permute-start | bytes 12296 | tf_op jit(solution)/shard_map/ppermute | solution.py:613

commit v6 on v5

--- a/solution.py
+++ b/solution.py
@@ -459,8 +459,8 @@
 
     low_tile = first + tiles * position - 3 + owners
     for m in range(tiles + 6):
-        apart = lax.rem(low_tile + m, owners) ^ position
-        chips, core = lax.div(apart, 2), lax.rem(apart, 2)
+        apart = ((low_tile + m) & (owners - 1)) ^ position
+        chips, core = apart >> 1, apart & 1
         part = slice(2 * (m // owners), 2 * (m // owners) + 2)
         pair = images[0][core, part, :]
         for i in range(1, owners // 2):
@@ -505,7 +505,7 @@
     adjoint = (q3, q2, q1, q0)
 
     for k in range(tiles):
-        owner = lax.rem(first + tiles * position + k, owners)
+        owner = (first + tiles * position + k) & (owners - 1)
         for w in range(2):
             e = MARGIN + 2 * k + w
             part = slice(w * LANES, (w + 1) * LANES)

time: 25.6 us -> 25.6 us (level)
  no operation moved by 1% of the time
where the time goes in v6:
time: 25.6 us; the launch traced here: 25.4 us
  blocking collectives  11.5 us (45%)
  starting transfers between devices  7.07 us (28%)
  Pallas kernels  4.43 us (17%)
  waiting for transfers between devices  1.63 us (6%)
  between operations  0.7 us (3%)
    all_to_all x1, blocking collectives, on_device(): lax.all_to_all(out, ('shot', 'box'), split_axis=0, concat_axis=0, tiled=T...  11.5 us
    ppermute x3, starting transfers between devices, on_device(): images[i] = lax.ppermute(picks[i], 'box', pairs)  3.99 us
    ppermute x1, starting transfers between devices, on_device(): got_b = lax.ppermute(send_b, ('shot', 'box'), swap_b)  2.56 us
    pallas_call x1, Pallas kernels, on_device(): pl.pallas_call(functools.partial(homogeneous_kernel, owners=owners, group...  1.66 us
    ppermute x3, waiting for transfers between devices, on_device(): images[i] = lax.ppermute(picks[i], 'box', pairs)  1.62 us
    pallas_call x1, Pallas kernels, on_device(): pl.pallas_call(pack_kernel, out_shape=(VMEM((PACK_TILES + pl.cdiv(rounds,...  1.43 us
    pallas_call x1, Pallas kernels, on_device(): pl.pallas_call(functools.partial(join_kernel, owners=owners, groups=group...  0.71 us
    pallas_call x1, Pallas kernels, on_device(): pl.pallas_call(functools.partial(scattered_kernel, owners=owners, groups=...  0.56 us
  transfers between devices with their start and end apart: 5, of which 1 were waited for; matrix products, arithmetic and copies ran while one was open for 0% of the time, Pallas kernels for 7%

profile of v6, /device:TPU:0, one launch (start us, length us, event | category | flops | bytes accessed | tf_op | source)
XLA Modules:
  0.0 25.4 jit_solution(15590246639786116309)
XLA Ops:
  0.0 1.4 %pack.1 = (f32[44,8,128]{2,1,0:T(8,128)S(1)}, f32[41,8,128]{2,1,0:T(8,128)S(1)}, s32[3,8,128]{2,1,0:T(8,128)S(1)}, f32[1,8,16,256]{3,2,1,0:T(8,128)S(1)}, f32[1,...) custom-call(s32[1,8]{1,0:T(1,128)} %sources_any.1, ...), custom_call_target="tpu_custom_call" | custom-call | tf_op jit(solution)/shard_map/pack/pallas_call | solution.py:572
  1.4 0.5 %collective-permute-start = (f32[44,8,128]{2,1,0:T(8,128)S(1)}, f32[44,8,128]{2,1,0:T(8,128)S(1)}, u32[]{:S(2)}, u32[]{:S(2)}) collective-permute-start(f32[44,8,128]{2,1,0:T(8,128)S(1)} %get-tuple-element.28), channel_id=1, source_target_pairs={{0,1},{1,0},{2,3},{3,2},{4,5},{5,4},{6,7},{7,6},{8,9},{9,8},{10,11... | collective-permute-start | bytes 540680 | tf_op jit(solution)/shard_map/ppermute | solution.py:599
  2.0 2.6 %collective-permute-start.1 = (f32[41,8,128]{2,1,0:T(8,128)S(1)}, f32[41,8,128]{2,1,0:T(8,128)S(1)}, u32[]{:S(2)}, u32[]{:S(2)}) collective-permute-start(f32[41,8,128]{2,1,0:T(8,128)S(1)} %get-tuple-element.39), channel_id=1, source_target_pairs={{0,8},{1,2},{2,1},{3,4},{4,3},{5,6},{6,5},{7,15},{8,0},{9,10},{10,... | collective-permute-start | bytes 503816 | tf_op jit(solution)/shard_map/ppermute | solution.py:600
  5.2 0.0 collective-permute-done.pack_a
  5.2 0.1 choose.1
  5.3 0.0 copy-start
  5.3 3.4 %collective-permute-start.2 = (f32[2,4,128]{2,1,0:T(4,128)S(1)}, f32[2,4,128]{2,1,0:T(4,128)S(1)}, u32[]{:S(2)}, u32[]{:S(2)}) collective-permute-start(f32[2,4,128]{2,1,0:T(4,128)S(1)} %get-tuple-element.44), channel_id=1, source_target_pairs={{0,7},{1,6},{2,5},{3,4},{4,3},{5,2},{6,1},{7,0},{8,15},{9,14},{10,... | collective-permute-start | bytes 12296 | tf_op jit(solution)/shard_map/ppermute | solution.py:613
  8.7 0.0 collective-permute-start.3
  8.7 0.6 %collective-permute-start.4 = (f32[2,4,128]{2,1,0:T(4,128)S(1)}, f32[2,4,128]{2,1,0:T(4,128)S(1)}, u32[]{:S(2)}, u32[]{:S(2)}) collective-permute-start(f32[2,4,128]{2,1,0:T(4,128)S(1)} %get-tuple-element.46), channel_id=1, source_target_pairs={{0,3},{1,2},{2,1},{3,0},{4,7},{5,6},{6,5},{7,4},{8,11},{9,10},{10,... | collective-permute-start | bytes 12296 | tf_op jit(solution)/shard_map/ppermute | solution.py:613
  9.3 0.0 copy-done
  9.3 0.1 copy.15.wavelet
  9.3 0.0 collective-permute-done.1.pack_b
  9.3 1.7 %homogeneous.1 = (f32[4,32,8,128]{3,2,1,0:T(8,128)S(1)}, f32[32,8,128]{2,1,0:T(8,128)S(1)}, f32[22,8,128]{2,1,0:T(8,128)S(1)}, f32[4,22,8,128]{3,2,1,0:T(8,128)S(1)}, f32[32,1,1152]{2,1,0:T(1,128)S(1)}) custom-call(s32[3,8,128]{2,1,0:T(8,128)S(1)} %get-tuple-element.30.info, f32[1,8,16,256]{3,2,1,0:T(8,128)S(1)} %get-tuple-element.31.un, ...), custom_call_target="tpu_custom_call" | custom-call | tf_op jit(solution)/shard_map/homogeneous/pallas_call | solution.py:619
  11.0 0.0 collective-permute-done.2.refs_0_
  11.0 1.6 %collective-permute-done.3.refs_1_ = f32[2,4,128]{2,1,0:T(4,128)S(1)} collective-permute-done((f32[2,4,128]{2,1,0:T(4,128)S(1)}, f32[2,4,128]{2,1,0:T(4,128)S(1)}, u32[]{:S(2)}, u32[]{:S(2)}) %collective-permute-start.3) | collective-permute-done | bytes 4128 | tf_op jit(solution)/shard_map/ppermute | solution.py:613
  12.6 0.0 collective-permute-done.4.refs_2_
  12.6 0.6 %scattered.1 = f32[32,1,1152]{2,1,0:T(1,128)S(1)} custom-call(s32[3,8,128]{2,1,0:T(8,128)S(1)} %get-tuple-element.30.info, f32[4,32,8,128]{3,2,1,0:T(8,128)S(1)} %get-tuple-element.40.acc, f32[32,8,128]{2,1,0:T(8,128)S(1)} %get-tuple-element.41.speed, f32[22,8,128]{2,1,0:T(8,128)S(1)} %get-tuple-element.42.hit, ...), custom_call_target="tpu_custom_call", output_to_operand_aliasing={{}: (9, {})} | custom-call | tf_op jit(solution)/shard_map/scattered/pallas_call | solution.py:637
  13.2 11.5 %all_to_all.5.received = f32[32,1,1152]{2,1,0:T(1,128)S(1)} all-to-all(f32[32,1,1152]{2,1,0:T(1,128)S(1)} %scattered.1), channel_id=1, replica_groups=mesh['shot'=4,'box'=8] {'shot','box'}, dimensions={0} | all-to-all | bytes 294912 | tf_op jit(solution)/shard_map/all_to_all | solution.py:648
  24.7 0.7 %join.1 = f32[12,1,2,256]{3,2,1,0:T(2,128)} custom-call(f32[32,1,1152]{2,1,0:T(1,128)S(1)} %all_to_all.5.received), custom_call_target="tpu_custom_call" | custom-call | tf_op jit(solution)/shard_map/join/pallas_call | solution.py:649
Async XLA Ops:
  1.4 3.7 %collective-permute-start = (f32[44,8,128]{2,1,0:T(8,128)S(1)}, f32[44,8,128]{2,1,0:T(8,128)S(1)}, u32[]{:S(2)}, u32[]{:S(2)}) collective-permute-start(f32[44,8,128]{2,1,0:T(8,128)S(1)} %get-tuple-element.28), channel_id=1, source_target_pairs={{0,1},{1,0},{2,3},{3,2},{4,5},{5,4},{6,7},{7,6},{8,9},{9,8},{10,11... | collective-permute-start | bytes 540680 | tf_op jit(solution)/shard_map/ppermute | solution.py:599
  2.0 7.4 %collective-permute-start.1 = (f32[41,8,128]{2,1,0:T(8,128)S(1)}, f32[41,8,128]{2,1,0:T(8,128)S(1)}, u32[]{:S(2)}, u32[]{:S(2)}) collective-permute-start(f32[41,8,128]{2,1,0:T(8,128)S(1)} %get-tuple-element.39), channel_id=1, source_target_pairs={{0,8},{1,2},{2,1},{3,4},{4,3},{5,6},{6,5},{7,15},{8,0},{9,10},{10,... | collective-permute-start | bytes 503816 | tf_op jit(solution)/shard_map/ppermute | solution.py:600
  5.3 4.0 %copy-start = (f32[1,8,4]{1,2,0:T(4,128)S(1)}, f32[1,8,4]{1,2,0:T(4,128)}, u32[]{:S(2)}) copy-start(f32[1,8,4]{1,2,0:T(4,128)} %param.20) | copy-start | bytes 388
  5.3 5.7 %collective-permute-start.2 = (f32[2,4,128]{2,1,0:T(4,128)S(1)}, f32[2,4,128]{2,1,0:T(4,128)S(1)}, u32[]{:S(2)}, u32[]{:S(2)}) collective-permute-start(f32[2,4,128]{2,1,0:T(4,128)S(1)} %get-tuple-element.44), channel_id=1, source_target_pairs={{0,7},{1,6},{2,5},{3,4},{4,3},{5,2},{6,1},{7,0},{8,15},{9,14},{10,... | collective-permute-start | bytes 12296 | tf_op jit(solution)/shard_map/ppermute | solution.py:613
  8.7 3.9 %collective-permute-start.3 = (f32[2,4,128]{2,1,0:T(4,128)S(1)}, f32[2,4,128]{2,1,0:T(4,128)S(1)}, u32[]{:S(2)}, u32[]{:S(2)}) collective-permute-start(f32[2,4,128]{2,1,0:T(4,128)S(1)} %get-tuple-element.45), channel_id=1, source_target_pairs={{0,5},{1,4},{2,7},{3,6},{4,1},{5,0},{6,3},{7,2},{8,13},{9,12},{10,... | collective-permute-start | bytes 12296 | tf_op jit(solution)/shard_map/ppermute | solution.py:613
  8.7 3.9 %collective-permute-start.4 = (f32[2,4,128]{2,1,0:T(4,128)S(1)}, f32[2,4,128]{2,1,0:T(4,128)S(1)}, u32[]{:S(2)}, u32[]{:S(2)}) collective-permute-start(f32[2,4,128]{2,1,0:T(4,128)S(1)} %get-tuple-element.46), channel_id=1, source_target_pairs={{0,3},{1,2},{2,1},{3,0},{4,7},{5,6},{6,5},{7,4},{8,11},{9,10},{10,... | collective-permute-start | bytes 12296 | tf_op jit(solution)/shard_map/ppermute | solution.py:613
